TPU v7x, 32 devices: a whole 2x2x4 slice. The times are simulated.
32 devices in a mesh: dp: 16 (over z, y, x), mp: 2 (over core).
Axes of the slice: x: 2, y: 2, z: 4, core: 2. Of those that a mesh axis runs over, the one named last changes fastest.
Arguments:
- tokens: bfloat16 [2048, 32, 768], P('dp'), may hold values from -6 to 6
- lengths: int32 [2048], P('dp'), may hold values from 1 to 32, as said below
- send_order: int32 [2048], P('dp'), may hold values from 0 to 127, as said below
- pooled_grad: float32 [2048, 768], P('dp'), may hold values from -6 to 6
- qkv_weight: float32 [3, 768, 768], P(None, 'dp', 'mp'), may hold values from -0.21875 to 0.21875
- out_weight: float32 [768, 768], P('mp', 'dp'), may hold values from -0.875 to 0.875
- in_weight: float32 [768, 3072], P('dp', 'mp'), may hold values from -0.21875 to 0.21875
- down_weight: float32 [3072, 768], P('mp', 'dp'), may hold values from -0.109375 to 0.109375
- vectors: float32 [9216], replicated
- qkv_moment: float32 [3, 768, 768], P(None, 'dp', 'mp'), may hold values from -7 to 7
- out_moment: float32 [768, 768], P('mp', 'dp'), may hold values from -7 to 7
- in_moment: float32 [768, 3072], P('dp', 'mp'), may hold values from -7 to 7
- down_moment: float32 [3072, 768], P('mp', 'dp'), may hold values from -7 to 7
- vec_moment: float32 [9216], replicated, may hold values from -7 to 7
- qkv_square: float32 [3, 768, 768], P(None, 'dp', 'mp'), may hold values from 0.1024 to 0.4096
- out_square: float32 [768, 768], P('mp', 'dp'), may hold values from 0.1024 to 0.4096
- in_square: float32 [768, 3072], P('dp', 'mp'), may hold values from 0.1024 to 0.4096
- down_square: float32 [3072, 768], P('mp', 'dp'), may hold values from 0.1024 to 0.4096
- vec_square: float32 [9216], replicated, may hold values from 0.1024 to 0.4096
- qkv_average: float32 [3, 768, 768], P(None, 'dp', 'mp'), may hold values from -0.21875 to 0.21875
- out_average: float32 [768, 768], P('mp', 'dp'), may hold values from -0.875 to 0.875
- in_average: float32 [768, 3072], P('dp', 'mp'), may hold values from -0.21875 to 0.21875
- down_average: float32 [3072, 768], P('mp', 'dp'), may hold values from -0.109375 to 0.109375
- vec_average: float32 [9216], replicated
Outputs:
- pooled: float32 [2048, 768], P('dp')
- tokens_grad: float32 [2048, 32, 768], P('dp', None, 'mp')
- qkv_grad: float32 [3, 768, 768], P(None, 'dp', 'mp')
- out_grad: float32 [768, 768], P('mp', 'dp')
- in_grad: float32 [768, 3072], P('dp', 'mp')
- down_grad: float32 [3072, 768], P('mp', 'dp')
- vec_grad: float32 [9216], replicated
- trust_ratio: float32 [6], replicated
- weight_norm: float32 [6], replicated
- update_norm: float32 [6], replicated
- new_qkv_moment: float32 [3, 768, 768], P(None, 'dp', 'mp')
- new_out_moment: float32 [768, 768], P('mp', 'dp')
- new_in_moment: float32 [768, 3072], P('dp', 'mp')
- new_down_moment: float32 [3072, 768], P('mp', 'dp')
- new_vec_moment: float32 [9216], replicated
- new_qkv_square: float32 [3, 768, 768], P(None, 'dp', 'mp')
- new_out_square: float32 [768, 768], P('mp', 'dp')
- new_in_square: float32 [768, 3072], P('dp', 'mp')
- new_down_square: float32 [3072, 768], P('mp', 'dp')
- new_vec_square: float32 [9216], replicated
- new_qkv_weight: float32 [3, 768, 768], P(None, 'dp', 'mp')
- new_out_weight: float32 [768, 768], P('mp', 'dp')
- new_in_weight: float32 [768, 3072], P('dp', 'mp')
- new_down_weight: float32 [3072, 768], P('mp', 'dp')
- new_vectors: float32 [9216], replicated
- new_qkv_average: float32 [3, 768, 768], P(None, 'dp', 'mp')
- new_out_average: float32 [768, 768], P('mp', 'dp')
- new_in_average: float32 [768, 3072], P('dp', 'mp')
- new_down_average: float32 [3072, 768], P('mp', 'dp')
- new_vec_average: float32 [9216], replicated
Inputs may be any that keep to these rules, and one draw needn't show every extreme that they name: `lengths`: every device's 128 sentences include one of length 32. `send_order`: each device's block of 128 entries is a permutation of 0 to 127 listing that device's sentences by non-falling length; send slot q goes to bucket q // 8.
All inputs are finite; a program needn't handle non-finite values.
Results may differ from a plain program's by a relative error of at most 0.0079.
Values may be sent and summed in bfloat16 or wider, within the bound.
No kernel may reach another device: no remote copies, remote signals or barrier semaphores. Data moves between devices by JAX's collectives and lax.ppermute only.
A program may use at most 320 MiB of HBM per device.

v0:
```python
import jax
import jax.numpy as jnp
from jax import lax
from jax.experimental import pallas as pl
from jax.experimental.pallas import tpu as pltpu
from jax.sharding import PartitionSpec as P

HEAD = 64
STEP = 10
TILE = 256
BLOCK = 128
GROUP = 6

beta_one = 0.9
beta_two = 0.999
adam_eps = 1e-06
weight_decay = 0.01
learn_rate = 0.3
vector_rate = 0.05
ema_keep = 0.9
norm_eps = 1e-12
masked_score = -1000000000.0
gelu_in = 0.7978845608028654
gelu_cube = 0.044715

BF = jnp.bfloat16
F32 = jnp.float32
VMEM_LIMIT = 62 * 1024 * 1024
SMALL_LIMIT = 14 * 1024 * 1024


def dp_dims(count):
    known = {16: ((4, 4), (2, 2), (2, 1)), 128: ((4, 32), (8, 4), (4, 1))}
    return known.get(count, ((count, 1),))


def dp_shift(value, dim, step):
    size, stride = dim
    count = lax.axis_size("dp")
    pairs = []
    for index in range(count):
        place = index // stride % size
        pairs.append((index, index + ((place + step) % size - place) * stride))
    return lax.ppermute(value, "dp", pairs)


def dp_place(dim):
    size, stride = dim
    return lax.rem(lax.div(lax.axis_index("dp"), stride), size)


def swap_core(value):
    return lax.ppermute(value, "mp", [(0, 1), (1, 0)])


def arrange(pieces, dim, axis):
    size, _ = dim
    place = dp_place(dim)
    if size == 2:
        return jnp.where(place == 0, jnp.stack(pieces, axis), jnp.stack(pieces[::-1], axis))
    ordered = []
    for target in range(size):
        which = lax.rem(target - place + size, size)
        chosen = pieces[0]
        for step in range(1, size):
            chosen = jnp.where(which == step, pieces[step], chosen)
        ordered.append(chosen)
    return jnp.stack(ordered, axis)


def gather_send(value, dim):
    return [value] + [dp_shift(value, dim, -step) for step in range(1, dim[0])]


def scatter_send(slabs, dim):
    return [dp_shift(slab, dim, step) for step, slab in enumerate(slabs, 1)]


def sum_all(value, dims):
    value = value + swap_core(value)
    count = lax.axis_size("dp")
    for size, stride in dims:
        bit = 1
        while bit < size:
            pairs = []
            for index in range(count):
                place = index // stride % size
                pairs.append((index, index + ((place ^ bit) - place) * stride))
            value = value + lax.ppermute(value, "dp", pairs)
            bit *= 2
    return value


def dot_nn(left, right):
    return jnp.dot(left, right, preferred_element_type=F32)


def dot_nt(left, right):
    return lax.dot_general(left, right, (((1,), (1,)), ((), ())), preferred_element_type=F32)


def dot_tn(left, right):
    return lax.dot_general(left, right, (((0,), (0,)), ((), ())), preferred_element_type=F32)


def vec_at(index, width, core=None, part=0, cols=None):
    if core is None:
        return slice(index * width, (index + 1) * width)
    which = core if part == 0 else 1 - core
    return pl.ds(pl.multiple_of(index * width + which * cols, BLOCK), cols)


def column_sums(value):
    rows, cols = value.shape
    return jnp.sum(value.reshape(rows // 8, 8, cols), axis=0)


def pack_kernel(
    core_ref, order_ref, len_ref, tok_ref, rows_ref, seg_ref, off_ref, tiles_ref, *stage
):
    core = core_ref[0]
    half = order_ref.shape[0] // 2
    total = rows_ref.shape[0]

    def clear(step, carry):
        rows = pl.ds(pl.multiple_of(step * BLOCK, BLOCK), BLOCK)
        for column in stage:
            column[rows, :] = jnp.zeros((BLOCK, BLOCK), F32)
        seg_ref[rows, :] = jnp.full((BLOCK, BLOCK), -1.0, F32)
        return carry

    lax.fori_loop(0, total // BLOCK, clear, 0)

    def start_of(cursor, count):
        inside = cursor & (BLOCK - 1)
        return jnp.where(inside + count > BLOCK, cursor - inside + BLOCK, cursor)

    def place(slot, cursor):
        sentence = order_ref[2 * slot + core]
        count = len_ref[sentence]
        start = start_of(cursor, count)
        off_ref[0, slot] = start
        span = tok_ref.shape[1]
        value = tok_ref[sentence].astype(F32)
        for index, column in enumerate(stage):
            column[pl.ds(start, span), :] = value[:, index * BLOCK : (index + 1) * BLOCK]
        row = lax.broadcasted_iota(jnp.int32, (span, BLOCK), 0)
        seg_ref[pl.ds(start, span), :] = jnp.where(row < count, slot.astype(F32), -1.0)
        return start + count

    used = lax.fori_loop(0, half, place, 0)
    tiles_ref[0] = (used + TILE - 1) // TILE

    def partner(slot, cursor):
        count = len_ref[order_ref[2 * slot + 1 - core]]
        start = start_of(cursor, count)
        off_ref[1, slot] = start
        return start + count

    lax.fori_loop(0, half, partner, 0)

    def low(step, carry):
        rows = pl.ds(pl.multiple_of(step * BLOCK, BLOCK), BLOCK)
        for index, column in enumerate(stage):
            rows_ref[rows, index * BLOCK : (index + 1) * BLOCK] = column[rows, :].astype(BF)
        return carry

    lax.fori_loop(0, total // BLOCK, low, 0)


def head_masks():
    lane = lax.broadcasted_iota(jnp.int32, (1, 2 * HEAD), 1)
    first = jnp.where(lane < HEAD, 1.0, 0.0)
    return first.astype(BF), (1.0 - first).astype(BF)


def two_heads(value, masks):
    return jnp.concatenate([value * masks[0], value * masks[1]], axis=0)


def same_sentence(seg):
    across = jnp.transpose(seg)
    return jnp.concatenate([seg, seg], axis=1) == jnp.concatenate([across, across], axis=1)


def softmax_rows(scores, mask):
    scores = jnp.where(mask, scores, masked_score)
    expon = jnp.exp(scores - jnp.max(scores, axis=0, keepdims=True))
    return expon * (1.0 / jnp.sum(expon, axis=0, keepdims=True))


def one_above_other(value):
    return jnp.concatenate([value[:, :BLOCK], value[:, BLOCK:]], axis=0)


def attn_forward_kernel(
    last, core_ref, rows_ref, seg_ref, vec_ref, qk0, vo0, qk1, vo1, qkv_ref, att_ref, norm_ref, inv_ref
):
    width = rows_ref.shape[1]
    half = width // 2
    core = core_ref[0]
    rows = rows_ref[...]
    weights = ((qk0, vo0), (qk1, vo1))
    for part, (qk, vo) in enumerate(weights):
        base = part * 3 * half
        value = dot_nn(rows, qk[...])
        query = value[:, :half] + vec_ref[:, vec_at(0, width, core, part, half)]
        qkv_ref[:, base : base + half] = query.astype(BF)
        qkv_ref[:, base + half : base + width] = value[:, half:].astype(BF)
        value = dot_nn(rows, vo[:, :half]) + vec_ref[:, vec_at(1, width, core, part, half)]
        qkv_ref[:, base + width : base + 3 * half] = value.astype(BF)
    masks = head_masks()
    for block in range(TILE // BLOCK):
        span = slice(block * BLOCK, (block + 1) * BLOCK)
        mask = same_sentence(seg_ref[span, :])
        for part in range(2):
            for pair in range(half // (2 * HEAD)):
                at = part * 3 * half + pair * 2 * HEAD
                query = qkv_ref[span, at : at + 2 * HEAD] * BF(HEAD**-0.5)
                key = qkv_ref[span, at + half : at + half + 2 * HEAD]
                value = qkv_ref[span, at + width : at + width + 2 * HEAD]
                probs = softmax_rows(dot_nt(key, two_heads(query, masks)), mask).astype(BF)
                mixed = dot_tn(one_above_other(probs), two_heads(value, masks))
                to = part * half + pair * 2 * HEAD
                att_ref[span, to : to + 2 * HEAD] = mixed.astype(BF)
    mixed = dot_nt(att_ref[:, :half], vo0[:, half:]) + dot_nt(att_ref[:, half:], vo1[:, half:])
    pre = rows.astype(F32) + (mixed + vec_ref[:, vec_at(2, width)])
    centre = pre - jnp.mean(pre, axis=-1, keepdims=True)
    inverse = lax.rsqrt(jnp.mean(centre * centre, axis=-1, keepdims=True) + norm_eps)
    norm_ref[...] = centre * inverse
    inv_ref[...] = jnp.broadcast_to(inverse, inv_ref.shape)


def norm_back(grad, normed, inverse, gain):
    scaled = grad * gain
    first = jnp.mean(scaled, axis=-1, keepdims=True)
    second = jnp.mean(scaled * normed, axis=-1, keepdims=True)
    return (scaled - first - normed * second) * inverse


def hidden_pieces(core, width):
    return [
        pl.ds(
            pl.multiple_of(8 * width + (2 * (core if part < 2 else 1 - core) + part % 2) * width, BLOCK),
            width,
        )
        for part in range(4)
    ]


def ffn_kernel(
    last, core_ref, norm_ref, inv_ref, seg_ref, att_ref, vec_ref, high_ref, rest_ref,
    w1_own, w1_other, w2_own, w2_other,
    grad_ref, emb_ref, sums_ref, down_own, down_other, in_own, in_other,
    sum1, sum2, sum3, act, slope, emb, counts, stage, sems,
):
    step = pl.program_id(0)
    width = norm_ref.shape[1]
    half = width // 2
    lanes = [slice(part % 2 * width, (part % 2 + 1) * width) for part in range(4)]
    w1 = [(w1_own, w1_other)[part // 2].at[:, lanes[part]] for part in range(4)]
    w2 = [(w2_own, w2_other)[part // 2].at[:, lanes[part]] for part in range(4)]
    hidden_at = hidden_pieces(core_ref[0], width)

    @pl.when(step == 0)
    def _():
        emb[...] = jnp.zeros_like(emb)
        counts[...] = jnp.zeros_like(counts)
        sums_ref[...] = jnp.zeros_like(sums_ref)
        sum1[...] = jnp.zeros_like(sum1)
        sum2[...] = jnp.zeros_like(sum2)
        sum3[...] = jnp.zeros_like(sum3)

    gain_one, shift_one = vec_ref[:, vec_at(4, width)], vec_ref[:, vec_at(5, width)]
    gain_two, shift_two = vec_ref[:, vec_at(6, width)], vec_ref[:, vec_at(7, width)]
    bias_ffn = vec_ref[:, vec_at(3, width)]
    hidden_low = (norm_ref[...] * gain_one + shift_one).astype(BF)
    for part in range(4):
        pre = dot_nn(hidden_low, w1[part][...]) + vec_ref[:, hidden_at[part]]
        square = pre * pre
        tanh = jnp.tanh(pre * (gelu_in + gelu_in * gelu_cube * square))
        gate = 0.5 + 0.5 * tanh
        out = pre * gate
        act[part] = out.astype(BF)
        slope[part] = gate + out * (1.0 - tanh) * (gelu_in + 3.0 * gelu_in * gelu_cube * square)
    total = dot_nt(act[0], w2[0][...])
    for part in range(1, 4):
        total = total + dot_nt(act[part], w2[part][...])
    pre = (norm_ref[...] * gain_one + shift_one) + (total + bias_ffn)
    centre = pre - jnp.mean(pre, axis=-1, keepdims=True)
    inverse = lax.rsqrt(jnp.mean(centre * centre, axis=-1, keepdims=True) + norm_eps)
    normed = centre * inverse
    final = normed * gain_two + shift_two
    final_high = final.astype(BF)
    final_rest = (final - final_high.astype(F32)).astype(BF)
    seg = seg_ref[...]
    lane = lax.broadcasted_iota(jnp.int32, seg.shape, 1).astype(F32)
    pick = jnp.where(seg == lane, 1.0, 0.0)
    pick_across = jnp.transpose(pick).astype(BF)
    pick = pick.astype(BF)
    emb[...] += dot_nn(pick_across, final_high) + dot_nn(pick_across, final_rest)
    counts[...] += dot_nn(pick_across, jnp.ones((TILE, BLOCK), BF))
    back = dot_nn(pick, high_ref[...]) + dot_nn(pick, rest_ref[...])
    sums_ref[:, vec_at(6, width)] += column_sums(back * normed)
    sums_ref[:, vec_at(7, width)] += column_sums(back)
    grad_two = norm_back(back, normed, inverse, gain_two)
    ffn_low = grad_two.astype(BF)
    sums_ref[:, vec_at(3, width)] += column_sums(ffn_low.astype(F32))
    grad_hidden = grad_two
    for part in range(4):
        grad_act = dot_nn(ffn_low, w2[part][...])
        grad_pre = (grad_act * slope[part]).astype(BF)
        sums_ref[:, hidden_at[part]] += column_sums(grad_pre.astype(F32))
        grad_hidden = grad_hidden + dot_nt(grad_pre, w1[part][...])
        sum1[part] += dot_tn(hidden_low, grad_pre)
        sum2[part] += dot_tn(ffn_low, act[part])
    normed_one = norm_ref[...]
    sums_ref[:, vec_at(4, width)] += column_sums(grad_hidden * normed_one)
    sums_ref[:, vec_at(5, width)] += column_sums(grad_hidden)
    grad_one = norm_back(grad_hidden, normed_one, inv_ref[:, :1], gain_one)
    grad_ref[...] = grad_one
    grad_low = grad_one.astype(BF)
    for part in range(2):
        sum3[part] += dot_tn(grad_low, att_ref[:, part * half : (part + 1) * half])
    sums_ref[:, vec_at(2, width)] += column_sums(grad_low.astype(F32))

    @pl.when(last)
    def _():
        places = []
        for outs, sums in (((down_own, down_other), sum2), ((in_own, in_other), sum1)):
            for index in (2, 3, 0, 1):
                target = outs[index // 2].at[:, pl.ds(index % 2 * width, width)]
                places.append((sums.at[index], target))
            if sums is sum2:
                for index in (1, 0):
                    places.append((sum3.at[index], outs[index].at[:, pl.ds(2 * width, half)]))
        store_sums(places, stage, sems)
        held = emb_ref.shape[0]
        number = jnp.maximum(counts[:held], 1.0)
        emb_ref[...] = emb[:held] / jnp.concatenate([number] * (width // BLOCK), axis=1)


def attn_backward_kernel(
    last, core_ref, grad_ref, rows_ref, qkv_ref, seg_ref, before_ref, qk0, vo0, qk1, vo1,
    mine_ref, dx_ref, total_ref, own, other, dqkv_ref, dx, sums, weights, stage, sems,
):
    width = grad_ref.shape[1]
    half = width // 2
    core = core_ref[0]

    @pl.when(pl.program_id(0) == 0)
    def _():
        sums[...] = before_ref[...]
        weights[...] = jnp.zeros_like(weights)

    grad_low = grad_ref[...].astype(BF)
    masks = head_masks()
    mask = [same_sentence(seg_ref[b * BLOCK : (b + 1) * BLOCK, :]) for b in range(TILE // BLOCK)]
    for part, vo in enumerate((vo0, vo1)):
        base = part * 3 * half
        grad_att = dot_nn(grad_low, vo[:, half:]).astype(BF)
        units = [(block, pair) for block in range(TILE // BLOCK) for pair in range(half // (2 * HEAD))]
        for start in range(0, len(units), GROUP):
            group = units[start : start + GROUP]
            spans = [slice(block * BLOCK, (block + 1) * BLOCK) for block, _ in group]
            ats = [pair * 2 * HEAD for _, pair in group]
            query_at = [slice(base + at, base + at + 2 * HEAD) for at in ats]
            key_at = [slice(base + half + at, base + half + at + 2 * HEAD) for at in ats]
            value_at = [slice(base + width + at, base + width + at + 2 * HEAD) for at in ats]
            each = range(len(group))
            query_two = [
                two_heads(qkv_ref[spans[i], query_at[i]] * BF(HEAD**-0.5), masks) for i in each
            ]
            att_two = [two_heads(grad_att[spans[i], ats[i] : ats[i] + 2 * HEAD], masks) for i in each]
            scores = [dot_nt(qkv_ref[spans[i], key_at[i]], query_two[i]) for i in each]
            grad_probs = [dot_nt(qkv_ref[spans[i], value_at[i]], att_two[i]) for i in each]
            probs = [softmax_rows(scores[i], mask[group[i][0]]) for i in each]
            for i in each:
                dqkv_ref[spans[i], value_at[i]] = dot_nn(probs[i].astype(BF), att_two[i]).astype(BF)
            inner = [jnp.sum(grad_probs[i] * probs[i], axis=0, keepdims=True) for i in each]
            grad_scores = [(probs[i] * (grad_probs[i] - inner[i])).astype(BF) for i in each]
            for i in each:
                dqkv_ref[spans[i], key_at[i]] = dot_nn(grad_scores[i], query_two[i]).astype(BF)
            for i in each:
                key_two = two_heads(qkv_ref[spans[i], key_at[i]], masks)
                grad_query = dot_tn(one_above_other(grad_scores[i]), key_two) * HEAD**-0.5
                dqkv_ref[spans[i], query_at[i]] = grad_query.astype(BF)
        sums[:, vec_at(0, width, core, part, half)] += column_sums(
            dqkv_ref[:, base : base + half].astype(F32)
        )
        sums[:, vec_at(1, width, core, part, half)] += column_sums(
            dqkv_ref[:, base + width : base + 3 * half].astype(F32)
        )

    rows = rows_ref[...]
    total = grad_ref[...]
    for part, (qk, vo) in enumerate(((qk0, vo0), (qk1, vo1))):
        base = part * 3 * half
        total = total + dot_nt(dqkv_ref[:, base : base + width], qk[...])
        total = total + dot_nt(dqkv_ref[:, base + width : base + 3 * half], vo[:, :half])
    dx[...] = total
    mine_ref[...] = dx[:, pl.ds(pl.multiple_of(core * half, half), half)]
    dx_ref[...] = dx[:, pl.ds(pl.multiple_of((1 - core) * half, half), half)].astype(BF)
    for part in range(2):
        weights[part] += dot_tn(rows, dqkv_ref[:, part * 3 * half : (part + 1) * 3 * half])

    @pl.when(last)
    def _():
        store_sums([(weights.at[1], other), (weights.at[0], own)], stage, sems)
        for row in range(total_ref.shape[0]):
            lanes = sums[:, row * BLOCK : (row + 1) * BLOCK]
            total_ref[row : row + 1, :] = jnp.sum(lanes, axis=0, keepdims=True)


def store_sums(places, stage, sems):
    copies = []
    for index, (source, target) in enumerate(places):
        slot = index % 2
        if index >= 2:
            copies[index - 2].wait()
        cols = source.shape[-1]
        stage[slot, :, :cols] = source[...].astype(BF)
        copies.append(pltpu.make_async_copy(stage.at[slot, :, pl.ds(0, cols)], target, sems.at[slot]))
        copies[index].start()
    copies[-2].wait()
    copies[-1].wait()


def unpack_kernel(core_ref, order_ref, len_ref, off_ref, mine_ref, recv_ref, out_ref, *columns):
    core = core_ref[0]
    half = order_ref.shape[0] // 2
    span, cols = out_ref.shape[1], out_ref.shape[2]
    each = cols // BLOCK

    def spread(step, carry):
        rows = pl.ds(pl.multiple_of(step * BLOCK, BLOCK), BLOCK)
        for index in range(each):
            lanes = slice(index * BLOCK, (index + 1) * BLOCK)
            columns[index][rows, :] = mine_ref[rows, lanes]
            columns[each + index][rows, :] = recv_ref[rows, lanes].astype(F32)
        return carry

    lax.fori_loop(0, recv_ref.shape[0] // BLOCK, spread, 0)
    row = lax.broadcasted_iota(jnp.int32, (span, BLOCK), 0)

    def place(slot, carry):
        for which in range(2):
            parity = core if which == 0 else 1 - core
            sentence = order_ref[2 * slot + parity]
            count = len_ref[sentence]
            start = off_ref[which, slot]
            for index in range(each):
                value = columns[which * each + index][pl.ds(start, span), :]
                out_ref[sentence, :, index * BLOCK : (index + 1) * BLOCK] = jnp.where(
                    row < count, value, 0.0
                )
        return carry

    lax.fori_loop(0, half, place, 0)


SMEM_SPEC = pl.BlockSpec(memory_space=pltpu.SMEM)
VMEM_SPEC = pl.BlockSpec(memory_space=pltpu.VMEM)
HBM_SPEC = pl.BlockSpec(memory_space=pl.ANY)


def params(limit=VMEM_LIMIT):
    return pltpu.CompilerParams(vmem_limit_bytes=limit)


def tile_spec(cols):
    return pl.BlockSpec((TILE, cols), lambda step, tiles: (jnp.minimum(step, tiles[0] - 1), 0))


def held_spec(*shape):
    return pl.BlockSpec(
        shape, lambda step, tiles: (0,) * len(shape), pipeline_mode=pl.Buffered(1)
    )


def column_spec(width, column):
    return pl.BlockSpec((width, width), lambda step, tiles: (0, column), pipeline_mode=pl.Buffered(1))


def tiled_call(kernel, out_shape, in_specs, out_specs, scratch_shapes, cost_estimate):
    def body(tiles_ref, *refs):
        @pl.when(pl.program_id(0) < tiles_ref[0])
        def _():
            kernel(pl.program_id(0) == tiles_ref[0] - 1, *refs)

    def call(tiles, most, *operands):
        return pl.pallas_call(
            body,
            grid_spec=pltpu.PrefetchScalarGridSpec(
                num_scalar_prefetch=1,
                grid=(most // TILE,),
                in_specs=in_specs,
                out_specs=out_specs,
                scratch_shapes=scratch_shapes,
            ),
            out_shape=out_shape,
            compiler_params=params(),
            cost_estimate=cost_estimate,
        )(tiles, *operands)

    return call


def shape_of(shape, dtype):
    return jax.ShapeDtypeStruct(shape, dtype)


def cost(flops, read):
    return pl.CostEstimate(flops=int(flops), bytes_accessed=int(read), transcendentals=0)


class Side:
    def __init__(self, terms, order):
        self.terms, self.order = terms, order

    def cols(self):
        _, _, lanes = self.terms[0]
        return lanes.stop - lanes.start


def slab_sums(sides, dims, joined=False, limit=SMALL_LIMIT):
    first = dims[0]
    places = jnp.stack([dp_place(dim) for dim in dims]).astype(jnp.int32)
    at_of = {dim: index for index, dim in enumerate(dims)}
    nexts = [first if joined else side.order[0] for side in sides]
    lead = 1 if joined else first[0]
    operands, in_specs, plan = [], [], []
    out_shape, out_specs, targets = [], [], []

    def index_map(term_dims, current, step, size, fixed):
        def of(grid, at):
            index = []
            for dim in term_dims:
                if dim == current:
                    index.append(lax.rem(at[at_of[dim]] + step, size))
                elif dim == first:
                    index.append(grid)
                else:
                    index.append(at[at_of[dim]] if dim in fixed else 0)
            return (*index, 0, 0)

        return of

    for number, (side, current) in enumerate(zip(sides, nexts)):
        size = current[0]
        rows = side.terms[0][0].shape[-2]
        left = [dim for dim in side.terms[-1][1] if dim != current]
        fixed = [dim for dim in dims if dim != current and dim not in left]
        steps = range(size) if joined else range(1, size)
        for step in steps:
            ids = []
            for array, term_dims, lanes in side.terms:
                block, pick = [], []
                for dim in term_dims:
                    whole = dim in left and dim != first
                    block.append(dim[0] if whole else 1)
                    pick.append(slice(None) if whole else 0)
                ids.append((len(operands), tuple(pick), lanes))
                operands.append(array)
                in_specs.append(
                    pl.BlockSpec((*block, rows, array.shape[-1]), index_map(term_dims, current, step, size, fixed))
                )
            plan.append((ids, number, step))
        if not joined:
            rest = [dim[0] for dim in left if dim != first]
            for step in steps:
                shape = (lead, *rest, rows, side.cols())
                out_shape.append(shape_of(shape, BF))
                out_specs.append(pl.BlockSpec((1, *shape[1:]), lambda grid, at, n=len(shape): (grid,) + (0,) * (n - 1)))
                targets.append((number, step))
    if joined:
        width = sum(side.cols() for side in sides)
        rows = sides[0].terms[0][0].shape[-2]
        for step in range(first[0]):
            out_shape.append(shape_of((rows, width), BF if step else F32))
            out_specs.append(pl.BlockSpec((rows, width), lambda grid, at: (0, 0)))
            targets.append((None, step))
    starts = [sum(side.cols() for side in sides[:number]) for number in range(len(sides))]

    def kernel(places_ref, *refs):
        ins, outs = refs[: len(operands)], refs[len(operands) :]
        for ids, number, step in plan:
            total = None
            for index, pick, lanes in ids:
                value = ins[index][(*pick, slice(None), lanes)].astype(F32)
                total = value if total is None else total + value
            if joined:
                out = outs[targets.index((None, step))]
                out[:, starts[number] : starts[number] + sides[number].cols()] = total.astype(out.dtype)
            else:
                out = outs[targets.index((number, step))]
                out[0] = total.astype(BF)

    sums = pl.pallas_call(
        kernel,
        grid_spec=pltpu.PrefetchScalarGridSpec(
            num_scalar_prefetch=1, grid=(lead,), in_specs=in_specs, out_specs=out_specs
        ),
        out_shape=out_shape,
        compiler_params=params(limit),
        cost_estimate=cost(0, 8e6),
    )(places, *operands)
    if joined:
        return sums
    return [[value for value, (which, _) in zip(sums, targets) if which == number] for number in range(len(sides))]


def adam_moments(grad_value, moment, square):
    moment_new = beta_one * moment + (1.0 - beta_one) * grad_value
    square_new = beta_two * square + (1.0 - beta_two) * grad_value * grad_value
    scaled = (
        moment_new
        / (1.0 - beta_one**STEP)
        / (jnp.sqrt(square_new / (1.0 - beta_two**STEP)) + adam_eps)
    )
    return (moment_new, square_new, scaled)


def square_sum(value):
    return jnp.sum(jnp.sum(value * value, axis=0, keepdims=True), axis=1, keepdims=True)


def note_norms(norms, matrix, weight, update):
    row = lax.broadcasted_iota(jnp.int32, norms.shape, 0)
    lane = lax.broadcasted_iota(jnp.int32, norms.shape, 1)
    here = jnp.where(row == 0, square_sum(weight), square_sum(update))
    return norms + jnp.where(jnp.logical_and(row < 2, lane == matrix), here, 0.0)


def ffn_update_kernel(own_ref, *refs):
    states, arrived, outs = refs[:9], refs[9:-13], refs[-13:]
    total = own_ref[...]
    for ref in arrived:
        total = total + ref[...].astype(F32)
    norms = jnp.zeros(outs[12].shape, F32)
    down = states[6].shape[1]
    out = states[0].shape[1]
    lanes = (slice(down, down + out), slice(down + out, total.shape[1]), slice(0, down))
    for index in range(3):
        weight, moment, square = states[3 * index : 3 * index + 3]
        grad = total[:, lanes[index]]
        moment_new, square_new, scaled = adam_moments(grad, moment[...], square[...])
        update = scaled + weight_decay * weight[...]
        for target, value in zip(outs[4 * index :], (grad, moment_new, square_new, update)):
            target[...] = value
        norms = note_norms(norms, 3 + index, weight[...], update)
    outs[12][...] = norms


def qkv_update_kernel(
    own_ref, weight_ref, moment_ref, square_ref, vec_ref, norms_ref, *refs
):
    arrived, (grad_out, moment_out, square_out, update_out, totals_ref) = refs[:-5], refs[-5:]
    cols = weight_ref.shape[2]
    total = own_ref[...]
    for ref in arrived:
        total = total + ref[...].astype(F32)
    rows = vec_ref.shape[0]
    norms = norms_ref[...]
    for index in range(3):
        grad = total[:, index * cols : (index + 1) * cols]
        moment, square, scaled = adam_moments(grad, moment_ref[index], square_ref[index])
        update = scaled + weight_decay * weight_ref[index]
        grad_out[index] = grad
        moment_out[index] = moment
        square_out[index] = square
        update_out[index] = update
        norms = note_norms(norms, index, weight_ref[index], update)
    totals_ref[:rows, :] = vec_ref[...]
    totals_ref[rows:, :] = norms


def finish_kernel(totals_ref, *refs):
    ins, outs = refs[:16], refs[16:]
    rows = totals_ref.shape[0] - 8
    weight_norm = jnp.sqrt(totals_ref[rows : rows + 1, :])
    update_norm = jnp.sqrt(totals_ref[rows + 1 : rows + 2, :])
    trust = weight_norm / update_norm
    lane = lax.broadcasted_iota(jnp.int32, trust.shape, 1)
    outs[12][0:1, :] = trust
    outs[12][1:2, :] = weight_norm
    outs[12][2:3, :] = update_norm

    def step(matrix):
        return learn_rate * jnp.sum(jnp.where(lane == matrix, trust, 0.0), axis=1, keepdims=True)

    for index in range(4):
        update, weight, average = ins[3 * index : 3 * index + 3]
        for piece in range(3 if index == 0 else 1):
            at = (piece,) if index == 0 else (Ellipsis,)
            new = weight[at] - step(piece if index == 0 else index + 2) * update[at]
            outs[2 * index][at] = new
            outs[2 * index + 1][at] = ema_keep * average[at] + (1.0 - ema_keep) * new
    vectors, moment, square, average = ins[12:16]
    grad = totals_ref[:rows, :]
    moment_new, square_new, scaled = adam_moments(grad, moment[...], square[...])
    new = vectors[...] - vector_rate * scaled
    outs[8][...] = moment_new
    outs[9][...] = square_new
    outs[10][...] = new
    outs[11][...] = ema_keep * average[...] + (1.0 - ema_keep) * new


def shards(
    tokens, lengths, send_order, pooled_grad,
    qkv_weight, out_weight, in_weight, down_weight, vectors,
    qkv_moment, out_moment, in_moment, down_moment, vec_moment,
    qkv_square, out_square, in_square, down_square, vec_square,
    qkv_average, out_average, in_average, down_average, vec_average,
):
    core = lax.axis_index("mp")
    count = lax.axis_size("dp")
    dims = dp_dims(count)
    sents, span, width = tokens.shape
    half = width // 2
    mine = sents // 2
    most = mine * span
    shard_rows = qkv_weight.shape[1]
    core_word = core.reshape(1).astype(jnp.int32)

    def flip(value):
        return jnp.where(core == 0, value, value[::-1])

    chunk = jnp.concatenate([qkv_weight[0], qkv_weight[1], qkv_weight[2], out_weight.T], axis=1)
    down_t = down_weight.T.astype(BF)
    first, others = dims[0], dims[1:]
    orders = (others, others[::-1])
    sides = (0, 1)

    def gather_start(pieces):
        value = arrange(pieces, first, 0)
        cols = value.shape[-1] // 2
        return [
            (value[..., side * cols : (side + 1) * cols], [first], orders[side]) for side in sides
        ]

    def gather_out(state):
        return [gather_send(value, order[0]) if order else [value] for value, _, order in state]

    def gather_in(state, pieces):
        after = []
        for (value, done, order), come in zip(state, pieces):
            if order:
                axis = sum(1 for other in done if other[1] > order[0][1])
                value = arrange(come, order[0], axis)
                done = done + [order[0]]
            after.append((value, done, order[1:]))
        return after

    def gather_end(state):
        return [value.reshape(width, -1) for value, _, _ in state]

    share = sents // count
    if share % 2 == 0:
        own = lax.dynamic_index_in_dim(
            pooled_grad.reshape(count, share // 2, 2, width), core, 2, keepdims=False
        )
        pair_grad = lax.all_to_all(own, "dp", 0, 0, tiled=True).reshape(mine, width)
    else:
        own = lax.all_to_all(pooled_grad, "dp", 0, 0, tiled=True)
        pair_grad = lax.dynamic_index_in_dim(
            own.reshape(mine, 2, width), core, 1, keepdims=False
        )

    pieces0 = gather_send(chunk.astype(BF), first)
    qkvo = gather_start(pieces0)
    pieces0 = gather_out(qkvo)
    own, held = lax.optimization_barrier((in_weight.astype(BF), [pieces[0] for pieces in pieces0]))
    pieces1 = gather_send(own, first)
    pieces0, pieces1, pair_grad = lax.optimization_barrier((pieces0, pieces1, pair_grad))
    qkvo = gather_in(qkvo, pieces0)
    pieces0 = gather_out(qkvo)
    held = [pieces[0] for pieces in pieces0]
    own, held = lax.optimization_barrier((down_t, held))
    pieces2 = gather_send(own, first)

    order_word, _ = lax.optimization_barrier((send_order, [pieces[0] for pieces in pieces0]))
    packed = pl.pallas_call(
        pack_kernel,
        out_shape=(
            shape_of((most, width), BF),
            shape_of((most, BLOCK), F32),
            shape_of((2, mine), jnp.int32),
            shape_of((1,), jnp.int32),
        ),
        in_specs=[SMEM_SPEC, SMEM_SPEC, SMEM_SPEC, VMEM_SPEC],
        out_specs=(VMEM_SPEC, VMEM_SPEC, SMEM_SPEC, SMEM_SPEC),
        scratch_shapes=[pltpu.VMEM((most, BLOCK), F32)] * (width // BLOCK),
        compiler_params=params(),
        cost_estimate=cost(0, 30e6),
    )(core_word, order_word, lengths, tokens)
    packed, pieces0, pieces2 = lax.optimization_barrier((packed, pieces0, pieces2))
    rows, seg, offsets, tiles = packed
    full = jnp.concatenate(gather_end(gather_in(qkvo, pieces0)), axis=1)
    full = (full, swap_core(full))
    weights = (full[0], full[0], full[1], full[1])
    ffn = [
        (arrange(pieces, first, 0), [first], orders[side]) for side, pieces in enumerate((pieces1, pieces2))
    ]
    ffn = gather_in(ffn, gather_out(ffn))
    ffn_pieces = gather_out(ffn)

    own_order = lax.dynamic_index_in_dim(send_order.reshape(mine, 2), core, 1, keepdims=False)
    own_count = lengths[own_order].astype(F32)[:, None]
    back = jnp.pad(pair_grad / own_count, ((0, BLOCK - mine), (0, 0)))
    back_high = back.astype(BF)
    back_rest = (back - back_high.astype(F32)).astype(BF)
    weight_specs = [column_spec(width, 0), column_spec(width, 1)] * 2
    long_spec = held_spec(width, 2 * width)
    vec_spec = held_spec(1, vectors.shape[0])
    vec_row = vectors.reshape(1, -1)
    row_total = most * 0.6
    mids = [pieces[0] for pieces in ffn_pieces]
    tiles, mids, _, _ = lax.optimization_barrier((tiles, mids, back_high, back_rest))
    qkv, att, normed, inverse = tiled_call(
        attn_forward_kernel,
        out_shape=(
            shape_of((most, 3 * width), BF),
            shape_of((most, width), BF),
            shape_of((most, width), F32),
            shape_of((most, BLOCK), F32),
        ),
        in_specs=[SMEM_SPEC, tile_spec(width), tile_spec(BLOCK), vec_spec] + weight_specs,
        out_specs=(tile_spec(3 * width), tile_spec(width), tile_spec(width), tile_spec(BLOCK)),
        scratch_shapes=[],
        cost_estimate=cost(2 * row_total * 4 * width * width * 2, 30e6),
    )(tiles, most, core_word, rows, seg, vec_row, *weights)
    normed, ffn_pieces = lax.optimization_barrier((normed, ffn_pieces))

    w1, w2 = [(value, swap_core(value)) for value in gather_end(gather_in(ffn, ffn_pieces))]
    down_shape = shape_of((width, 2 * width + half), BF)
    in_shape = shape_of((width, 2 * width), BF)
    grad_one, emb, vec_ffn, down_own, down_other, in_own, in_other = tiled_call(
        ffn_kernel,
        out_shape=(
            shape_of((most, width), F32),
            shape_of((mine, width), F32),
            shape_of((8, vectors.shape[0]), F32),
            down_shape,
            down_shape,
            in_shape,
            in_shape,
        ),
        in_specs=[
            SMEM_SPEC, tile_spec(width), tile_spec(BLOCK), tile_spec(BLOCK), tile_spec(width), vec_spec,
        ]
        + [held_spec(BLOCK, width)] * 2
        + [long_spec] * 4,
        out_specs=(tile_spec(width), held_spec(mine, width), held_spec(8, vectors.shape[0])) + (HBM_SPEC,) * 4,
        scratch_shapes=[
            pltpu.VMEM((4, width, width), F32),
            pltpu.VMEM((4, width, width), F32),
            pltpu.VMEM((2, width, half), F32),
            pltpu.VMEM((4, TILE, width), BF),
            pltpu.VMEM((4, TILE, width), F32),
            pltpu.VMEM((BLOCK, width), F32),
            pltpu.VMEM((BLOCK, BLOCK), F32),
            pltpu.VMEM((2, width, width), BF),
            pltpu.SemaphoreType.DMA((2,)),
        ],
        cost_estimate=cost(2 * row_total * 24 * width * width, 30e6),
    )(
        tiles, most, core_word, normed, inverse, seg, att, vec_row, back_high, back_rest, *w1, *w2
    )

    def scatter_start(parts):
        sides = []
        for side, (lanes, *arrays) in enumerate(parts):
            terms = [
                (array.reshape(*[size for size, _ in dims], shard_rows, -1), list(dims), lanes)
                for array in arrays
            ]
            sides.append(Side(terms, orders[side][::-1]))
        return sides

    def scatter_out(sides, limit=SMALL_LIMIT):
        if len({side.order[0][0] for side in sides}) == 1:
            return slab_sums(sides, dims, limit=limit)
        return [slab_sums([side], dims, limit=limit)[0] for side in sides]

    def scatter_go(sides, slabs):
        return [scatter_send(sent, side.order[0]) for side, sent in zip(sides, slabs)]

    def scatter_in(sides, arrived):
        after = []
        for side, come in zip(sides, arrived):
            left = [dim for dim in side.terms[-1][1] if dim != side.order[0]]
            new = [(array, left, slice(0, side.cols())) for array in come]
            after.append(Side(side.terms + new, side.order[1:]))
        return after

    def go_pooled(value):
        return lax.all_to_all(value, "dp", 0, 0, tiled=True)

    come = [swap_core(down_other), swap_core(in_other)]
    grad_send = scatter_start(
        ((slice(0, 2 * width + half), down_own, come[0]), (slice(0, 2 * width), in_own, come[1]))
    )
    slabs = scatter_out(grad_send, VMEM_LIMIT)
    pooled = go_pooled(emb.reshape(count, share // 2, width)) if share % 2 == 0 else emb
    tiles, slabs, pooled = lax.optimization_barrier((tiles, slabs, pooled))
    qkv_shape = shape_of((width, 3 * half), BF)
    dx_mine, dx_other, vec_local, own, other = tiled_call(
        attn_backward_kernel,
        out_shape=(
            shape_of((most, half), F32),
            shape_of((most, half), BF),
            shape_of((vectors.shape[0] // BLOCK, BLOCK), F32),
            qkv_shape,
            qkv_shape,
        ),
        in_specs=[
            SMEM_SPEC, tile_spec(width), tile_spec(width), tile_spec(3 * width), tile_spec(BLOCK),
            held_spec(8, vectors.shape[0]),
        ]
        + weight_specs,
        out_specs=(tile_spec(half), tile_spec(half), held_spec(vectors.shape[0] // BLOCK, BLOCK))
        + (HBM_SPEC,) * 2,
        scratch_shapes=[
            pltpu.VMEM((TILE, 3 * width), BF),
            pltpu.VMEM((TILE, width), F32),
            pltpu.VMEM((8, vectors.shape[0]), F32),
            pltpu.VMEM((2, width, 3 * half), F32),
            pltpu.VMEM((2, width, 3 * half), BF),
            pltpu.SemaphoreType.DMA((2,)),
        ],
        cost_estimate=cost(2 * row_total * 18 * width * width, 30e6),
    )(tiles, most, core_word, grad_one, rows, qkv, seg, vec_ffn, *weights)
    arrived, own, other, dx_other = lax.optimization_barrier(
        (scatter_go(grad_send, slabs), own, other, dx_other)
    )
    grad_send = scatter_in(grad_send, arrived)
    slabs = scatter_out(grad_send, VMEM_LIMIT)
    come = swap_core(other)
    own, come, slabs = lax.optimization_barrier((own, come, slabs))
    cut = 3 * half // (2 * BLOCK) * BLOCK
    qkv_send = scatter_start(((slice(0, cut), own, come), (slice(cut, 3 * half), own, come)))
    qkv_slabs = scatter_out(qkv_send)
    order_word, slabs = lax.optimization_barrier((send_order, slabs))

    tokens_grad = pl.pallas_call(
        unpack_kernel,
        out_shape=shape_of((sents, span, half), F32),
        in_specs=[SMEM_SPEC] * 4 + [VMEM_SPEC] * 2,
        out_specs=VMEM_SPEC,
        scratch_shapes=[pltpu.VMEM((most, BLOCK), F32)] * (2 * half // BLOCK),
        compiler_params=params(),
        cost_estimate=cost(0, 20e6),
    )(core_word, order_word, lengths, offsets, dx_mine, swap_core(dx_other))
    arrived, tokens_grad, qkv_slabs = lax.optimization_barrier(
        (scatter_go(grad_send, slabs), tokens_grad, qkv_slabs)
    )
    grad_send = scatter_in(grad_send, arrived)
    ffn_grad, *slabs = slab_sums(grad_send, dims, joined=True, limit=VMEM_LIMIT)
    qkv_slabs, slabs = lax.optimization_barrier((qkv_slabs, slabs))
    last_go = scatter_send(slabs, first)
    go = scatter_go(qkv_send, qkv_slabs)
    qkv_send = scatter_in(qkv_send, go)
    while qkv_send[0].order:
        go = scatter_go(qkv_send, scatter_out(qkv_send))
        go, last_go, pooled = lax.optimization_barrier((go, last_go, pooled))
        qkv_send = scatter_in(qkv_send, go)
    qkv_grad, *slabs = slab_sums(qkv_send, dims, joined=True)
    go = scatter_send(slabs, first)

    both = flip(jnp.stack([pooled, swap_core(pooled)]))
    if share % 2 == 0:
        pooled = jnp.moveaxis(both, 0, 2).reshape(sents, width)
    else:
        both = jnp.moveaxis(both, 0, 1).reshape(sents, width)
        pooled = go_pooled(both)

    go, pooled = lax.optimization_barrier((go, pooled))
    ffn_states = [
        (out_weight.T, out_moment.T, out_square.T),
        (in_weight, in_moment, in_square),
        (down_weight.T, down_moment.T, down_square.T),
    ]
    shapes = [shape_of(state[0].shape, F32) for state in ffn_states for _ in range(4)]
    *ffn_new, norms = pl.pallas_call(
        ffn_update_kernel,
        out_shape=shapes + [shape_of((8, BLOCK), F32)],
        in_specs=[VMEM_SPEC] * (10 + len(last_go)),
        out_specs=[VMEM_SPEC] * 13,
        compiler_params=params(SMALL_LIMIT),
        cost_estimate=cost(0, 4e6),
    )(ffn_grad, *[value for state in ffn_states for value in state], *last_go)
    out_grad, out_m, out_s, out_u, in_grad, in_m, in_s, in_u, down_grad, down_m, down_s, down_u = ffn_new
    lines = vectors.shape[0] // BLOCK
    like = [shape_of(qkv_weight.shape, F32)]
    qkv_grad, qkv_m, qkv_s, qkv_u, totals = pl.pallas_call(
        qkv_update_kernel,
        out_shape=like * 4 + [shape_of((lines + 8, BLOCK), F32)],
        in_specs=[VMEM_SPEC] * (6 + len(go)),
        out_specs=[VMEM_SPEC] * 5,
        compiler_params=params(SMALL_LIMIT),
        cost_estimate=cost(0, 4e6),
    )(qkv_grad, qkv_weight, qkv_moment, qkv_square, vec_local, norms, *go)
    totals = sum_all(totals, dims)
    states = [
        (qkv_u, qkv_weight, qkv_average),
        (out_u, out_weight.T, out_average.T),
        (in_u, in_weight, in_average),
        (down_u, down_weight.T, down_average.T),
    ]
    pieces = [value.reshape(lines, BLOCK) for value in (vectors, vec_moment, vec_square, vec_average)]
    shapes = [shape_of(update.shape, F32) for update, _, _ in states for _ in range(2)]
    shapes += [shape_of((lines, BLOCK), F32)] * 4 + [shape_of((8, BLOCK), F32)]
    (
        new_qkv, qkv_a, new_out, out_a, new_in, in_a, new_down, down_a, vec_m, vec_s, new_vec, vec_a, ratios,
    ) = pl.pallas_call(
        finish_kernel,
        out_shape=shapes,
        in_specs=[VMEM_SPEC] * 17,
        out_specs=[VMEM_SPEC] * len(shapes),
        compiler_params=params(SMALL_LIMIT),
        cost_estimate=cost(0, 4e6),
    )(totals, *[value for state in states for value in state], *pieces)
    vec_grad, vec_m, vec_s, new_vec, vec_a = [
        value.reshape(-1) for value in (totals[:lines], vec_m, vec_s, new_vec, vec_a)
    ]
    trust_ratio, weight_norm, update_norm = [ratios[index, :6] for index in range(3)]
    out_grad, out_m, out_s, new_out, out_a = [value.T for value in (out_grad, out_m, out_s, new_out, out_a)]
    down_grad, down_m, down_s, new_down, down_a = [
        value.T for value in (down_grad, down_m, down_s, new_down, down_a)
    ]
    return (
        pooled, tokens_grad, qkv_grad, out_grad, in_grad, down_grad, vec_grad,
        trust_ratio, weight_norm, update_norm,
        qkv_m, out_m, in_m, down_m, vec_m,
        qkv_s, out_s, in_s, down_s, vec_s,
        new_qkv, new_out, new_in, new_down, new_vec,
        qkv_a, out_a, in_a, down_a, vec_a,
    )


def solution(mesh):
    matrices = (P(None, "dp", "mp"), P("mp", "dp"), P("dp", "mp"), P("mp", "dp"), P())
    return jax.shard_map(
        shards,
        mesh=mesh,
        in_specs=(P("dp", None, None), P("dp"), P("dp"), P("dp", None)) + matrices * 4,
        out_specs=(P("dp", None), P("dp", None, "mp")) + matrices + (P(), P(), P()) + matrices * 4,
        check_vma=False,
    )
```

profile of v0, /device:TPU:0, one launch (start us, length us, event | category | flops | bytes accessed | tf_op | source)
XLA Modules:
  0.0 334.9 jit_solution(6664833782990665928)
XLA Ops:
  2.6 3.1 collective-permute-start
  5.6 2.6 collective-permute-start.1
  11.7 3.9 %all-to-all-start = ((f32[16,4,768]{2,1,0:T(4,128)}), f32[16,4,768]{2,1,0:T(4,128)S(1)}, u32[]{:S(2)}, u32[]{:S(2)}) async-start(f32[16,4,768]{2,1,0:T(4,128)} %bitcast.105), calls=%async_computation | async-start | bytes 393216 | tf_op jit(solution)/shard_map/all_to_all | solution.py:763
  15.7 2.2 collective-permute-done.1
  18.3 1.6 collective-permute-start.3
  21.4 7.9 %collective-permute-start.5 = (bf16[48,1536]{1,0:T(8,128)(2,1)S(1)}, bf16[48,1536]{1,0:T(8,128)(2,1)S(1)}, u32[]{:S(2)}, u32[]{:S(2)}) collective-permute-start(bf16[48,1536]{1,0:T(8,128)(2,1)S(1)} %convert_element_type.25), channel_id=1, source_target_pairs={{0,24},{2,26},{4,28},{6,30},{8,0},{10,2},{12,4},{14,6},{16,8},{18,... | collective-permute-start | bytes 442376 | tf_op jit(solution)/shard_map/ppermute | solution.py:44
  30.1 3.1 collective-permute-done.5
  33.2 8.2 %collective-permute-done.6 = bf16[48,1536]{1,0:T(8,128)(2,1)S(1)} collective-permute-done((bf16[48,1536]{1,0:T(8,128)(2,1)S(1)}, bf16[48,1536]{1,0:T(8,128)(2,1)S(1)}, u32[]{:S(2)}, u32[]{:S(2)}) %collective-permute-start.6) | collective-permute-done | bytes 147488 | tf_op jit(solution)/shard_map/ppermute | solution.py:44
  44.3 1.9 collective-permute-start.12
  47.4 7.7 %shard_map.463 = (bf16[2048,768]{1,0:T(8,128)(2,1)}, f32[2048,128]{1,0:T(8,128)}, s32[2,64]{1,0:T(2,128)}, s32[1]{0:T(128)}) custom-call(s32[1]{0:T(128)} %bitcast.3.core_ref.refs_0_, s32[128]{0:T(128)} %order_ref.1, s32[128]{0:T(128)} %len_ref.3, bf16[128,32,768]{2,1,0:T(8,128)(2,1)} %tok_ref.1), custom_call_target="tpu_custom_call" | custom-call | bytes 30000000 | tf_op jit(solution)/shard_map/pallas_call | solution.py:783
  55.1 1.6 collective-permute-done.11
  63.1 1.6 collective-permute-start.14
  65.5 10.9 %collective-permute-done.13 = bf16[4,48,1536]{2,1,0:T(8,128)(2,1)S(1)} collective-permute-done((bf16[4,48,1536]{2,1,0:T(8,128)(2,1)S(1)}, bf16[4,48,1536]{2,1,0:T(8,128)(2,1)S(1)}, u32[]{:S(2)}, u32[]{:S(2)}) %collective-permute-start.13) | collective-permute-done | bytes 589856 | tf_op jit(solution)/shard_map/ppermute | solution.py:44
  76.6 1.6 collective-permute-start.16
  82.7 19.3 %shard_map.464 = (bf16[2048,2304]{1,0:T(8,128)(2,1)}, bf16[2048,768]{1,0:T(8,128)(2,1)}, f32[2048,768]{1,0:T(8,128)}, f32[2048,128]{1,0:T(8,128)}) custom-call(s32[1]{0:T(128)} %get-tuple-element.208.tiles_ref, s32[1]{0:T(128)} %bitcast.3.core_ref.refs_0_, bf16[2048,768]{1,0:T(8,128)(2,1)} %get-tuple-element.185.refs_1_.refs_2_, ...), custom_call_target="tpu_custom_call" | custom-call | flops 11596411904 | bytes 30000000 | tf_op jit(solution)/shard_map/pallas_call | solution.py:492
  103.2 2.6 collective-permute-done.17
  105.8 2.0 maximum_select_fusion
  108.1 3.5 %maximum_select_fusion.1 = bf16[4,2,2,48,1536]{4,3,0,2,1:T(8,128)(2,1)S(1)} fusion(bf16[4,1,2,48,1536]{4,3,0,2,1:T(8,128)(2,1)} %bitcast.40, bf16[4,1,2,48,1536]{4,3,0,2,1:T(8,128)(2,1)} %bitcast.39, pred[]{:T(512)S(6)} %eq.30), kind=kLoop, calls=%fused_computation.3 | loop fusion | flops 3538944 | bytes 4718593 | tf_op jit(solution)/shard_map/jit(_where)/select_n | solution.py:60
  113.3 3.1 collective-permute-done.19.refs_11_
  117.8 66.3 %shard_map.465 = (f32[2048,768]{1,0:T(8,128)}, f32[64,768]{1,0:T(8,128)}, f32[8,9216]{1,0:T(8,128)}, bf16[768,1920]{1,0:T(8,128)(2,1)}, bf16[768,1920]{1,0:T(8,1...) custom-call(s32[1]{0:T(128)} %get-tuple-element.208.tiles_ref, s32[1]{0:T(128)} %bitcast.3.core_ref.refs_0_, ...), custom_call_target="tpu_custom_call" | custom-call | flops 34789236736 | bytes 30000000 | tf_op jit(solution)/shard_map/pallas_call | solution.py:492
  184.7 1.7 reshape.160
  186.4 5.0 %all-to-all-start.1 = ((f32[16,4,768]{2,1,0:T(4,128)}), f32[16,4,768]{2,1,0:T(4,128)}, u32[]{:S(2)}, u32[]{:S(2)}) async-start(f32[16,4,768]{2,1,0:T(4,128)} %reshape.160), calls=%async_computation.1 | async-start | bytes 393216 | tf_op jit(solution)/shard_map/all_to_all | solution.py:898
  193.3 5.3 %shard_map.466 = (bf16[4,2,48,1920]{3,2,1,0:T(8,128)(2,1)}, bf16[4,2,48,1536]{3,2,1,0:T(8,128)(2,1)}) custom-call(s32[3]{0:T(128)} %pad_add_fusion.places_ref, bf16[4,2,2,48,1920]{4,3,2,1,0:T(8,128)(2,1)} %bitcast.134, bf16[4,2,2,48,1920]{4,3,2,1,0:T(8,128)(2,1)} %bitcast.43.refs_1_.refs_5_.refs_9_.refs_13_, bf16[4,2,2,48,1536]{4,3,2,1,0:T(8,128)(2,1)} %bitcast.140, ...), custom_call_target="tpu_custom_call" | custom-call | bytes 8000000 | tf_op jit(solution)/shard_map/pallas_call | solution.py:599
  198.6 1.8 all-to-all-done.1
  201.8 28.7 %shard_map.467 = (f32[2048,384]{1,0:T(8,128)}, bf16[2048,384]{1,0:T(8,128)(2,1)}, f32[72,128]{1,0:T(8,128)}, bf16[768,1152]{1,0:T(8,128)(2,1)}, bf16[768,1152]{1,0:T(8,128)(2,1)}) custom-call(s32[1]{0:T(128)} %get-tuple-element.208.tiles_ref, s32[1]{0:T(128)} %bitcast.3.core_ref.refs_0_, f32[2048,768]{1,0:T(8,128)} %get-tuple-element.209.refs_1_, ...), custom_call_target="tpu_custom_call" | custom-call | flops 26091925504 | bytes 30000000 | tf_op jit(solution)/shard_map/pallas_call | solution.py:492
  230.6 2.6 collective-permute-done.22.refs_2_.refs_6_.refs_10_.refs_14_
  234.8 5.0 %shard_map.468 = (bf16[4,48,1920]{2,1,0:T(8,128)(2,1)}, bf16[4,48,1536]{2,1,0:T(8,128)(2,1)}) custom-call(s32[3]{0:T(128)} %pad_add_fusion.places_ref, bf16[4,2,2,48,1920]{4,3,2,1,0:T(8,128)(2,1)} %bitcast.135, bf16[4,2,2,48,1920]{4,3,2,1,0:T(8,128)(2,1)} %bitcast.43.refs_1_.refs_5_.refs_9_.refs_13_, bf16[4,2,48,1920]{3,2,1,0:T(8,128)(2,1)} %copy-done.38, ...), custom_call_target="tpu_custom_call" | custom-call | bytes 8000000 | tf_op jit(solution)/shard_map/pallas_call | solution.py:599
  241.6 3.1 shard_map.470
  246.3 6.7 %shard_map.469 = f32[128,32,384]{2,1,0:T(8,128)} custom-call(s32[1]{0:T(128)} %bitcast.3.core_ref.refs_0_, s32[128]{0:T(128)} %order_ref.1, s32[128]{0:T(128)} %len_ref.3, s32[2,64]{1,0:T(2,128)} %get-tuple-element.228.off_ref, f32[2048,384]{1,0:T(8,128)} %get-tuple-element.229.mine_ref, bf16[2048,384]{1,0:T(8,128)(2,1)} %collective-permute-done.27.recv_ref), custom_call_target="tpu_custom_call" | custom-call | bytes 20000000 | tf_op jit(solution)/shard_map/pallas_call | solution.py:946
  253.0 3.2 collective-permute-done.26.refs_19_.refs_23_.refs_27_.refs_31_
  256.2 2.2 collective-permute-done.25.refs_3_.refs_7_.refs_11_.refs_15_
  258.4 5.0 %shard_map.471 = (f32[48,3456]{1,0:T(8,128)}, bf16[48,3456]{1,0:T(8,128)(2,1)}, bf16[48,3456]{1,0:T(8,128)(2,1)}, bf16[48,3456]{1,0:T(8,128)(2,1)}) custom-call(s32[3]{0:T(128)} %pad_add_fusion.places_ref, bf16[4,2,2,48,1920]{4,3,2,1,0:T(8,128)(2,1)} %bitcast.136, bf16[4,2,2,48,1920]{4,3,2,1,0:T(8,128)(2,1)} %bitcast.43.refs_1_.refs_5_.refs_9_.refs_13_, ...), custom_call_target="tpu_custom_call" | custom-call | bytes 8000000 | tf_op jit(solution)/shard_map/pallas_call | solution.py:599
  266.4 2.4 collective-permute-start.33
  268.8 2.3 collective-permute-start.34
  271.1 3.6 %collective-permute-done.28.refs_2_.refs_6_.refs_10_.refs_14_ = bf16[4,2,48,512]{3,2,1,0:T(8,128)(2,1)S(1)} collective-permute-done((bf16[4,2,48,512]{3,2,1,0:T(8,128)(2,1)}, bf16[4,2,48,512]{3,2,1,0:T(8,128)(2,1)S(1)}, u32[]{:S(2)}, u32[]{:S(2)}) %collective-permute-start.28) | collective-permute-done | bytes 393248 | tf_op jit(solution)/shard_map/ppermute | solution.py:44
  275.8 2.7 shard_map.472
  278.6 1.6 collective-permute-start.31
  281.3 8.6 %collective-permute-done.33.refs_10_ = bf16[48,3456]{1,0:T(8,128)(2,1)S(1)} collective-permute-done((bf16[48,3456]{1,0:T(8,128)(2,1)}, bf16[48,3456]{1,0:T(8,128)(2,1)S(1)}, u32[]{:S(2)}, u32[]{:S(2)}) %collective-permute-start.33) | collective-permute-done | bytes 331808 | tf_op jit(solution)/shard_map/ppermute | solution.py:44
  291.6 3.0 shard_map.473
  294.6 6.7 %collective-permute-start.35 = (bf16[48,1152]{1,0:T(8,128)(2,1)}, bf16[48,1152]{1,0:T(8,128)(2,1)S(1)}, u32[]{:S(2)}, u32[]{:S(2)}) collective-permute-start(bf16[48,1152]{1,0:T(8,128)(2,1)} %get-tuple-element.250), channel_id=1, source_target_pairs={{0,8},{2,10},{4,12},{6,14},{8,16},{10,18},{12,20},{14,22},{16,24},... | collective-permute-start | bytes 331784 | tf_op jit(solution)/shard_map/ppermute | solution.py:44
  301.2 2.8 collective-permute-start.36
  304.1 2.2 shard_map.474
  308.7 2.1 reshape.163
  314.5 2.9 collective-permute-start.40
  317.4 2.0 collective-permute-done.40
  320.4 3.8 %collective-permute-done.41 = f32[80,128]{1,0:T(8,128)S(1)} collective-permute-done((f32[80,128]{1,0:T(8,128)S(1)}, f32[80,128]{1,0:T(8,128)S(1)}, u32[]{:S(2)}, u32[]{:S(2)}) %collective-permute-start.41) | collective-permute-done | bytes 40992 | tf_op jit(solution)/shard_map/ppermute | solution.py:89
  325.4 2.8 collective-permute-done.42
  329.8 2.5 collective-permute-done.43
  (230 shorter events, 56.2 us)
Async XLA Ops:
  2.6 13.1 %collective-permute-start = (bf16[48,1536]{1,0:T(8,128)(2,1)S(1)}, bf16[48,1536]{1,0:T(8,128)(2,1)S(1)}, u32[]{:S(2)}, u32[]{:S(2)}) collective-permute-start(bf16[48,1536]{1,0:T(8,128)(2,1)S(1)} %pad_maximum_fusion.5), channel_id=1, source_target_pairs={{0,8},{2,10},{4,12},{6,14},{8,16},{10,18},{12,20},{14,22},{16,24},... | collective-permute-start | bytes 442376 | tf_op jit(solution)/shard_map/ppermute | solution.py:44
  5.6 12.3 %collective-permute-start.1 = (bf16[48,1536]{1,0:T(8,128)(2,1)S(1)}, bf16[48,1536]{1,0:T(8,128)(2,1)S(1)}, u32[]{:S(2)}, u32[]{:S(2)}) collective-permute-start(bf16[48,1536]{1,0:T(8,128)(2,1)S(1)} %pad_maximum_fusion.5), channel_id=1, source_target_pairs={{0,16},{2,18},{4,20},{6,22},{8,24},{10,26},{12,28},{14,30},{16,0},... | collective-permute-start | bytes 442376 | tf_op jit(solution)/shard_map/ppermute | solution.py:44
  8.2 9.7 %collective-permute-start.2 = (bf16[48,1536]{1,0:T(8,128)(2,1)S(1)}, bf16[48,1536]{1,0:T(8,128)(2,1)S(1)}, u32[]{:S(2)}, u32[]{:S(2)}) collective-permute-start(bf16[48,1536]{1,0:T(8,128)(2,1)S(1)} %pad_maximum_fusion.5), channel_id=1, source_target_pairs={{0,24},{2,26},{4,28},{6,30},{8,0},{10,2},{12,4},{14,6},{16,8},{18,... | collective-permute-start | bytes 442376 | tf_op jit(solution)/shard_map/ppermute | solution.py:44
  11.7 18.3 %all-to-all-start = ((f32[16,4,768]{2,1,0:T(4,128)}), f32[16,4,768]{2,1,0:T(4,128)S(1)}, u32[]{:S(2)}, u32[]{:S(2)}) async-start(f32[16,4,768]{2,1,0:T(4,128)} %bitcast.105), calls=%async_computation | async-start | bytes 393216 | tf_op jit(solution)/shard_map/all_to_all | solution.py:763
  18.3 23.0 %collective-permute-start.3 = (bf16[4,48,768]{2,1,0:T(8,128)(2,1)S(1)}, bf16[4,48,768]{2,1,0:T(8,128)(2,1)S(1)}, u32[]{:S(2)}, u32[]{:S(2)}) collective-permute-start(bf16[4,48,768]{2,1,0:T(8,128)(2,1)S(1)} %get-tuple-element.164), channel_id=1, source_target_pairs={{0,4},{2,6},{4,0},{6,2},{8,12},{10,14},{12,8},{14,10},{16,20},{18,... | collective-permute-start | bytes 884744 | tf_op jit(solution)/shard_map/ppermute | solution.py:44
  19.9 21.5 %collective-permute-start.4 = (bf16[4,48,768]{2,1,0:T(8,128)(2,1)S(1)}, bf16[4,48,768]{2,1,0:T(8,128)(2,1)S(1)}, u32[]{:S(2)}, u32[]{:S(2)}) collective-permute-start(bf16[4,48,768]{2,1,0:T(8,128)(2,1)S(1)} %get-tuple-element.166), channel_id=1, source_target_pairs={{0,2},{2,0},{4,6},{6,4},{8,10},{10,8},{12,14},{14,12},{16,18},{18,... | collective-permute-start | bytes 884744 | tf_op jit(solution)/shard_map/ppermute | solution.py:44
  21.4 11.7 %collective-permute-start.5 = (bf16[48,1536]{1,0:T(8,128)(2,1)S(1)}, bf16[48,1536]{1,0:T(8,128)(2,1)S(1)}, u32[]{:S(2)}, u32[]{:S(2)}) collective-permute-start(bf16[48,1536]{1,0:T(8,128)(2,1)S(1)} %convert_element_type.25), channel_id=1, source_target_pairs={{0,24},{2,26},{4,28},{6,30},{8,0},{10,2},{12,4},{14,6},{16,8},{18,... | collective-permute-start | bytes 442376 | tf_op jit(solution)/shard_map/ppermute | solution.py:44
  29.3 12.0 %collective-permute-start.6 = (bf16[48,1536]{1,0:T(8,128)(2,1)S(1)}, bf16[48,1536]{1,0:T(8,128)(2,1)S(1)}, u32[]{:S(2)}, u32[]{:S(2)}) collective-permute-start(bf16[48,1536]{1,0:T(8,128)(2,1)S(1)} %convert_element_type.25), channel_id=1, source_target_pairs={{0,16},{2,18},{4,20},{6,22},{8,24},{10,26},{12,28},{14,30},{16,0},... | collective-permute-start | bytes 442376 | tf_op jit(solution)/shard_map/ppermute | solution.py:44
  29.3 12.0 %collective-permute-start.7 = (bf16[48,1536]{1,0:T(8,128)(2,1)S(1)}, bf16[48,1536]{1,0:T(8,128)(2,1)S(1)}, u32[]{:S(2)}, u32[]{:S(2)}) collective-permute-start(bf16[48,1536]{1,0:T(8,128)(2,1)S(1)} %convert_element_type.25), channel_id=1, source_target_pairs={{0,8},{2,10},{4,12},{6,14},{8,16},{10,18},{12,20},{14,22},{16,24},... | collective-permute-start | bytes 442376 | tf_op jit(solution)/shard_map/ppermute | solution.py:44
  42.2 14.6 %collective-permute-start.8 = (bf16[4,2,48,768]{3,2,0,1:T(8,128)(2,1)S(1)}, bf16[4,2,48,768]{3,2,0,1:T(8,128)(2,1)}, u32[]{:S(2)}, u32[]{:S(2)}) collective-permute-start(bf16[4,2,48,768]{3,2,0,1:T(8,128)(2,1)S(1)} %maximum_select_fusion.6), channel_id=1, source_target_pairs={{0,2},{2,0},{4,6},{6,4},{8,10},{10,8},{12,14},{14,12},{16,18},{18,... | collective-permute-start | bytes 1769480 | tf_op jit(solution)/shard_map/ppermute | solution.py:44
  42.9 14.1 %collective-permute-start.9 = (bf16[4,2,48,768]{3,2,0,1:T(8,128)(2,1)S(1)}, bf16[4,2,48,768]{3,2,0,1:T(8,128)(2,1)}, u32[]{:S(2)}, u32[]{:S(2)}) collective-permute-start(bf16[4,2,48,768]{3,2,0,1:T(8,128)(2,1)S(1)} %maximum_select_fusion.7), channel_id=1, source_target_pairs={{0,4},{2,6},{4,0},{6,2},{8,12},{10,14},{12,8},{14,10},{16,20},{18,... | collective-permute-start | bytes 1769480 | tf_op jit(solution)/shard_map/ppermute | solution.py:44
  43.6 11.5 %collective-permute-start.10 = (bf16[48,1536]{1,0:T(8,128)(2,1)S(1)}, bf16[48,1536]{1,0:T(8,128)(2,1)S(1)}, u32[]{:S(2)}, u32[]{:S(2)}) collective-permute-start(bf16[48,1536]{1,0:T(8,128)(2,1)S(1)} %bitcast_convert_fusion), channel_id=1, source_target_pairs={{0,24},{2,26},{4,28},{6,30},{8,0},{10,2},{12,4},{14,6},{16,8},{18,... | collective-permute-start | bytes 442376 | tf_op jit(solution)/shard_map/ppermute | solution.py:44
  43.7 13.0 %collective-permute-start.11 = (bf16[48,1536]{1,0:T(8,128)(2,1)S(1)}, bf16[48,1536]{1,0:T(8,128)(2,1)S(1)}, u32[]{:S(2)}, u32[]{:S(2)}) collective-permute-start(bf16[48,1536]{1,0:T(8,128)(2,1)S(1)} %bitcast_convert_fusion), channel_id=1, source_target_pairs={{0,16},{2,18},{4,20},{6,22},{8,24},{10,26},{12,28},{14,30},{16,0},... | collective-permute-start | bytes 442376 | tf_op jit(solution)/shard_map/ppermute | solution.py:44
  44.3 12.4 %collective-permute-start.12 = (bf16[48,1536]{1,0:T(8,128)(2,1)S(1)}, bf16[48,1536]{1,0:T(8,128)(2,1)S(1)}, u32[]{:S(2)}, u32[]{:S(2)}) collective-permute-start(bf16[48,1536]{1,0:T(8,128)(2,1)S(1)} %bitcast_convert_fusion), channel_id=1, source_target_pairs={{0,8},{2,10},{4,12},{6,14},{8,16},{10,18},{12,20},{14,22},{16,24},... | collective-permute-start | bytes 442376 | tf_op jit(solution)/shard_map/ppermute | solution.py:44
  60.3 21.0 %collective-permute-start.15 = (bf16[768,1536]{1,0:T(8,128)(2,1)S(1)}, bf16[768,1536]{1,0:T(8,128)(2,1)S(1)}, u32[]{:S(2)}, u32[]{:S(2)}) collective-permute-start(bf16[768,1536]{1,0:T(8,128)(2,1)S(1)} %pad_maximum_fusion.refs_4_.refs_5_.refs_6_.refs_7_), channel_id=1, source_target_pairs={{0,1},{1,0},{2,3},{3,2},{4,5},{5,4},{6,7},{7,6},{8,9},{9,8},{10,11... | collective-permute-start | bytes 7077896 | tf_op jit(solution)/shard_map/ppermute | solution.py:53
  61.7 14.7 %collective-permute-start.13 = (bf16[4,48,1536]{2,1,0:T(8,128)(2,1)S(1)}, bf16[4,48,1536]{2,1,0:T(8,128)(2,1)S(1)}, u32[]{:S(2)}, u32[]{:S(2)}) collective-permute-start(bf16[4,48,1536]{2,1,0:T(8,128)(2,1)S(1)} %get-tuple-element.303), channel_id=1, source_target_pairs={{0,4},{2,6},{4,0},{6,2},{8,12},{10,14},{12,8},{14,10},{16,20},{18,... | collective-permute-start | bytes 1769480 | tf_op jit(solution)/shard_map/ppermute | solution.py:44
  63.1 15.0 %collective-permute-start.14 = (bf16[4,48,1536]{2,1,0:T(8,128)(2,1)S(1)}, bf16[4,48,1536]{2,1,0:T(8,128)(2,1)S(1)}, u32[]{:S(2)}, u32[]{:S(2)}) collective-permute-start(bf16[4,48,1536]{2,1,0:T(8,128)(2,1)S(1)} %get-tuple-element.297), channel_id=1, source_target_pairs={{0,2},{2,0},{4,6},{6,4},{8,10},{10,8},{12,14},{14,12},{16,18},{18,... | collective-permute-start | bytes 1769480 | tf_op jit(solution)/shard_map/ppermute | solution.py:44
  76.6 26.6 %collective-permute-start.16 = (bf16[4,2,48,1536]{3,2,0,1:T(8,128)(2,1)S(1)}, bf16[4,2,48,1536]{3,2,0,1:T(8,128)(2,1)}, u32[]{:S(2)}, u32[]{:S(2)}) collective-permute-start(bf16[4,2,48,1536]{3,2,0,1:T(8,128)(2,1)S(1)} %maximum_select_fusion.2), channel_id=1, source_target_pairs={{0,2},{2,0},{4,6},{6,4},{8,10},{10,8},{12,14},{14,12},{16,18},{18,... | collective-permute-start | bytes 3538952 | tf_op jit(solution)/shard_map/ppermute | solution.py:44
  79.4 26.4 %collective-permute-start.17 = (bf16[4,2,48,1536]{3,2,0,1:T(8,128)(2,1)}, bf16[4,2,48,1536]{3,2,0,1:T(8,128)(2,1)}, u32[]{:S(2)}, u32[]{:S(2)}) collective-permute-start(bf16[4,2,48,1536]{3,2,0,1:T(8,128)(2,1)} %maximum_select_fusion.3), channel_id=1, source_target_pairs={{0,4},{2,6},{4,0},{6,2},{8,12},{10,14},{12,8},{14,10},{16,20},{18,... | collective-permute-start | bytes 3538952 | tf_op jit(solution)/shard_map/ppermute | solution.py:44
  108.0 4.6 %collective-permute-start.18 = (bf16[768,1536]{1,0:T(8,128)(2,1)S(1)}, bf16[768,1536]{1,0:T(8,128)(2,1)S(1)}, u32[]{:S(2)}, u32[]{:S(2)}) collective-permute-start(bf16[768,1536]{1,0:T(8,128)(2,1)S(1)} %bitcast.151), channel_id=1, source_target_pairs={{0,1},{1,0},{2,3},{3,2},{4,5},{5,4},{6,7},{7,6},{8,9},{9,8},{10,11... | collective-permute-start | bytes 7077896 | tf_op jit(solution)/shard_map/ppermute | solution.py:53
  111.8 4.6 %collective-permute-start.19 = (bf16[768,1536]{1,0:T(8,128)(2,1)S(1)}, bf16[768,1536]{1,0:T(8,128)(2,1)S(1)}, u32[]{:S(2)}, u32[]{:S(2)}) collective-permute-start(bf16[768,1536]{1,0:T(8,128)(2,1)S(1)} %bitcast.153), channel_id=1, source_target_pairs={{0,1},{1,0},{2,3},{3,2},{4,5},{5,4},{6,7},{7,6},{8,9},{9,8},{10,11... | collective-permute-start | bytes 7077896 | tf_op jit(solution)/shard_map/ppermute | solution.py:53
  184.1 9.2 %collective-permute-start.20 = (bf16[768,1920]{1,0:T(8,128)(2,1)}, bf16[768,1920]{1,0:T(8,128)(2,1)}, u32[]{:S(2)}, u32[]{:S(2)}) collective-permute-start(bf16[768,1920]{1,0:T(8,128)(2,1)} %get-tuple-element.200), channel_id=1, source_target_pairs={{0,1},{1,0},{2,3},{3,2},{4,5},{5,4},{6,7},{7,6},{8,9},{9,8},{10,11... | collective-permute-start | bytes 8847368 | tf_op jit(solution)/shard_map/ppermute | solution.py:53
  184.4 9.0 %collective-permute-start.21 = (bf16[768,1536]{1,0:T(8,128)(2,1)}, bf16[768,1536]{1,0:T(8,128)(2,1)}, u32[]{:S(2)}, u32[]{:S(2)}) collective-permute-start(bf16[768,1536]{1,0:T(8,128)(2,1)} %get-tuple-element.202), channel_id=1, source_target_pairs={{0,1},{1,0},{2,3},{3,2},{4,5},{5,4},{6,7},{7,6},{8,9},{9,8},{10,11... | collective-permute-start | bytes 7077896 | tf_op jit(solution)/shard_map/ppermute | solution.py:53
  186.4 14.0 %all-to-all-start.1 = ((f32[16,4,768]{2,1,0:T(4,128)}), f32[16,4,768]{2,1,0:T(4,128)}, u32[]{:S(2)}, u32[]{:S(2)}) async-start(f32[16,4,768]{2,1,0:T(4,128)} %reshape.160), calls=%async_computation.1 | async-start | bytes 393216 | tf_op jit(solution)/shard_map/all_to_all | solution.py:898
  200.4 32.8 %collective-permute-start.22 = (bf16[4,2,48,1920]{3,2,1,0:T(8,128)(2,1)}, bf16[4,2,48,1920]{3,2,1,0:T(8,128)(2,1)S(1)}, u32[]{:S(2)}, u32[]{:S(2)}) collective-permute-start(bf16[4,2,48,1920]{3,2,1,0:T(8,128)(2,1)} %get-tuple-element.206), channel_id=1, source_target_pairs={{0,2},{2,0},{4,6},{6,4},{8,10},{10,8},{12,14},{14,12},{16,18},{18,... | collective-permute-start | bytes 4423688 | tf_op jit(solution)/shard_map/ppermute | solution.py:44
  201.4 29.2 %collective-permute-start.23 = (bf16[4,2,48,1536]{3,2,1,0:T(8,128)(2,1)}, bf16[4,2,48,1536]{3,2,1,0:T(8,128)(2,1)}, u32[]{:S(2)}, u32[]{:S(2)}) collective-permute-start(bf16[4,2,48,1536]{3,2,1,0:T(8,128)(2,1)} %get-tuple-element.207), channel_id=1, source_target_pairs={{0,4},{2,6},{4,0},{6,2},{8,12},{10,14},{12,8},{14,10},{16,20},{18,... | collective-permute-start | bytes 3538952 | tf_op jit(solution)/shard_map/ppermute | solution.py:44
  234.3 5.5 %collective-permute-start.24 = (bf16[768,1152]{1,0:T(8,128)(2,1)}, bf16[768,1152]{1,0:T(8,128)(2,1)}, u32[]{:S(2)}, u32[]{:S(2)}) collective-permute-start(bf16[768,1152]{1,0:T(8,128)(2,1)} %get-tuple-element.216), channel_id=1, source_target_pairs={{0,1},{1,0},{2,3},{3,2},{4,5},{5,4},{6,7},{7,6},{8,9},{9,8},{10,11... | collective-permute-start | bytes 5308424 | tf_op jit(solution)/shard_map/ppermute | solution.py:53
  234.3 11.3 %collective-permute-start.27 = (bf16[2048,384]{1,0:T(8,128)(2,1)}, bf16[2048,384]{1,0:T(8,128)(2,1)}, u32[]{:S(2)}, u32[]{:S(2)}) collective-permute-start(bf16[2048,384]{1,0:T(8,128)(2,1)} %get-tuple-element.230), channel_id=1, source_target_pairs={{0,1},{1,0},{2,3},{3,2},{4,5},{5,4},{6,7},{7,6},{8,9},{9,8},{10,11... | collective-permute-start | bytes 4718600 | tf_op jit(solution)/shard_map/ppermute | solution.py:53
  239.8 18.6 %collective-permute-start.25 = (bf16[4,48,1920]{2,1,0:T(8,128)(2,1)}, bf16[4,48,1920]{2,1,0:T(8,128)(2,1)}, u32[]{:S(2)}, u32[]{:S(2)}) collective-permute-start(bf16[4,48,1920]{2,1,0:T(8,128)(2,1)} %get-tuple-element.225), channel_id=1, source_target_pairs={{0,4},{2,6},{4,0},{6,2},{8,12},{10,14},{12,8},{14,10},{16,20},{18,... | collective-permute-start | bytes 2211848 | tf_op jit(solution)/shard_map/ppermute | solution.py:44
  241.1 15.1 %collective-permute-start.26 = (bf16[4,48,1536]{2,1,0:T(8,128)(2,1)}, bf16[4,48,1536]{2,1,0:T(8,128)(2,1)}, u32[]{:S(2)}, u32[]{:S(2)}) collective-permute-start(bf16[4,48,1536]{2,1,0:T(8,128)(2,1)} %get-tuple-element.226), channel_id=1, source_target_pairs={{0,2},{2,0},{4,6},{6,4},{8,10},{10,8},{12,14},{14,12},{16,18},{18,... | collective-permute-start | bytes 1769480 | tf_op jit(solution)/shard_map/ppermute | solution.py:44
  263.4 12.4 %collective-permute-start.29 = (bf16[4,2,48,640]{3,2,1,0:T(8,128)(2,1)}, bf16[4,2,48,640]{3,2,1,0:T(8,128)(2,1)S(1)}, u32[]{:S(2)}, u32[]{:S(2)}) collective-permute-start(bf16[4,2,48,640]{3,2,1,0:T(8,128)(2,1)} %copy-done.35), channel_id=1, source_target_pairs={{0,4},{2,6},{4,0},{6,2},{8,12},{10,14},{12,8},{14,10},{16,20},{18,... | collective-permute-start | bytes 1474568 | tf_op jit(solution)/shard_map/ppermute | solution.py:44
  264.7 10.0 %collective-permute-start.28 = (bf16[4,2,48,512]{3,2,1,0:T(8,128)(2,1)}, bf16[4,2,48,512]{3,2,1,0:T(8,128)(2,1)S(1)}, u32[]{:S(2)}, u32[]{:S(2)}) collective-permute-start(bf16[4,2,48,512]{3,2,1,0:T(8,128)(2,1)} %copy-done.36), channel_id=1, source_target_pairs={{0,2},{2,0},{4,6},{6,4},{8,10},{10,8},{12,14},{14,12},{16,18},{18,... | collective-permute-start | bytes 1179656 | tf_op jit(solution)/shard_map/ppermute | solution.py:44
  265.3 15.2 %collective-permute-start.32 = (bf16[48,3456]{1,0:T(8,128)(2,1)}, bf16[48,3456]{1,0:T(8,128)(2,1)S(1)}, u32[]{:S(2)}, u32[]{:S(2)}) collective-permute-start(bf16[48,3456]{1,0:T(8,128)(2,1)} %get-tuple-element.244), channel_id=1, source_target_pairs={{0,8},{2,10},{4,12},{6,14},{8,16},{10,18},{12,20},{14,22},{16,24},... | collective-permute-start | bytes 995336 | tf_op jit(solution)/shard_map/ppermute | solution.py:44
  266.4 23.5 %collective-permute-start.33 = (bf16[48,3456]{1,0:T(8,128)(2,1)}, bf16[48,3456]{1,0:T(8,128)(2,1)S(1)}, u32[]{:S(2)}, u32[]{:S(2)}) collective-permute-start(bf16[48,3456]{1,0:T(8,128)(2,1)} %get-tuple-element.245), channel_id=1, source_target_pairs={{0,16},{2,18},{4,20},{6,22},{8,24},{10,26},{12,28},{14,30},{16,0},... | collective-permute-start | bytes 995336 | tf_op jit(solution)/shard_map/ppermute | solution.py:44
  268.8 21.9 %collective-permute-start.34 = (bf16[48,3456]{1,0:T(8,128)(2,1)}, bf16[48,3456]{1,0:T(8,128)(2,1)S(1)}, u32[]{:S(2)}, u32[]{:S(2)}) collective-permute-start(bf16[48,3456]{1,0:T(8,128)(2,1)} %get-tuple-element.246), channel_id=1, source_target_pairs={{0,24},{2,26},{4,28},{6,30},{8,0},{10,2},{12,4},{14,6},{16,8},{18,... | collective-permute-start | bytes 995336 | tf_op jit(solution)/shard_map/ppermute | solution.py:44
  278.6 12.8 %collective-permute-start.31 = (bf16[4,48,640]{2,1,0:T(8,128)(2,1)S(1)}, bf16[4,48,640]{2,1,0:T(8,128)(2,1)S(1)}, u32[]{:S(2)}, u32[]{:S(2)}) collective-permute-start(bf16[4,48,640]{2,1,0:T(8,128)(2,1)S(1)} %get-tuple-element.243), channel_id=1, source_target_pairs={{0,2},{2,0},{4,6},{6,4},{8,10},{10,8},{12,14},{14,12},{16,18},{18,... | collective-permute-start | bytes 737288 | tf_op jit(solution)/shard_map/ppermute | solution.py:44
  280.2 11.2 %collective-permute-start.30 = (bf16[4,48,512]{2,1,0:T(8,128)(2,1)S(1)}, bf16[4,48,512]{2,1,0:T(8,128)(2,1)S(1)}, u32[]{:S(2)}, u32[]{:S(2)}) collective-permute-start(bf16[4,48,512]{2,1,0:T(8,128)(2,1)S(1)} %get-tuple-element.242), channel_id=1, source_target_pairs={{0,4},{2,6},{4,0},{6,2},{8,12},{10,14},{12,8},{14,10},{16,20},{18,... | collective-permute-start | bytes 589832 | tf_op jit(solution)/shard_map/ppermute | solution.py:44
  291.4 14.9 %collective-permute-start.38 = (f32[16,4,768]{2,1,0:T(4,128)}, f32[16,4,768]{2,1,0:T(4,128)}, u32[]{:S(2)}, u32[]{:S(2)}) collective-permute-start(f32[16,4,768]{2,1,0:T(4,128)} %all-to-all-done.1), channel_id=1, source_target_pairs={{0,1},{1,0},{2,3},{3,2},{4,5},{5,4},{6,7},{7,6},{8,9},{9,8},{10,11... | collective-permute-start | bytes 589832 | tf_op jit(solution)/shard_map/ppermute | solution.py:53
  294.6 16.3 %collective-permute-start.35 = (bf16[48,1152]{1,0:T(8,128)(2,1)}, bf16[48,1152]{1,0:T(8,128)(2,1)S(1)}, u32[]{:S(2)}, u32[]{:S(2)}) collective-permute-start(bf16[48,1152]{1,0:T(8,128)(2,1)} %get-tuple-element.250), channel_id=1, source_target_pairs={{0,8},{2,10},{4,12},{6,14},{8,16},{10,18},{12,20},{14,22},{16,24},... | collective-permute-start | bytes 331784 | tf_op jit(solution)/shard_map/ppermute | solution.py:44
  301.2 10.9 %collective-permute-start.36 = (bf16[48,1152]{1,0:T(8,128)(2,1)}, bf16[48,1152]{1,0:T(8,128)(2,1)S(1)}, u32[]{:S(2)}, u32[]{:S(2)}) collective-permute-start(bf16[48,1152]{1,0:T(8,128)(2,1)} %get-tuple-element.251), channel_id=1, source_target_pairs={{0,16},{2,18},{4,20},{6,22},{8,24},{10,26},{12,28},{14,30},{16,0},... | collective-permute-start | bytes 331784 | tf_op jit(solution)/shard_map/ppermute | solution.py:44
  304.0 8.1 %collective-permute-start.37 = (bf16[48,1152]{1,0:T(8,128)(2,1)}, bf16[48,1152]{1,0:T(8,128)(2,1)S(1)}, u32[]{:S(2)}, u32[]{:S(2)}) collective-permute-start(bf16[48,1152]{1,0:T(8,128)(2,1)} %get-tuple-element.252), channel_id=1, source_target_pairs={{0,24},{2,26},{4,28},{6,30},{8,0},{10,2},{12,4},{14,6},{16,8},{18,... | collective-permute-start | bytes 331784 | tf_op jit(solution)/shard_map/ppermute | solution.py:44
  308.7 24.2 %copy-start.21 = (f32[1536,48]{0,1:T(8,128)S(1)}, f32[1536,48]{0,1:T(8,128)}, u32[]{:S(2)}) copy-start(f32[1536,48]{0,1:T(8,128)} %param.46) | copy-start | bytes 884740
  308.7 24.2 %copy-start.24 = (f32[3,48,384]{2,1,0:T(8,128)S(1)}, f32[3,48,384]{2,1,0:T(8,128)}, u32[]{:S(2)}) copy-start(f32[3,48,384]{2,1,0:T(8,128)} %refs_2_.1) | copy-start | bytes 663556
  313.3 1.2 collective-permute-start.39
  314.5 4.8 %collective-permute-start.40 = (f32[80,128]{1,0:T(8,128)S(1)}, f32[80,128]{1,0:T(8,128)S(1)}, u32[]{:S(2)}, u32[]{:S(2)}) collective-permute-start(f32[80,128]{1,0:T(8,128)S(1)} %add.61), channel_id=1, source_target_pairs={{0,8},{2,10},{4,12},{6,14},{8,0},{10,2},{12,4},{14,6},{16,24},{18,... | collective-permute-start | bytes 122888 | tf_op jit(solution)/shard_map/ppermute | solution.py:89
  319.3 4.9 %collective-permute-start.41 = (f32[80,128]{1,0:T(8,128)S(1)}, f32[80,128]{1,0:T(8,128)S(1)}, u32[]{:S(2)}, u32[]{:S(2)}) collective-permute-start(f32[80,128]{1,0:T(8,128)S(1)} %add.62), channel_id=1, source_target_pairs={{0,16},{2,18},{4,20},{6,22},{8,24},{10,26},{12,28},{14,30},{16,0},... | collective-permute-start | bytes 122888 | tf_op jit(solution)/shard_map/ppermute | solution.py:89
  324.2 4.0 %collective-permute-start.42 = (f32[80,128]{1,0:T(8,128)S(1)}, f32[80,128]{1,0:T(8,128)S(1)}, u32[]{:S(2)}, u32[]{:S(2)}) collective-permute-start(f32[80,128]{1,0:T(8,128)S(1)} %add.63), channel_id=1, source_target_pairs={{0,4},{2,6},{4,0},{6,2},{8,12},{10,14},{12,8},{14,10},{16,20},{18,... | collective-permute-start | bytes 122888 | tf_op jit(solution)/shard_map/ppermute | solution.py:89
  328.3 4.0 %collective-permute-start.43 = (f32[80,128]{1,0:T(8,128)S(1)}, f32[80,128]{1,0:T(8,128)S(1)}, u32[]{:S(2)}, u32[]{:S(2)}) collective-permute-start(f32[80,128]{1,0:T(8,128)S(1)} %add.64), channel_id=1, source_target_pairs={{0,2},{2,0},{4,6},{6,4},{8,10},{10,8},{12,14},{14,12},{16,18},{18,... | collective-permute-start | bytes 122888 | tf_op jit(solution)/shard_map/ppermute | solution.py:89
  (58 other events, 544.3 us)
where the time goes:
time: 336 us; the launch traced here: 335 us
  Pallas kernels  158 us (47%)
  waiting for transfers between devices  71.8 us (21%)
  starting transfers between devices  67.7 us (20%)
  local copies, waits for them, and re-layouts  20.7 us (6%)
  other arithmetic  15.6 us (5%)
    pallas_call x3, Pallas kernels, call(): pl.pallas_call(body, grid_spec=pltpu.PrefetchScalarGridSpec(num_scalar_pr...  114 us
    ppermute x31, waiting for transfers between devices, dp_shift(): return lax.ppermute(value, 'dp', pairs)  52.6 us
    ppermute x31, starting transfers between devices, dp_shift(): return lax.ppermute(value, 'dp', pairs)  50.6 us
    pallas_call x6, Pallas kernels, slab_sums(): pl.pallas_call(kernel, grid_spec=pltpu.PrefetchScalarGridSpec(num_scalar_...  24.1 us
    unnamed x121, local copies, waits for them, and re-layouts  11.1 us
    ppermute x4, waiting for transfers between devices, sum_all(): value = value + lax.ppermute(value, 'dp', pairs)  11.1 us
    select_n x8, other arithmetic, arrange(): jnp.where(place == 0, jnp.stack(pieces, axis), jnp.stack(pieces[::-1], ax...  9.99 us
    pallas_call x1, Pallas kernels, shards(): pl.pallas_call(pack_kernel, out_shape=(shape_of((most, width), BF), shape...  7.67 us
  transfers between devices with their start and end apart: 46, of which 24 were waited for; matrix products, arithmetic and copies ran while one was open for 5% of the time, Pallas kernels for 25%

commit v1 on v0

--- a/solution.py
+++ b/solution.py
@@ -1,3 +1,5 @@
+import functools
+
 import jax
 import jax.numpy as jnp
 from jax import lax
@@ -249,9 +251,9 @@
 
 
 def ffn_kernel(
-    last, core_ref, norm_ref, inv_ref, seg_ref, att_ref, vec_ref, high_ref, rest_ref,
+    last, core_ref, norm_ref, inv_ref, seg_ref, att_ref, vec_ref, high_ref, low_ref,
     w1_own, w1_other, w2_own, w2_other,
-    grad_ref, emb_ref, sums_ref, down_own, down_other, in_own, in_other,
+    grad_ref, emb_ref, sums_ref, down_own, down_other, in_own, in_other, rest_own, rest_other,
     sum1, sum2, sum3, act, slope, emb, counts, stage, sems,
 ):
     step = pl.program_id(0)
@@ -267,9 +269,6 @@
         emb[...] = jnp.zeros_like(emb)
         counts[...] = jnp.zeros_like(counts)
         sums_ref[...] = jnp.zeros_like(sums_ref)
-        sum1[...] = jnp.zeros_like(sum1)
-        sum2[...] = jnp.zeros_like(sum2)
-        sum3[...] = jnp.zeros_like(sum3)
 
     gain_one, shift_one = vec_ref[:, vec_at(4, width)], vec_ref[:, vec_at(5, width)]
     gain_two, shift_two = vec_ref[:, vec_at(6, width)], vec_ref[:, vec_at(7, width)]
@@ -300,41 +299,56 @@
     pick = pick.astype(BF)
     emb[...] += dot_nn(pick_across, final_high) + dot_nn(pick_across, final_rest)
     counts[...] += dot_nn(pick_across, jnp.ones((TILE, BLOCK), BF))
-    back = dot_nn(pick, high_ref[...]) + dot_nn(pick, rest_ref[...])
+    back = dot_nn(pick, high_ref[...]) + dot_nn(pick, low_ref[...])
     sums_ref[:, vec_at(6, width)] += column_sums(back * normed)
     sums_ref[:, vec_at(7, width)] += column_sums(back)
     grad_two = norm_back(back, normed, inverse, gain_two)
     ffn_low = grad_two.astype(BF)
     sums_ref[:, vec_at(3, width)] += column_sums(ffn_low.astype(F32))
-    grad_hidden = grad_two
+    grad_hidden, pres = grad_two, []
     for part in range(4):
         grad_act = dot_nn(ffn_low, w2[part][...])
         grad_pre = (grad_act * slope[part]).astype(BF)
         sums_ref[:, hidden_at[part]] += column_sums(grad_pre.astype(F32))
         grad_hidden = grad_hidden + dot_nt(grad_pre, w1[part][...])
-        sum1[part] += dot_tn(hidden_low, grad_pre)
-        sum2[part] += dot_tn(ffn_low, act[part])
+        pres.append(grad_pre)
     normed_one = norm_ref[...]
     sums_ref[:, vec_at(4, width)] += column_sums(grad_hidden * normed_one)
     sums_ref[:, vec_at(5, width)] += column_sums(grad_hidden)
     grad_one = norm_back(grad_hidden, normed_one, inv_ref[:, :1], gain_one)
     grad_ref[...] = grad_one
     grad_low = grad_one.astype(BF)
+    sums_ref[:, vec_at(2, width)] += column_sums(grad_low.astype(F32))
+
+    fresh = step == 0
+    rest = (rest_own, rest_other)
+    places, at = [], 0
+    for outs, sums in (((down_own, down_other), sum2), ((in_own, in_other), sum1)):
+        cut = outs[0].shape[1] - width
+        for index in (2, 3, 0, 1):
+            out = outs[index // 2]
+            if index % 2 == 0:
+                targets = [(0, out.at[:, pl.ds(0, width)])]
+            else:
+                targets = [(0, out.at[:, pl.ds(width, cut)]), (cut, rest[index // 2].at[:, pl.ds(at, width - cut)])]
+            places.append((sums.at[index], targets))
+        at += width - cut
+    for index in (1, 0):
+        places.append((sum3.at[index], [(0, rest[index].at[:, pl.ds(at, half)])]))
+    for part in range(4):
+        sum2[part] = jnp.where(fresh, 0.0, sum2[part]) + dot_tn(ffn_low, act[part])
+    pl.when(last)(lambda: store_sums(places[:4], stage, sems))
+    for part in range(4):
+        sum1[part] = jnp.where(fresh, 0.0, sum1[part]) + dot_tn(hidden_low, pres[part])
     for part in range(2):
-        sum3[part] += dot_tn(grad_low, att_ref[:, part * half : (part + 1) * half])
-    sums_ref[:, vec_at(2, width)] += column_sums(grad_low.astype(F32))
+        sum3[part] = jnp.where(fresh, 0.0, sum3[part]) + dot_tn(
+            grad_low, att_ref[:, part * half : (part + 1) * half]
+        )
 
     @pl.when(last)
     def _():
-        places = []
-        for outs, sums in (((down_own, down_other), sum2), ((in_own, in_other), sum1)):
-            for index in (2, 3, 0, 1):
-                target = outs[index // 2].at[:, pl.ds(index % 2 * width, width)]
-                places.append((sums.at[index], target))
-            if sums is sum2:
-                for index in (1, 0):
-                    places.append((sum3.at[index], outs[index].at[:, pl.ds(2 * width, half)]))
-        store_sums(places, stage, sems)
+        store_sums(places[4:], stage, sems, 4)
+        stores_done(places, stage, sems)
         held = emb_ref.shape[0]
         number = jnp.maximum(counts[:held], 1.0)
         emb_ref[...] = emb[:held] / jnp.concatenate([number] * (width // BLOCK), axis=1)
@@ -351,7 +365,6 @@
     @pl.when(pl.program_id(0) == 0)
     def _():
         sums[...] = before_ref[...]
-        weights[...] = jnp.zeros_like(weights)
 
     grad_low = grad_ref[...].astype(BF)
     masks = head_masks()
@@ -402,28 +415,32 @@
     mine_ref[...] = dx[:, pl.ds(pl.multiple_of(core * half, half), half)]
     dx_ref[...] = dx[:, pl.ds(pl.multiple_of((1 - core) * half, half), half)].astype(BF)
     for part in range(2):
-        weights[part] += dot_tn(rows, dqkv_ref[:, part * 3 * half : (part + 1) * 3 * half])
+        before = jnp.where(pl.program_id(0) == 0, 0.0, weights[part])
+        weights[part] = before + dot_tn(rows, dqkv_ref[:, part * 3 * half : (part + 1) * 3 * half])
 
     @pl.when(last)
     def _():
-        store_sums([(weights.at[1], other), (weights.at[0], own)], stage, sems)
+        places = [(weights.at[1], [(0, other)]), (weights.at[0], [(0, own)])]
+        store_sums(places, stage, sems)
         for row in range(total_ref.shape[0]):
             lanes = sums[:, row * BLOCK : (row + 1) * BLOCK]
             total_ref[row : row + 1, :] = jnp.sum(lanes, axis=0, keepdims=True)
-
-
-def store_sums(places, stage, sems):
-    copies = []
-    for index, (source, target) in enumerate(places):
-        slot = index % 2
-        if index >= 2:
-            copies[index - 2].wait()
-        cols = source.shape[-1]
-        stage[slot, :, :cols] = source[...].astype(BF)
-        copies.append(pltpu.make_async_copy(stage.at[slot, :, pl.ds(0, cols)], target, sems.at[slot]))
-        copies[index].start()
-    copies[-2].wait()
-    copies[-1].wait()
+        stores_done(places, stage, sems)
+
+
+def store_sums(places, stage, sems, start=0):
+    for slot, (source, targets) in enumerate(places, start):
+        stage[slot, :, : source.shape[-1]] = source[...].astype(BF)
+        for index, (at, target) in enumerate(targets):
+            lanes = pl.ds(at, target.shape[-1])
+            pltpu.make_async_copy(stage.at[slot, :, lanes], target, sems.at[slot, index]).start()
+
+
+def stores_done(places, stage, sems):
+    for slot, (_, targets) in enumerate(places):
+        for index, (at, target) in enumerate(targets):
+            lanes = pl.ds(at, target.shape[-1])
+            pltpu.make_async_copy(stage.at[slot, :, lanes], target, sems.at[slot, index]).wait()
 
 
 def unpack_kernel(core_ref, order_ref, len_ref, off_ref, mine_ref, recv_ref, out_ref, *columns):
@@ -523,56 +540,60 @@
         return lanes.stop - lanes.start
 
 
-def slab_sums(sides, dims, joined=False, limit=SMALL_LIMIT):
+def slab_sums(sides, dims, joined=False, also=None, limit=SMALL_LIMIT):
     first = dims[0]
     places = jnp.stack([dp_place(dim) for dim in dims]).astype(jnp.int32)
     at_of = {dim: index for index, dim in enumerate(dims)}
-    nexts = [first if joined else side.order[0] for side in sides]
     lead = 1 if joined else first[0]
     operands, in_specs, plan = [], [], []
     out_shape, out_specs, targets = [], [], []
 
-    def index_map(term_dims, current, step, size, fixed):
+    def index_map(term_dims, current, step, left):
         def of(grid, at):
             index = []
             for dim in term_dims:
-                if dim == current:
-                    index.append(lax.rem(at[at_of[dim]] + step, size))
-                elif dim == first:
+                if dim == first and (dim in left or (dim == current and not joined)):
                     index.append(grid)
+                elif dim == current:
+                    index.append(lax.rem(at[at_of[dim]] + step, dim[0]))
                 else:
-                    index.append(at[at_of[dim]] if dim in fixed else 0)
+                    index.append(0 if dim in left else at[at_of[dim]])
             return (*index, 0, 0)
 
         return of
 
-    for number, (side, current) in enumerate(zip(sides, nexts)):
-        size = current[0]
+    for number, side in enumerate([*sides, *([also] if also else [])]):
+        main = number < len(sides)
+        current = first if joined and main else side.order[0]
         rows = side.terms[0][0].shape[-2]
         left = [dim for dim in side.terms[-1][1] if dim != current]
-        fixed = [dim for dim in dims if dim != current and dim not in left]
-        steps = range(size) if joined else range(1, size)
-        for step in steps:
+        rest = [dim[0] for dim in left if dim != first]
+        for step in range(current[0]) if joined else range(1, current[0]):
             ids = []
-            for array, term_dims, lanes in side.terms:
-                block, pick = [], []
-                for dim in term_dims:
-                    whole = dim in left and dim != first
-                    block.append(dim[0] if whole else 1)
-                    pick.append(slice(None) if whole else 0)
-                ids.append((len(operands), tuple(pick), lanes))
-                operands.append(array)
-                in_specs.append(
-                    pl.BlockSpec((*block, rows, array.shape[-1]), index_map(term_dims, current, step, size, fixed))
+            shared = ids if current != first or joined or step == 1 else plan[-1][0]
+            if shared is ids:
+                for array, term_dims, lanes in side.terms:
+                    block, pick = [], []
+                    for dim in term_dims:
+                        whole = dim in left and dim != first
+                        block.append(dim[0] if whole else 1)
+                        pick.append(slice(None) if whole else 0)
+                    ids.append((len(operands), tuple(pick), lanes))
+                    operands.append(array)
+                    spec = (*block, rows, array.shape[-1])
+                    in_specs.append(pl.BlockSpec(spec, index_map(term_dims, current, step, left)))
+            plan.append((shared, number, step))
+            if joined and main:
+                continue
+            over = main and not joined
+            shape = (lead if over else 1, *rest, rows, side.cols())
+            out_shape.append(shape_of(shape, F32 if step == 0 else BF))
+            out_specs.append(
+                pl.BlockSpec(
+                    (1, *shape[1:]), lambda grid, at, n=len(shape), over=over: (grid if over else 0,) + (0,) * (n - 1)
                 )
-            plan.append((ids, number, step))
-        if not joined:
-            rest = [dim[0] for dim in left if dim != first]
-            for step in steps:
-                shape = (lead, *rest, rows, side.cols())
-                out_shape.append(shape_of(shape, BF))
-                out_specs.append(pl.BlockSpec((1, *shape[1:]), lambda grid, at, n=len(shape): (grid,) + (0,) * (n - 1)))
-                targets.append((number, step))
+            )
+            targets.append((number, step))
     if joined:
         width = sum(side.cols() for side in sides)
         rows = sides[0].terms[0][0].shape[-2]
@@ -584,17 +605,30 @@
 
     def kernel(places_ref, *refs):
         ins, outs = refs[: len(operands)], refs[len(operands) :]
-        for ids, number, step in plan:
+
+        def total_of(ids):
             total = None
             for index, pick, lanes in ids:
                 value = ins[index][(*pick, slice(None), lanes)].astype(F32)
                 total = value if total is None else total + value
-            if joined:
+            return total
+
+        def keep(out, ids):
+            out[0] = total_of(ids).astype(out.dtype)
+
+        for ids, number, step in plan:
+            if number >= len(sides):
+                out = outs[targets.index((number, step))]
+                if also.order[0] == first:
+                    here = lax.rem(places_ref[0] + step, first[0])
+                else:
+                    here = 0
+                pl.when(pl.program_id(0) == here)(lambda out=out, ids=ids: keep(out, ids))
+            elif joined:
                 out = outs[targets.index((None, step))]
-                out[:, starts[number] : starts[number] + sides[number].cols()] = total.astype(out.dtype)
+                out[:, starts[number] : starts[number] + sides[number].cols()] = total_of(ids).astype(out.dtype)
             else:
-                out = outs[targets.index((number, step))]
-                out[0] = total.astype(BF)
+                keep(outs[targets.index((number, step))], ids)
 
     sums = pl.pallas_call(
         kernel,
@@ -605,9 +639,11 @@
         compiler_params=params(limit),
         cost_estimate=cost(0, 8e6),
     )(places, *operands)
+    more = [value[0] for value, (which, _) in zip(sums, targets) if which == len(sides)]
     if joined:
-        return sums
-    return [[value for value, (which, _) in zip(sums, targets) if which == number] for number in range(len(sides))]
+        return [value for value, (which, _) in zip(sums, targets) if which is None], more
+    lists = [[value for value, (which, _) in zip(sums, targets) if which == number] for number in range(len(sides))]
+    return [*lists, more] if also else lists
 
 
 def adam_moments(grad_value, moment, square):
@@ -632,18 +668,23 @@
     return norms + jnp.where(jnp.logical_and(row < 2, lane == matrix), here, 0.0)
 
 
-def ffn_update_kernel(own_ref, *refs):
+def ffn_update_kernel(count, own_ref, rest_ref, *refs):
     states, arrived, outs = refs[:9], refs[9:-13], refs[-13:]
-    total = own_ref[...]
-    for ref in arrived:
+    total, rest = own_ref[...], rest_ref[...]
+    for ref in arrived[:count]:
         total = total + ref[...].astype(F32)
+    for ref in arrived[count:]:
+        rest = rest + ref[...].astype(F32)
     norms = jnp.zeros(outs[12].shape, F32)
-    down = states[6].shape[1]
-    out = states[0].shape[1]
-    lanes = (slice(down, down + out), slice(down + out, total.shape[1]), slice(0, down))
+    cut = states[6].shape[1] - BLOCK
+    grads = (
+        rest[:, 3 * BLOCK :],
+        jnp.concatenate([total[:, cut:], rest[:, BLOCK : 3 * BLOCK]], axis=1),
+        jnp.concatenate([total[:, :cut], rest[:, :BLOCK]], axis=1),
+    )
     for index in range(3):
         weight, moment, square = states[3 * index : 3 * index + 3]
-        grad = total[:, lanes[index]]
+        grad = grads[index]
         moment_new, square_new, scaled = adam_moments(grad, moment[...], square[...])
         update = scaled + weight_decay * weight[...]
         for target, value in zip(outs[4 * index :], (grad, moment_new, square_new, update)):
@@ -833,9 +874,12 @@
     normed, ffn_pieces = lax.optimization_barrier((normed, ffn_pieces))
 
     w1, w2 = [(value, swap_core(value)) for value in gather_end(gather_in(ffn, ffn_pieces))]
-    down_shape = shape_of((width, 2 * width + half), BF)
-    in_shape = shape_of((width, 2 * width), BF)
-    grad_one, emb, vec_ffn, down_own, down_other, in_own, in_other = tiled_call(
+    down_shape = shape_of((width, 2 * width - BLOCK), BF)
+    in_shape = shape_of((width, 2 * width - 2 * BLOCK), BF)
+    rest_shape = shape_of((width, half + 3 * BLOCK), BF)
+    (
+        grad_one, emb, vec_ffn, down_own, down_other, in_own, in_other, rest_own, rest_other,
+    ) = tiled_call(
         ffn_kernel,
         out_shape=(
             shape_of((most, width), F32),
@@ -845,13 +889,15 @@
             down_shape,
             in_shape,
             in_shape,
+            rest_shape,
+            rest_shape,
         ),
         in_specs=[
             SMEM_SPEC, tile_spec(width), tile_spec(BLOCK), tile_spec(BLOCK), tile_spec(width), vec_spec,
         ]
         + [held_spec(BLOCK, width)] * 2
         + [long_spec] * 4,
-        out_specs=(tile_spec(width), held_spec(mine, width), held_spec(8, vectors.shape[0])) + (HBM_SPEC,) * 4,
+        out_specs=(tile_spec(width), held_spec(mine, width), held_spec(8, vectors.shape[0])) + (HBM_SPEC,) * 6,
         scratch_shapes=[
             pltpu.VMEM((4, width, width), F32),
             pltpu.VMEM((4, width, width), F32),
@@ -860,8 +906,8 @@
             pltpu.VMEM((4, TILE, width), F32),
             pltpu.VMEM((BLOCK, width), F32),
             pltpu.VMEM((BLOCK, BLOCK), F32),
-            pltpu.VMEM((2, width, width), BF),
-            pltpu.SemaphoreType.DMA((2,)),
+            pltpu.VMEM((10, width, width), BF),
+            pltpu.SemaphoreType.DMA((10, 2)),
         ],
         cost_estimate=cost(2 * row_total * 24 * width * width, 30e6),
     )(
@@ -878,10 +924,11 @@
             sides.append(Side(terms, orders[side][::-1]))
         return sides
 
-    def scatter_out(sides, limit=SMALL_LIMIT):
+    def scatter_out(sides, limit=SMALL_LIMIT, also=None):
         if len({side.order[0][0] for side in sides}) == 1:
-            return slab_sums(sides, dims, limit=limit)
-        return [slab_sums([side], dims, limit=limit)[0] for side in sides]
+            return slab_sums(sides, dims, also=also, limit=limit)
+        heads = [slab_sums([side], dims, limit=limit)[0] for side in sides[:-1]]
+        return heads + slab_sums(sides[-1:], dims, also=also, limit=limit)
 
     def scatter_go(sides, slabs):
         return [scatter_send(sent, side.order[0]) for side, sent in zip(sides, slabs)]
@@ -897,13 +944,15 @@
     def go_pooled(value):
         return lax.all_to_all(value, "dp", 0, 0, tiled=True)
 
-    come = [swap_core(down_other), swap_core(in_other)]
+    come = [swap_core(down_other), swap_core(in_other), swap_core(rest_other)]
     grad_send = scatter_start(
-        ((slice(0, 2 * width + half), down_own, come[0]), (slice(0, 2 * width), in_own, come[1]))
+        ((slice(0, down_shape.shape[1]), down_own, come[0]), (slice(0, in_shape.shape[1]), in_own, come[1]))
     )
-    slabs = scatter_out(grad_send, VMEM_LIMIT)
+    (rest_send,) = scatter_start(((slice(0, rest_shape.shape[1]), rest_own, come[2]),))
+    rest_send.order = dims[:1] + others[::-1]
+    *slabs, rest_slabs = scatter_out(grad_send, VMEM_LIMIT, rest_send)
     pooled = go_pooled(emb.reshape(count, share // 2, width)) if share % 2 == 0 else emb
-    tiles, slabs, pooled = lax.optimization_barrier((tiles, slabs, pooled))
+    tiles, slabs, rest_slabs, pooled = lax.optimization_barrier((tiles, slabs, rest_slabs, pooled))
     qkv_shape = shape_of((width, 3 * half), BF)
     dx_mine, dx_other, vec_local, own, other = tiled_call(
         attn_backward_kernel,
@@ -927,17 +976,18 @@
             pltpu.VMEM((8, vectors.shape[0]), F32),
             pltpu.VMEM((2, width, 3 * half), F32),
             pltpu.VMEM((2, width, 3 * half), BF),
-            pltpu.SemaphoreType.DMA((2,)),
+            pltpu.SemaphoreType.DMA((2, 1)),
         ],
         cost_estimate=cost(2 * row_total * 18 * width * width, 30e6),
     )(tiles, most, core_word, grad_one, rows, qkv, seg, vec_ffn, *weights)
-    arrived, own, other, dx_other = lax.optimization_barrier(
-        (scatter_go(grad_send, slabs), own, other, dx_other)
+    arrived, rest_arrived, own, other, dx_other = lax.optimization_barrier(
+        (scatter_go(grad_send, slabs), scatter_go([rest_send], [rest_slabs]), own, other, dx_other)
     )
     grad_send = scatter_in(grad_send, arrived)
-    slabs = scatter_out(grad_send, VMEM_LIMIT)
+    (rest_send,) = scatter_in([rest_send], rest_arrived)
+    *slabs, rest_slabs = scatter_out(grad_send, VMEM_LIMIT, rest_send)
     come = swap_core(other)
-    own, come, slabs = lax.optimization_barrier((own, come, slabs))
+    own, come, slabs, rest_slabs = lax.optimization_barrier((own, come, slabs, rest_slabs))
     cut = 3 * half // (2 * BLOCK) * BLOCK
     qkv_send = scatter_start(((slice(0, cut), own, come), (slice(cut, 3 * half), own, come)))
     qkv_slabs = scatter_out(qkv_send)
@@ -952,20 +1002,24 @@
         compiler_params=params(),
         cost_estimate=cost(0, 20e6),
     )(core_word, order_word, lengths, offsets, dx_mine, swap_core(dx_other))
-    arrived, tokens_grad, qkv_slabs = lax.optimization_barrier(
-        (scatter_go(grad_send, slabs), tokens_grad, qkv_slabs)
+    arrived, rest_arrived, tokens_grad, qkv_slabs = lax.optimization_barrier(
+        (scatter_go(grad_send, slabs), scatter_go([rest_send], [rest_slabs]), tokens_grad, qkv_slabs)
     )
     grad_send = scatter_in(grad_send, arrived)
-    ffn_grad, *slabs = slab_sums(grad_send, dims, joined=True, limit=VMEM_LIMIT)
+    (rest_send,) = scatter_in([rest_send], rest_arrived)
+    (ffn_grad, *slabs), (rest_grad, *rest_slabs) = slab_sums(
+        grad_send, dims, joined=True, also=rest_send, limit=VMEM_LIMIT
+    )
     qkv_slabs, slabs = lax.optimization_barrier((qkv_slabs, slabs))
     last_go = scatter_send(slabs, first)
     go = scatter_go(qkv_send, qkv_slabs)
     qkv_send = scatter_in(qkv_send, go)
     while qkv_send[0].order:
         go = scatter_go(qkv_send, scatter_out(qkv_send))
-        go, last_go, pooled = lax.optimization_barrier((go, last_go, pooled))
+        go, last_go, pooled, rest_slabs = lax.optimization_barrier((go, last_go, pooled, rest_slabs))
         qkv_send = scatter_in(qkv_send, go)
-    qkv_grad, *slabs = slab_sums(qkv_send, dims, joined=True)
+    rest_go = scatter_send(rest_slabs, rest_send.order[0])
+    (qkv_grad, *slabs), _ = slab_sums(qkv_send, dims, joined=True)
     go = scatter_send(slabs, first)
 
     both = flip(jnp.stack([pooled, swap_core(pooled)]))
@@ -983,13 +1037,13 @@
     ]
     shapes = [shape_of(state[0].shape, F32) for state in ffn_states for _ in range(4)]
     *ffn_new, norms = pl.pallas_call(
-        ffn_update_kernel,
+        functools.partial(ffn_update_kernel, len(last_go)),
         out_shape=shapes + [shape_of((8, BLOCK), F32)],
-        in_specs=[VMEM_SPEC] * (10 + len(last_go)),
+        in_specs=[VMEM_SPEC] * (11 + len(last_go) + len(rest_go)),
         out_specs=[VMEM_SPEC] * 13,
         compiler_params=params(SMALL_LIMIT),
         cost_estimate=cost(0, 4e6),
-    )(ffn_grad, *[value for state in ffn_states for value in state], *last_go)
+    )(ffn_grad, rest_grad, *[value for state in ffn_states for value in state], *last_go, *rest_go)
     out_grad, out_m, out_s, out_u, in_grad, in_m, in_s, in_u, down_grad, down_m, down_s, down_u = ffn_new
     lines = vectors.shape[0] // BLOCK
     like = [shape_of(qkv_weight.shape, F32)]

time: 336 us -> 328 us (0.976)
  waiting for transfers between devices: 71.8 us -> 60.8 us
  starting transfers between devices: 67.7 us -> 73.7 us
  Pallas kernels: 158 us -> 154 us
    ppermute x31 -> x36, waiting for transfers between devices: 52.6 us -> 45.5 us  [dp_shift(): return lax.ppermute(value, 'dp', pairs)]
    pallas_call x3, Pallas kernels: 114 us -> 110 us  [call(): pl.pallas_call(body, grid_spec=pltpu.PrefetchScalarGridSpec(num_scalar_pr...]
    ppermute x31 -> x36, starting transfers between devices: 50.6 us -> 55 us  [dp_shift(): return lax.ppermute(value, 'dp', pairs)]
    unnamed x121 -> x113, local copies, waits for them, and re-layouts: 11.1 us -> 13.3 us
  transfers between devices with their start and end apart: 46 -> 52, of which waited for: 24 -> 21; matrix products, arithmetic and copies ran while one was open for 5% -> 5% of each run, Pallas kernels for 25% -> 26%
where the time goes in v1:
time: 328 us; the launch traced here: 327 us
  Pallas kernels  154 us (47%)
  starting transfers between devices  73.7 us (22%)
  waiting for transfers between devices  60.8 us (19%)
  local copies, waits for them, and re-layouts  20 us (6%)
  other arithmetic  16.7 us (5%)
    pallas_call x3, Pallas kernels, call(): pl.pallas_call(body, grid_spec=pltpu.PrefetchScalarGridSpec(num_scalar_pr...  110 us
    ppermute x36, starting transfers between devices, dp_shift(): return lax.ppermute(value, 'dp', pairs)  55 us
    ppermute x36, waiting for transfers between devices, dp_shift(): return lax.ppermute(value, 'dp', pairs)  45.5 us
    pallas_call x6, Pallas kernels, slab_sums(): pl.pallas_call(kernel, grid_spec=pltpu.PrefetchScalarGridSpec(num_scalar_...  24.6 us
    unnamed x113, local copies, waits for them, and re-layouts  13.3 us
    select_n x8, other arithmetic, arrange(): jnp.where(place == 0, jnp.stack(pieces, axis), jnp.stack(pieces[::-1], ax...  10.1 us
    ppermute x4, waiting for transfers between devices, sum_all(): value = value + lax.ppermute(value, 'dp', pairs)  9.56 us
    ppermute x4, starting transfers between devices, sum_all(): value = value + lax.ppermute(value, 'dp', pairs)  8.15 us
  transfers between devices with their start and end apart: 52, of which 21 were waited for; matrix products, arithmetic and copies ran while one was open for 5% of the time, Pallas kernels for 26%

profile of v1, /device:TPU:0, one launch (start us, length us, event | category | flops | bytes accessed | tf_op | source)
XLA Modules:
  0.0 327.2 jit_solution(4184879453183973717)
XLA Ops:
  2.6 3.1 collective-permute-start
  5.7 2.6 collective-permute-start.1
  10.8 3.9 %all-to-all-start = ((f32[16,4,768]{2,1,0:T(4,128)}), f32[16,4,768]{2,1,0:T(4,128)S(1)}, u32[]{:S(2)}, u32[]{:S(2)}) async-start(f32[16,4,768]{2,1,0:T(4,128)} %bitcast.113), calls=%async_computation | async-start | bytes 393216 | tf_op jit(solution)/shard_map/all_to_all | solution.py:804
  14.8 3.2 collective-permute-done.1
  18.4 1.6 collective-permute-start.3
  21.5 7.9 %collective-permute-start.5 = (bf16[48,1536]{1,0:T(8,128)(2,1)S(1)}, bf16[48,1536]{1,0:T(8,128)(2,1)S(1)}, u32[]{:S(2)}, u32[]{:S(2)}) collective-permute-start(bf16[48,1536]{1,0:T(8,128)(2,1)S(1)} %convert_element_type.25), channel_id=1, source_target_pairs={{0,24},{2,26},{4,28},{6,30},{8,0},{10,2},{12,4},{14,6},{16,8},{18,... | collective-permute-start | bytes 442376 | tf_op jit(solution)/shard_map/ppermute | solution.py:46
  30.1 3.1 collective-permute-done.5
  33.2 8.2 %collective-permute-done.6 = bf16[48,1536]{1,0:T(8,128)(2,1)S(1)} collective-permute-done((bf16[48,1536]{1,0:T(8,128)(2,1)S(1)}, bf16[48,1536]{1,0:T(8,128)(2,1)S(1)}, u32[]{:S(2)}, u32[]{:S(2)}) %collective-permute-start.6) | collective-permute-done | bytes 147488 | tf_op jit(solution)/shard_map/ppermute | solution.py:46
  44.0 1.9 collective-permute-start.12
  47.1 7.6 %shard_map.463 = (bf16[2048,768]{1,0:T(8,128)(2,1)}, f32[2048,128]{1,0:T(8,128)}, s32[2,64]{1,0:T(2,128)}, s32[1]{0:T(128)}) custom-call(s32[1]{0:T(128)} %bitcast.3.core_ref.refs_0_, s32[128]{0:T(128)} %order_ref.1, s32[128]{0:T(128)} %len_ref.3, bf16[128,32,768]{2,1,0:T(8,128)(2,1)} %tok_ref.1), custom_call_target="tpu_custom_call" | custom-call | bytes 30000000 | tf_op jit(solution)/shard_map/pallas_call | solution.py:824
  54.7 1.6 collective-permute-done.11
  63.6 1.6 collective-permute-start.14
  65.9 9.8 %collective-permute-done.13 = bf16[4,48,1536]{2,1,0:T(8,128)(2,1)S(1)} collective-permute-done((bf16[4,48,1536]{2,1,0:T(8,128)(2,1)S(1)}, bf16[4,48,1536]{2,1,0:T(8,128)(2,1)S(1)}, u32[]{:S(2)}, u32[]{:S(2)}) %collective-permute-start.13) | collective-permute-done | bytes 589856 | tf_op jit(solution)/shard_map/ppermute | solution.py:46
  75.9 1.6 collective-permute-start.16
  82.5 19.3 %shard_map.464 = (bf16[2048,2304]{1,0:T(8,128)(2,1)}, bf16[2048,768]{1,0:T(8,128)(2,1)}, f32[2048,768]{1,0:T(8,128)}, f32[2048,128]{1,0:T(8,128)}) custom-call(s32[1]{0:T(128)} %get-tuple-element.233.tiles_ref, s32[1]{0:T(128)} %bitcast.3.core_ref.refs_0_, bf16[2048,768]{1,0:T(8,128)(2,1)} %get-tuple-element.202.refs_1_.refs_2_, ...), custom_call_target="tpu_custom_call" | custom-call | flops 11596411904 | bytes 30000000 | tf_op jit(solution)/shard_map/pallas_call | solution.py:509
  103.4 2.2 collective-permute-done.17
  105.6 2.0 maximum_select_fusion
  107.9 3.5 %maximum_select_fusion.1 = bf16[4,2,2,48,1536]{4,3,0,2,1:T(8,128)(2,1)S(1)} fusion(bf16[4,1,2,48,1536]{4,3,0,2,1:T(8,128)(2,1)} %bitcast.40, bf16[4,1,2,48,1536]{4,3,0,2,1:T(8,128)(2,1)} %bitcast.39, pred[]{:T(512)S(6)} %eq.30), kind=kLoop, calls=%fused_computation.3 | loop fusion | flops 3538944 | bytes 4718593 | tf_op jit(solution)/shard_map/jit(_where)/select_n | solution.py:62
  113.0 3.2 collective-permute-done.19.refs_11_
  117.7 62.8 %shard_map.465 = (f32[2048,768]{1,0:T(8,128)}, f32[64,768]{1,0:T(8,128)}, f32[8,9216]{1,0:T(8,128)}, bf16[768,1408]{1,0:T(8,128)(2,1)}, bf16[768,1408]{1,0:T(8,1...) custom-call(s32[1]{0:T(128)} %get-tuple-element.233.tiles_ref, ...), custom_call_target="tpu_custom_call" | custom-call | flops 34789236736 | bytes 30000000 | tf_op jit(solution)/shard_map/pallas_call | solution.py:509
  181.2 1.7 reshape.168
  182.9 5.4 %all-to-all-start.1 = ((f32[16,4,768]{2,1,0:T(4,128)}), f32[16,4,768]{2,1,0:T(4,128)}, u32[]{:S(2)}, u32[]{:S(2)}) async-start(f32[16,4,768]{2,1,0:T(4,128)} %reshape.168), calls=%async_computation.1 | async-start | bytes 393216 | tf_op jit(solution)/shard_map/all_to_all | solution.py:945
  191.8 5.8 %shard_map.466 = (bf16[4,2,48,1408]{3,2,1,0:T(8,128)(2,1)}, bf16[4,2,48,1280]{3,2,1,0:T(8,128)(2,1)}, bf16[1,2,2,48,768]{4,3,2,1,0:T(8,128)(2,1)}, bf16[1,2,2,48...) custom-call(s32[3]{0:T(128)} %pad_add_fusion.places_ref, bf16[4,2,2,48,1408]{4,3,2,1,0:T(8,128)(2,1)} %bitcast.143, ...), custom_call_target="tpu_custom_call" | custom-call | bytes 8000000 | tf_op jit(solution)/shard_map/pallas_call | solution.py:633
  197.7 1.6 collective-permute-start.23
  202.0 2.3 collective-permute-start.26
  204.3 1.6 collective-permute-start.27
  205.8 27.9 %shard_map.467 = (f32[2048,384]{1,0:T(8,128)}, bf16[2048,384]{1,0:T(8,128)(2,1)}, f32[72,128]{1,0:T(8,128)}, bf16[768,1152]{1,0:T(8,128)(2,1)}, bf16[768,1152]{1,0:T(8,128)(2,1)}) custom-call(s32[1]{0:T(128)} %get-tuple-element.233.tiles_ref, s32[1]{0:T(128)} %bitcast.3.core_ref.refs_0_, f32[2048,768]{1,0:T(8,128)} %get-tuple-element.234.refs_1_, ...), custom_call_target="tpu_custom_call" | custom-call | flops 26091925504 | bytes 30000000 | tf_op jit(solution)/shard_map/pallas_call | solution.py:509
  235.2 5.2 %shard_map.468 = (bf16[4,48,1408]{2,1,0:T(8,128)(2,1)}, bf16[4,48,1280]{2,1,0:T(8,128)(2,1)}, bf16[1,2,48,768]{3,2,1,0:T(8,128)(2,1)}) custom-call(s32[3]{0:T(128)} %pad_add_fusion.places_ref, bf16[4,2,2,48,1408]{4,3,2,1,0:T(8,128)(2,1)} %bitcast.144, bf16[4,2,2,48,1408]{4,3,2,1,0:T(8,128)(2,1)} %bitcast.43.refs_1_.refs_5_.refs_9_.refs_13_, ...), custom_call_target="tpu_custom_call" | custom-call | bytes 8000000 | tf_op jit(solution)/shard_map/pallas_call | solution.py:633
  243.0 3.1 shard_map.470
  247.8 6.7 %shard_map.469 = f32[128,32,384]{2,1,0:T(8,128)} custom-call(s32[1]{0:T(128)} %bitcast.3.core_ref.refs_0_, s32[128]{0:T(128)} %order_ref.1, s32[128]{0:T(128)} %len_ref.3, s32[2,64]{1,0:T(2,128)} %get-tuple-element.258.off_ref, f32[2048,384]{1,0:T(8,128)} %get-tuple-element.259.mine_ref, bf16[2048,384]{1,0:T(8,128)(2,1)} %collective-permute-done.32.recv_ref), custom_call_target="tpu_custom_call" | custom-call | bytes 20000000 | tf_op jit(solution)/shard_map/pallas_call | solution.py:996
  254.4 3.2 collective-permute-done.31.refs_37_.refs_43_
  258.2 4.8 %shard_map.471 = (f32[1,48,768]{2,1,0:T(8,128)}, bf16[1,48,768]{2,1,0:T(8,128)(2,1)}, f32[48,2688]{1,0:T(8,128)}, bf16[48,2688]{1,0:T(8,128)(2,1)}, bf16[48,2688]{1,0:T(8,128)(2,1)}, /*index=5*/bf16[48,2688]{1,0:T(8,128)(2,1)}) custom-call(s32[3]{0:T(128)} %pad_add_fusion.places_ref, bf16[4,2,2,48,1408]{4,3,2,1,0:T(8,128)(2,1)} %bitcast.145, ...), custom_call_target="tpu_custom_call" | custom-call | bytes 8000000 | tf_op jit(solution)/shard_map/pallas_call | solution.py:633
  263.0 1.6 collective-permute-start.34
  266.2 3.0 collective-permute-start.39
  269.2 5.5 %collective-permute-done.33.refs_2_.refs_6_.refs_10_.refs_14_ = bf16[4,2,48,512]{3,2,1,0:T(8,128)(2,1)S(1)} collective-permute-done((bf16[4,2,48,512]{3,2,1,0:T(8,128)(2,1)}, bf16[4,2,48,512]{3,2,1,0:T(8,128)(2,1)S(1)}, u32[]{:S(2)}, u32[]{:S(2)}) %collective-permute-start.33) | collective-permute-done | bytes 393248 | tf_op jit(solution)/shard_map/ppermute | solution.py:46
  275.6 2.7 shard_map.472
  278.4 1.6 collective-permute-start.36
  280.8 4.7 %collective-permute-done.38.refs_10_ = bf16[48,2688]{1,0:T(8,128)(2,1)S(1)} collective-permute-done((bf16[48,2688]{1,0:T(8,128)(2,1)}, bf16[48,2688]{1,0:T(8,128)(2,1)S(1)}, u32[]{:S(2)}, u32[]{:S(2)}) %collective-permute-start.38) | collective-permute-done | bytes 258080 | tf_op jit(solution)/shard_map/ppermute | solution.py:46
  288.3 2.9 shard_map.473
  291.9 4.3 %collective-permute-start.40 = (bf16[48,1152]{1,0:T(8,128)(2,1)}, bf16[48,1152]{1,0:T(8,128)(2,1)S(1)}, u32[]{:S(2)}, u32[]{:S(2)}) collective-permute-start(bf16[48,1152]{1,0:T(8,128)(2,1)} %get-tuple-element.282), channel_id=1, source_target_pairs={{0,8},{2,10},{4,12},{6,14},{8,16},{10,18},{12,20},{14,22},{16,24},... | collective-permute-start | bytes 331784 | tf_op jit(solution)/shard_map/ppermute | solution.py:46
  296.6 2.0 collective-permute-start.42
  298.7 2.9 shard_map.474
  306.8 2.8 collective-permute-start.46
  309.7 2.0 collective-permute-done.46
  311.6 2.5 collective-permute-start.47
  314.2 2.4 collective-permute-done.47
  317.8 2.7 collective-permute-done.48
  322.1 2.5 collective-permute-done.49
  (234 shorter events, 59.4 us)
Async XLA Ops:
  2.6 12.2 %collective-permute-start = (bf16[48,1536]{1,0:T(8,128)(2,1)S(1)}, bf16[48,1536]{1,0:T(8,128)(2,1)S(1)}, u32[]{:S(2)}, u32[]{:S(2)}) collective-permute-start(bf16[48,1536]{1,0:T(8,128)(2,1)S(1)} %pad_maximum_fusion.5), channel_id=1, source_target_pairs={{0,8},{2,10},{4,12},{6,14},{8,16},{10,18},{12,20},{14,22},{16,24},... | collective-permute-start | bytes 442376 | tf_op jit(solution)/shard_map/ppermute | solution.py:46
  5.7 12.3 %collective-permute-start.1 = (bf16[48,1536]{1,0:T(8,128)(2,1)S(1)}, bf16[48,1536]{1,0:T(8,128)(2,1)S(1)}, u32[]{:S(2)}, u32[]{:S(2)}) collective-permute-start(bf16[48,1536]{1,0:T(8,128)(2,1)S(1)} %pad_maximum_fusion.5), channel_id=1, source_target_pairs={{0,16},{2,18},{4,20},{6,22},{8,24},{10,26},{12,28},{14,30},{16,0},... | collective-permute-start | bytes 442376 | tf_op jit(solution)/shard_map/ppermute | solution.py:46
  8.3 9.7 %collective-permute-start.2 = (bf16[48,1536]{1,0:T(8,128)(2,1)S(1)}, bf16[48,1536]{1,0:T(8,128)(2,1)S(1)}, u32[]{:S(2)}, u32[]{:S(2)}) collective-permute-start(bf16[48,1536]{1,0:T(8,128)(2,1)S(1)} %pad_maximum_fusion.5), channel_id=1, source_target_pairs={{0,24},{2,26},{4,28},{6,30},{8,0},{10,2},{12,4},{14,6},{16,8},{18,... | collective-permute-start | bytes 442376 | tf_op jit(solution)/shard_map/ppermute | solution.py:46
  10.8 19.3 %all-to-all-start = ((f32[16,4,768]{2,1,0:T(4,128)}), f32[16,4,768]{2,1,0:T(4,128)S(1)}, u32[]{:S(2)}, u32[]{:S(2)}) async-start(f32[16,4,768]{2,1,0:T(4,128)} %bitcast.113), calls=%async_computation | async-start | bytes 393216 | tf_op jit(solution)/shard_map/all_to_all | solution.py:804
  18.4 23.0 %collective-permute-start.3 = (bf16[4,48,768]{2,1,0:T(8,128)(2,1)S(1)}, bf16[4,48,768]{2,1,0:T(8,128)(2,1)S(1)}, u32[]{:S(2)}, u32[]{:S(2)}) collective-permute-start(bf16[4,48,768]{2,1,0:T(8,128)(2,1)S(1)} %get-tuple-element.181), channel_id=1, source_target_pairs={{0,4},{2,6},{4,0},{6,2},{8,12},{10,14},{12,8},{14,10},{16,20},{18,... | collective-permute-start | bytes 884744 | tf_op jit(solution)/shard_map/ppermute | solution.py:46
  20.0 21.4 %collective-permute-start.4 = (bf16[4,48,768]{2,1,0:T(8,128)(2,1)S(1)}, bf16[4,48,768]{2,1,0:T(8,128)(2,1)S(1)}, u32[]{:S(2)}, u32[]{:S(2)}) collective-permute-start(bf16[4,48,768]{2,1,0:T(8,128)(2,1)S(1)} %get-tuple-element.183), channel_id=1, source_target_pairs={{0,2},{2,0},{4,6},{6,4},{8,10},{10,8},{12,14},{14,12},{16,18},{18,... | collective-permute-start | bytes 884744 | tf_op jit(solution)/shard_map/ppermute | solution.py:46
  21.5 11.7 %collective-permute-start.5 = (bf16[48,1536]{1,0:T(8,128)(2,1)S(1)}, bf16[48,1536]{1,0:T(8,128)(2,1)S(1)}, u32[]{:S(2)}, u32[]{:S(2)}) collective-permute-start(bf16[48,1536]{1,0:T(8,128)(2,1)S(1)} %convert_element_type.25), channel_id=1, source_target_pairs={{0,24},{2,26},{4,28},{6,30},{8,0},{10,2},{12,4},{14,6},{16,8},{18,... | collective-permute-start | bytes 442376 | tf_op jit(solution)/shard_map/ppermute | solution.py:46
  29.4 12.0 %collective-permute-start.6 = (bf16[48,1536]{1,0:T(8,128)(2,1)S(1)}, bf16[48,1536]{1,0:T(8,128)(2,1)S(1)}, u32[]{:S(2)}, u32[]{:S(2)}) collective-permute-start(bf16[48,1536]{1,0:T(8,128)(2,1)S(1)} %convert_element_type.25), channel_id=1, source_target_pairs={{0,16},{2,18},{4,20},{6,22},{8,24},{10,26},{12,28},{14,30},{16,0},... | collective-permute-start | bytes 442376 | tf_op jit(solution)/shard_map/ppermute | solution.py:46
  29.4 12.0 %collective-permute-start.7 = (bf16[48,1536]{1,0:T(8,128)(2,1)S(1)}, bf16[48,1536]{1,0:T(8,128)(2,1)S(1)}, u32[]{:S(2)}, u32[]{:S(2)}) collective-permute-start(bf16[48,1536]{1,0:T(8,128)(2,1)S(1)} %convert_element_type.25), channel_id=1, source_target_pairs={{0,8},{2,10},{4,12},{6,14},{8,16},{10,18},{12,20},{14,22},{16,24},... | collective-permute-start | bytes 442376 | tf_op jit(solution)/shard_map/ppermute | solution.py:46
  41.6 14.8 %collective-permute-start.8 = (bf16[4,2,48,768]{3,2,0,1:T(8,128)(2,1)S(1)}, bf16[4,2,48,768]{3,2,0,1:T(8,128)(2,1)}, u32[]{:S(2)}, u32[]{:S(2)}) collective-permute-start(bf16[4,2,48,768]{3,2,0,1:T(8,128)(2,1)S(1)} %maximum_select_fusion.6), channel_id=1, source_target_pairs={{0,2},{2,0},{4,6},{6,4},{8,10},{10,8},{12,14},{14,12},{16,18},{18,... | collective-permute-start | bytes 1769480 | tf_op jit(solution)/shard_map/ppermute | solution.py:46
  42.3 14.1 %collective-permute-start.9 = (bf16[4,2,48,768]{3,2,0,1:T(8,128)(2,1)S(1)}, bf16[4,2,48,768]{3,2,0,1:T(8,128)(2,1)}, u32[]{:S(2)}, u32[]{:S(2)}) collective-permute-start(bf16[4,2,48,768]{3,2,0,1:T(8,128)(2,1)S(1)} %maximum_select_fusion.7), channel_id=1, source_target_pairs={{0,4},{2,6},{4,0},{6,2},{8,12},{10,14},{12,8},{14,10},{16,20},{18,... | collective-permute-start | bytes 1769480 | tf_op jit(solution)/shard_map/ppermute | solution.py:46
  43.1 11.6 %collective-permute-start.10 = (bf16[48,1536]{1,0:T(8,128)(2,1)S(1)}, bf16[48,1536]{1,0:T(8,128)(2,1)}, u32[]{:S(2)}, u32[]{:S(2)}) collective-permute-start(bf16[48,1536]{1,0:T(8,128)(2,1)S(1)} %bitcast_convert_fusion), channel_id=1, source_target_pairs={{0,24},{2,26},{4,28},{6,30},{8,0},{10,2},{12,4},{14,6},{16,8},{18,... | collective-permute-start | bytes 442376 | tf_op jit(solution)/shard_map/ppermute | solution.py:46
  43.2 13.2 %collective-permute-start.11 = (bf16[48,1536]{1,0:T(8,128)(2,1)S(1)}, bf16[48,1536]{1,0:T(8,128)(2,1)}, u32[]{:S(2)}, u32[]{:S(2)}) collective-permute-start(bf16[48,1536]{1,0:T(8,128)(2,1)S(1)} %bitcast_convert_fusion), channel_id=1, source_target_pairs={{0,16},{2,18},{4,20},{6,22},{8,24},{10,26},{12,28},{14,30},{16,0},... | collective-permute-start | bytes 442376 | tf_op jit(solution)/shard_map/ppermute | solution.py:46
  44.0 12.3 %collective-permute-start.12 = (bf16[48,1536]{1,0:T(8,128)(2,1)S(1)}, bf16[48,1536]{1,0:T(8,128)(2,1)}, u32[]{:S(2)}, u32[]{:S(2)}) collective-permute-start(bf16[48,1536]{1,0:T(8,128)(2,1)S(1)} %bitcast_convert_fusion), channel_id=1, source_target_pairs={{0,8},{2,10},{4,12},{6,14},{8,16},{10,18},{12,20},{14,22},{16,24},... | collective-permute-start | bytes 442376 | tf_op jit(solution)/shard_map/ppermute | solution.py:46
  59.7 21.5 %collective-permute-start.15 = (bf16[768,1536]{1,0:T(8,128)(2,1)S(1)}, bf16[768,1536]{1,0:T(8,128)(2,1)S(1)}, u32[]{:S(2)}, u32[]{:S(2)}) collective-permute-start(bf16[768,1536]{1,0:T(8,128)(2,1)S(1)} %pad_maximum_fusion.refs_4_.refs_5_.refs_6_.refs_7_), channel_id=1, source_target_pairs={{0,1},{1,0},{2,3},{3,2},{4,5},{5,4},{6,7},{7,6},{8,9},{9,8},{10,11... | collective-permute-start | bytes 7077896 | tf_op jit(solution)/shard_map/ppermute | solution.py:55
  61.1 14.6 %collective-permute-start.13 = (bf16[4,48,1536]{2,1,0:T(8,128)(2,1)S(1)}, bf16[4,48,1536]{2,1,0:T(8,128)(2,1)S(1)}, u32[]{:S(2)}, u32[]{:S(2)}) collective-permute-start(bf16[4,48,1536]{2,1,0:T(8,128)(2,1)S(1)} %get-tuple-element.337), channel_id=1, source_target_pairs={{0,4},{2,6},{4,0},{6,2},{8,12},{10,14},{12,8},{14,10},{16,20},{18,... | collective-permute-start | bytes 1769480 | tf_op jit(solution)/shard_map/ppermute | solution.py:46
  63.6 15.3 %collective-permute-start.14 = (bf16[4,48,1536]{2,1,0:T(8,128)(2,1)S(1)}, bf16[4,48,1536]{2,1,0:T(8,128)(2,1)S(1)}, u32[]{:S(2)}, u32[]{:S(2)}) collective-permute-start(bf16[4,48,1536]{2,1,0:T(8,128)(2,1)S(1)} %get-tuple-element.331), channel_id=1, source_target_pairs={{0,2},{2,0},{4,6},{6,4},{8,10},{10,8},{12,14},{14,12},{16,18},{18,... | collective-permute-start | bytes 1769480 | tf_op jit(solution)/shard_map/ppermute | solution.py:46
  75.9 27.4 %collective-permute-start.16 = (bf16[4,2,48,1536]{3,2,0,1:T(8,128)(2,1)S(1)}, bf16[4,2,48,1536]{3,2,0,1:T(8,128)(2,1)}, u32[]{:S(2)}, u32[]{:S(2)}) collective-permute-start(bf16[4,2,48,1536]{3,2,0,1:T(8,128)(2,1)S(1)} %maximum_select_fusion.2), channel_id=1, source_target_pairs={{0,2},{2,0},{4,6},{6,4},{8,10},{10,8},{12,14},{14,12},{16,18},{18,... | collective-permute-start | bytes 3538952 | tf_op jit(solution)/shard_map/ppermute | solution.py:46
  80.1 25.5 %collective-permute-start.17 = (bf16[4,2,48,1536]{3,2,0,1:T(8,128)(2,1)}, bf16[4,2,48,1536]{3,2,0,1:T(8,128)(2,1)}, u32[]{:S(2)}, u32[]{:S(2)}) collective-permute-start(bf16[4,2,48,1536]{3,2,0,1:T(8,128)(2,1)} %maximum_select_fusion.3), channel_id=1, source_target_pairs={{0,4},{2,6},{4,0},{6,2},{8,12},{10,14},{12,8},{14,10},{16,20},{18,... | collective-permute-start | bytes 3538952 | tf_op jit(solution)/shard_map/ppermute | solution.py:46
  111.6 4.6 %collective-permute-start.19 = (bf16[768,1536]{1,0:T(8,128)(2,1)S(1)}, bf16[768,1536]{1,0:T(8,128)(2,1)S(1)}, u32[]{:S(2)}, u32[]{:S(2)}) collective-permute-start(bf16[768,1536]{1,0:T(8,128)(2,1)S(1)} %bitcast.176), channel_id=1, source_target_pairs={{0,1},{1,0},{2,3},{3,2},{4,5},{5,4},{6,7},{7,6},{8,9},{9,8},{10,11... | collective-permute-start | bytes 7077896 | tf_op jit(solution)/shard_map/ppermute | solution.py:55
  180.5 10.1 %collective-permute-start.20 = (bf16[768,1408]{1,0:T(8,128)(2,1)}, bf16[768,1408]{1,0:T(8,128)(2,1)}, u32[]{:S(2)}, u32[]{:S(2)}) collective-permute-start(bf16[768,1408]{1,0:T(8,128)(2,1)} %get-tuple-element.217), channel_id=1, source_target_pairs={{0,1},{1,0},{2,3},{3,2},{4,5},{5,4},{6,7},{7,6},{8,9},{9,8},{10,11... | collective-permute-start | bytes 6488072 | tf_op jit(solution)/shard_map/ppermute | solution.py:55
  180.7 8.8 %collective-permute-start.21 = (bf16[768,1280]{1,0:T(8,128)(2,1)}, bf16[768,1280]{1,0:T(8,128)(2,1)S(1)}, u32[]{:S(2)}, u32[]{:S(2)}) collective-permute-start(bf16[768,1280]{1,0:T(8,128)(2,1)} %get-tuple-element.219), channel_id=1, source_target_pairs={{0,1},{1,0},{2,3},{3,2},{4,5},{5,4},{6,7},{7,6},{8,9},{9,8},{10,11... | collective-permute-start | bytes 5898248 | tf_op jit(solution)/shard_map/ppermute | solution.py:55
  181.0 8.5 %collective-permute-start.22 = (bf16[768,768]{1,0:T(8,128)(2,1)}, bf16[768,768]{1,0:T(8,128)(2,1)S(1)}, u32[]{:S(2)}, u32[]{:S(2)}) collective-permute-start(bf16[768,768]{1,0:T(8,128)(2,1)} %get-tuple-element.221), channel_id=1, source_target_pairs={{0,1},{1,0},{2,3},{3,2},{4,5},{5,4},{6,7},{7,6},{8,9},{9,8},{10,11... | collective-permute-start | bytes 3538952 | tf_op jit(solution)/shard_map/ppermute | solution.py:55
  182.9 14.8 %all-to-all-start.1 = ((f32[16,4,768]{2,1,0:T(4,128)}), f32[16,4,768]{2,1,0:T(4,128)}, u32[]{:S(2)}, u32[]{:S(2)}) async-start(f32[16,4,768]{2,1,0:T(4,128)} %reshape.168), calls=%async_computation.1 | async-start | bytes 393216 | tf_op jit(solution)/shard_map/all_to_all | solution.py:945
  197.7 36.2 %collective-permute-start.23 = (bf16[4,2,48,1408]{3,2,1,0:T(8,128)(2,1)}, bf16[4,2,48,1408]{3,2,1,0:T(8,128)(2,1)S(1)}, u32[]{:S(2)}, u32[]{:S(2)}) collective-permute-start(bf16[4,2,48,1408]{3,2,1,0:T(8,128)(2,1)} %get-tuple-element.228), channel_id=1, source_target_pairs={{0,2},{2,0},{4,6},{6,4},{8,10},{10,8},{12,14},{14,12},{16,18},{18,... | collective-permute-start | bytes 3244040 | tf_op jit(solution)/shard_map/ppermute | solution.py:46
  199.2 34.6 %collective-permute-start.24 = (bf16[4,2,48,1280]{3,2,1,0:T(8,128)(2,1)}, bf16[4,2,48,1280]{3,2,1,0:T(8,128)(2,1)}, u32[]{:S(2)}, u32[]{:S(2)}) collective-permute-start(bf16[4,2,48,1280]{3,2,1,0:T(8,128)(2,1)} %get-tuple-element.229), channel_id=1, source_target_pairs={{0,4},{2,6},{4,0},{6,2},{8,12},{10,14},{12,8},{14,10},{16,20},{18,... | collective-permute-start | bytes 2949128 | tf_op jit(solution)/shard_map/ppermute | solution.py:46
  200.4 33.3 %collective-permute-start.25 = (bf16[2,2,48,768]{3,2,1,0:T(8,128)(2,1)}, bf16[2,2,48,768]{3,2,1,0:T(8,128)(2,1)S(1)}, u32[]{:S(2)}, u32[]{:S(2)}) collective-permute-start(bf16[2,2,48,768]{3,2,1,0:T(8,128)(2,1)} %bitcast.191), channel_id=1, source_target_pairs={{0,8},{2,10},{4,12},{6,14},{8,16},{10,18},{12,20},{14,22},{16,24},... | collective-permute-start | bytes 884744 | tf_op jit(solution)/shard_map/ppermute | solution.py:46
  202.0 31.8 %collective-permute-start.26 = (bf16[2,2,48,768]{3,2,1,0:T(8,128)(2,1)}, bf16[2,2,48,768]{3,2,1,0:T(8,128)(2,1)S(1)}, u32[]{:S(2)}, u32[]{:S(2)}) collective-permute-start(bf16[2,2,48,768]{3,2,1,0:T(8,128)(2,1)} %bitcast.190), channel_id=1, source_target_pairs={{0,16},{2,18},{4,20},{6,22},{8,24},{10,26},{12,28},{14,30},{16,0},... | collective-permute-start | bytes 884744 | tf_op jit(solution)/shard_map/ppermute | solution.py:46
  204.3 29.5 %collective-permute-start.27 = (bf16[2,2,48,768]{3,2,1,0:T(8,128)(2,1)}, bf16[2,2,48,768]{3,2,1,0:T(8,128)(2,1)S(1)}, u32[]{:S(2)}, u32[]{:S(2)}) collective-permute-start(bf16[2,2,48,768]{3,2,1,0:T(8,128)(2,1)} %bitcast.189), channel_id=1, source_target_pairs={{0,24},{2,26},{4,28},{6,30},{8,0},{10,2},{12,4},{14,6},{16,8},{18,... | collective-permute-start | bytes 884744 | tf_op jit(solution)/shard_map/ppermute | solution.py:46
  234.6 5.8 %collective-permute-start.28 = (bf16[768,1152]{1,0:T(8,128)(2,1)}, bf16[768,1152]{1,0:T(8,128)(2,1)}, u32[]{:S(2)}, u32[]{:S(2)}) collective-permute-start(bf16[768,1152]{1,0:T(8,128)(2,1)} %get-tuple-element.241), channel_id=1, source_target_pairs={{0,1},{1,0},{2,3},{3,2},{4,5},{5,4},{6,7},{7,6},{8,9},{9,8},{10,11... | collective-permute-start | bytes 5308424 | tf_op jit(solution)/shard_map/ppermute | solution.py:55
  235.0 12.8 %collective-permute-start.32 = (bf16[2048,384]{1,0:T(8,128)(2,1)}, bf16[2048,384]{1,0:T(8,128)(2,1)}, u32[]{:S(2)}, u32[]{:S(2)}) collective-permute-start(bf16[2048,384]{1,0:T(8,128)(2,1)} %get-tuple-element.260), channel_id=1, source_target_pairs={{0,1},{1,0},{2,3},{3,2},{4,5},{5,4},{6,7},{7,6},{8,9},{9,8},{10,11... | collective-permute-start | bytes 4718600 | tf_op jit(solution)/shard_map/ppermute | solution.py:55
  240.4 17.2 %collective-permute-start.29 = (bf16[4,48,1408]{2,1,0:T(8,128)(2,1)}, bf16[4,48,1408]{2,1,0:T(8,128)(2,1)}, u32[]{:S(2)}, u32[]{:S(2)}) collective-permute-start(bf16[4,48,1408]{2,1,0:T(8,128)(2,1)} %get-tuple-element.254), channel_id=1, source_target_pairs={{0,4},{2,6},{4,0},{6,2},{8,12},{10,14},{12,8},{14,10},{16,20},{18,... | collective-permute-start | bytes 1622024 | tf_op jit(solution)/shard_map/ppermute | solution.py:46
  241.0 16.6 %collective-permute-start.30 = (bf16[4,48,1280]{2,1,0:T(8,128)(2,1)}, bf16[4,48,1280]{2,1,0:T(8,128)(2,1)}, u32[]{:S(2)}, u32[]{:S(2)}) collective-permute-start(bf16[4,48,1280]{2,1,0:T(8,128)(2,1)} %get-tuple-element.255), channel_id=1, source_target_pairs={{0,2},{2,0},{4,6},{6,4},{8,10},{10,8},{12,14},{14,12},{16,18},{18,... | collective-permute-start | bytes 1474568 | tf_op jit(solution)/shard_map/ppermute | solution.py:46
  242.5 15.0 %collective-permute-start.31 = (bf16[2,48,768]{2,1,0:T(8,128)(2,1)}, bf16[2,48,768]{2,1,0:T(8,128)(2,1)S(1)}, u32[]{:S(2)}, u32[]{:S(2)}) collective-permute-start(bf16[2,48,768]{2,1,0:T(8,128)(2,1)} %bitcast.192), channel_id=1, source_target_pairs={{0,2},{2,0},{4,6},{6,4},{8,10},{10,8},{12,14},{14,12},{16,18},{18,... | collective-permute-start | bytes 442376 | tf_op jit(solution)/shard_map/ppermute | solution.py:46
  263.0 12.6 %collective-permute-start.34 = (bf16[4,2,48,640]{3,2,1,0:T(8,128)(2,1)}, bf16[4,2,48,640]{3,2,1,0:T(8,128)(2,1)S(1)}, u32[]{:S(2)}, u32[]{:S(2)}) collective-permute-start(bf16[4,2,48,640]{3,2,1,0:T(8,128)(2,1)} %copy-done.36), channel_id=1, source_target_pairs={{0,4},{2,6},{4,0},{6,2},{8,12},{10,14},{12,8},{14,10},{16,20},{18,... | collective-permute-start | bytes 1474568 | tf_op jit(solution)/shard_map/ppermute | solution.py:46
  264.6 10.2 %collective-permute-start.33 = (bf16[4,2,48,512]{3,2,1,0:T(8,128)(2,1)}, bf16[4,2,48,512]{3,2,1,0:T(8,128)(2,1)S(1)}, u32[]{:S(2)}, u32[]{:S(2)}) collective-permute-start(bf16[4,2,48,512]{3,2,1,0:T(8,128)(2,1)} %copy-done.37), channel_id=1, source_target_pairs={{0,2},{2,0},{4,6},{6,4},{8,10},{10,8},{12,14},{14,12},{16,18},{18,... | collective-permute-start | bytes 1179656 | tf_op jit(solution)/shard_map/ppermute | solution.py:46
  265.4 15.4 %collective-permute-start.37 = (bf16[48,2688]{1,0:T(8,128)(2,1)}, bf16[48,2688]{1,0:T(8,128)(2,1)S(1)}, u32[]{:S(2)}, u32[]{:S(2)}) collective-permute-start(bf16[48,2688]{1,0:T(8,128)(2,1)} %get-tuple-element.275), channel_id=1, source_target_pairs={{0,8},{2,10},{4,12},{6,14},{8,16},{10,18},{12,20},{14,22},{16,24},... | collective-permute-start | bytes 774152 | tf_op jit(solution)/shard_map/ppermute | solution.py:46
  265.6 19.9 %collective-permute-start.38 = (bf16[48,2688]{1,0:T(8,128)(2,1)}, bf16[48,2688]{1,0:T(8,128)(2,1)S(1)}, u32[]{:S(2)}, u32[]{:S(2)}) collective-permute-start(bf16[48,2688]{1,0:T(8,128)(2,1)} %get-tuple-element.276), channel_id=1, source_target_pairs={{0,16},{2,18},{4,20},{6,22},{8,24},{10,26},{12,28},{14,30},{16,0},... | collective-permute-start | bytes 774152 | tf_op jit(solution)/shard_map/ppermute | solution.py:46
  266.2 19.9 %collective-permute-start.39 = (bf16[48,2688]{1,0:T(8,128)(2,1)}, bf16[48,2688]{1,0:T(8,128)(2,1)S(1)}, u32[]{:S(2)}, u32[]{:S(2)}) collective-permute-start(bf16[48,2688]{1,0:T(8,128)(2,1)} %get-tuple-element.277), channel_id=1, source_target_pairs={{0,24},{2,26},{4,28},{6,30},{8,0},{10,2},{12,4},{14,6},{16,8},{18,... | collective-permute-start | bytes 774152 | tf_op jit(solution)/shard_map/ppermute | solution.py:46
  278.4 8.5 %collective-permute-start.36 = (bf16[4,48,640]{2,1,0:T(8,128)(2,1)S(1)}, bf16[4,48,640]{2,1,0:T(8,128)(2,1)S(1)}, u32[]{:S(2)}, u32[]{:S(2)}) collective-permute-start(bf16[4,48,640]{2,1,0:T(8,128)(2,1)S(1)} %get-tuple-element.274), channel_id=1, source_target_pairs={{0,2},{2,0},{4,6},{6,4},{8,10},{10,8},{12,14},{14,12},{16,18},{18,... | collective-permute-start | bytes 737288 | tf_op jit(solution)/shard_map/ppermute | solution.py:46
  280.0 6.9 %collective-permute-start.35 = (bf16[4,48,512]{2,1,0:T(8,128)(2,1)S(1)}, bf16[4,48,512]{2,1,0:T(8,128)(2,1)S(1)}, u32[]{:S(2)}, u32[]{:S(2)}) collective-permute-start(bf16[4,48,512]{2,1,0:T(8,128)(2,1)S(1)} %get-tuple-element.273), channel_id=1, source_target_pairs={{0,4},{2,6},{4,0},{6,2},{8,12},{10,14},{12,8},{14,10},{16,20},{18,... | collective-permute-start | bytes 589832 | tf_op jit(solution)/shard_map/ppermute | solution.py:46
  286.9 14.8 %collective-permute-start.43 = (f32[16,4,768]{2,1,0:T(4,128)}, f32[16,4,768]{2,1,0:T(4,128)}, u32[]{:S(2)}, u32[]{:S(2)}) collective-permute-start(f32[16,4,768]{2,1,0:T(4,128)} %all-to-all-done.1), channel_id=1, source_target_pairs={{0,1},{1,0},{2,3},{3,2},{4,5},{5,4},{6,7},{7,6},{8,9},{9,8},{10,11... | collective-permute-start | bytes 589832 | tf_op jit(solution)/shard_map/ppermute | solution.py:55
  286.9 11.7 %collective-permute-start.44 = (bf16[48,768]{1,0:T(8,128)(2,1)}, bf16[48,768]{1,0:T(8,128)(2,1)}, u32[]{:S(2)}, u32[]{:S(2)}) collective-permute-start(bf16[48,768]{1,0:T(8,128)(2,1)} %bitcast.54), channel_id=1, source_target_pairs={{0,4},{2,6},{4,0},{6,2},{8,12},{10,14},{12,8},{14,10},{16,20},{18,... | collective-permute-start | bytes 221192 | tf_op jit(solution)/shard_map/ppermute | solution.py:46
  291.9 12.4 %collective-permute-start.40 = (bf16[48,1152]{1,0:T(8,128)(2,1)}, bf16[48,1152]{1,0:T(8,128)(2,1)S(1)}, u32[]{:S(2)}, u32[]{:S(2)}) collective-permute-start(bf16[48,1152]{1,0:T(8,128)(2,1)} %get-tuple-element.282), channel_id=1, source_target_pairs={{0,8},{2,10},{4,12},{6,14},{8,16},{10,18},{12,20},{14,22},{16,24},... | collective-permute-start | bytes 331784 | tf_op jit(solution)/shard_map/ppermute | solution.py:46
  296.2 8.3 %collective-permute-start.41 = (bf16[48,1152]{1,0:T(8,128)(2,1)}, bf16[48,1152]{1,0:T(8,128)(2,1)S(1)}, u32[]{:S(2)}, u32[]{:S(2)}) collective-permute-start(bf16[48,1152]{1,0:T(8,128)(2,1)} %get-tuple-element.283), channel_id=1, source_target_pairs={{0,16},{2,18},{4,20},{6,22},{8,24},{10,26},{12,28},{14,30},{16,0},... | collective-permute-start | bytes 331784 | tf_op jit(solution)/shard_map/ppermute | solution.py:46
  296.6 7.9 %collective-permute-start.42 = (bf16[48,1152]{1,0:T(8,128)(2,1)}, bf16[48,1152]{1,0:T(8,128)(2,1)S(1)}, u32[]{:S(2)}, u32[]{:S(2)}) collective-permute-start(bf16[48,1152]{1,0:T(8,128)(2,1)} %get-tuple-element.284), channel_id=1, source_target_pairs={{0,24},{2,26},{4,28},{6,30},{8,0},{10,2},{12,4},{14,6},{16,8},{18,... | collective-permute-start | bytes 331784 | tf_op jit(solution)/shard_map/ppermute | solution.py:46
  306.8 4.8 %collective-permute-start.46 = (f32[80,128]{1,0:T(8,128)S(1)}, f32[80,128]{1,0:T(8,128)S(1)}, u32[]{:S(2)}, u32[]{:S(2)}) collective-permute-start(f32[80,128]{1,0:T(8,128)S(1)} %add.61), channel_id=1, source_target_pairs={{0,8},{2,10},{4,12},{6,14},{8,0},{10,2},{12,4},{14,6},{16,24},{18,... | collective-permute-start | bytes 122888 | tf_op jit(solution)/shard_map/ppermute | solution.py:91
  311.6 4.9 %collective-permute-start.47 = (f32[80,128]{1,0:T(8,128)S(1)}, f32[80,128]{1,0:T(8,128)S(1)}, u32[]{:S(2)}, u32[]{:S(2)}) collective-permute-start(f32[80,128]{1,0:T(8,128)S(1)} %add.62), channel_id=1, source_target_pairs={{0,16},{2,18},{4,20},{6,22},{8,24},{10,26},{12,28},{14,30},{16,0},... | collective-permute-start | bytes 122888 | tf_op jit(solution)/shard_map/ppermute | solution.py:91
  (60 other events, 469.1 us)

commit v2 on v1

--- a/solution.py
+++ b/solution.py
@@ -133,14 +133,23 @@
 
     lax.fori_loop(0, total // BLOCK, clear, 0)
 
-    def start_of(cursor, count):
+    def choose(carry, parity):
+        cursor, short, long = carry
         inside = cursor & (BLOCK - 1)
-        return jnp.where(inside + count > BLOCK, cursor - inside + BLOCK, cursor)
-
-    def place(slot, cursor):
-        sentence = order_ref[2 * slot + core]
+        room = BLOCK - inside
+        fits = len_ref[order_ref[2 * long + parity]] <= room
+        takes = jnp.logical_and(
+            jnp.logical_not(fits), len_ref[order_ref[2 * short + parity]] <= room
+        )
+        slot = jnp.where(takes, short, long)
+        start = jnp.where(jnp.logical_or(fits, takes), cursor, cursor + room)
+        sentence = order_ref[2 * slot + parity]
         count = len_ref[sentence]
-        start = start_of(cursor, count)
+        left = (start + count, jnp.where(takes, short + 1, short), jnp.where(takes, long, long - 1))
+        return slot, sentence, count, start, left
+
+    def place(step, carry):
+        slot, sentence, count, start, carry = choose(carry, core)
         off_ref[0, slot] = start
         span = tok_ref.shape[1]
         value = tok_ref[sentence].astype(F32)
@@ -148,18 +157,17 @@
             column[pl.ds(start, span), :] = value[:, index * BLOCK : (index + 1) * BLOCK]
         row = lax.broadcasted_iota(jnp.int32, (span, BLOCK), 0)
         seg_ref[pl.ds(start, span), :] = jnp.where(row < count, slot.astype(F32), -1.0)
-        return start + count
-
-    used = lax.fori_loop(0, half, place, 0)
+        return carry
+
+    def partner(step, carry):
+        slot, _, _, start, carry = choose(carry, 1 - core)
+        off_ref[1, slot] = start
+        return carry
+
+    begin = (jnp.int32(0), jnp.int32(0), jnp.int32(half - 1))
+    used, _, _ = lax.fori_loop(0, half, place, begin)
     tiles_ref[0] = (used + TILE - 1) // TILE
-
-    def partner(slot, cursor):
-        count = len_ref[order_ref[2 * slot + 1 - core]]
-        start = start_of(cursor, count)
-        off_ref[1, slot] = start
-        return start + count
-
-    lax.fori_loop(0, half, partner, 0)
+    lax.fori_loop(0, half, partner, begin)
 
     def low(step, carry):
         rows = pl.ds(pl.multiple_of(step * BLOCK, BLOCK), BLOCK)

time: 328 us -> 328 us (level)
  no operation moved by 1% of the time
where the time goes in v2:
time: 328 us; the launch traced here: 327 us
  Pallas kernels  155 us (47%)
  starting transfers between devices  72.2 us (22%)
  waiting for transfers between devices  61.3 us (19%)
  local copies, waits for them, and re-layouts  20 us (6%)
  other arithmetic  16.7 us (5%)
    pallas_call x3, Pallas kernels, call(): pl.pallas_call(body, grid_spec=pltpu.PrefetchScalarGridSpec(num_scalar_pr...  110 us
    ppermute x36, starting transfers between devices, dp_shift(): return lax.ppermute(value, 'dp', pairs)  54 us
    ppermute x36, waiting for transfers between devices, dp_shift(): return lax.ppermute(value, 'dp', pairs)  45.5 us
    pallas_call x6, Pallas kernels, slab_sums(): pl.pallas_call(kernel, grid_spec=pltpu.PrefetchScalarGridSpec(num_scalar_...  24.6 us
    unnamed x113, local copies, waits for them, and re-layouts  13.3 us
    ppermute x4, waiting for transfers between devices, sum_all(): value = value + lax.ppermute(value, 'dp', pairs)  10.2 us
    select_n x8, other arithmetic, arrange(): jnp.where(place == 0, jnp.stack(pieces, axis), jnp.stack(pieces[::-1], ax...  10.1 us
    pallas_call x1, Pallas kernels, shards(): pl.pallas_call(pack_kernel, out_shape=(shape_of((most, width), BF), shape...  8.63 us
  transfers between devices with their start and end apart: 52, of which 21 were waited for; matrix products, arithmetic and copies ran while one was open for 5% of the time, Pallas kernels for 26%

profile of v2, /device:TPU:0, one launch (start us, length us, event | category | flops | bytes accessed | tf_op | source)
XLA Modules:
  0.0 327.3 jit_solution(5656414269538508457)
XLA Ops:
  2.6 3.1 collective-permute-start
  5.7 2.6 collective-permute-start.1
  10.8 3.9 %all-to-all-start = ((f32[16,4,768]{2,1,0:T(4,128)}), f32[16,4,768]{2,1,0:T(4,128)S(1)}, u32[]{:S(2)}, u32[]{:S(2)}) async-start(f32[16,4,768]{2,1,0:T(4,128)} %bitcast.113), calls=%async_computation | async-start | bytes 393216 | tf_op jit(solution)/shard_map/all_to_all | solution.py:812
  14.8 3.2 collective-permute-done.1
  18.4 1.6 collective-permute-start.3
  20.0 1.5 collective-permute-start.4
  21.5 7.9 %collective-permute-start.5 = (bf16[48,1536]{1,0:T(8,128)(2,1)S(1)}, bf16[48,1536]{1,0:T(8,128)(2,1)S(1)}, u32[]{:S(2)}, u32[]{:S(2)}) collective-permute-start(bf16[48,1536]{1,0:T(8,128)(2,1)S(1)} %convert_element_type.25), channel_id=1, source_target_pairs={{0,24},{2,26},{4,28},{6,30},{8,0},{10,2},{12,4},{14,6},{16,8},{18,... | collective-permute-start | bytes 442376 | tf_op jit(solution)/shard_map/ppermute | solution.py:46
  30.1 3.1 collective-permute-done.5
  33.2 8.2 %collective-permute-done.6 = bf16[48,1536]{1,0:T(8,128)(2,1)S(1)} collective-permute-done((bf16[48,1536]{1,0:T(8,128)(2,1)S(1)}, bf16[48,1536]{1,0:T(8,128)(2,1)S(1)}, u32[]{:S(2)}, u32[]{:S(2)}) %collective-permute-start.6) | collective-permute-done | bytes 147488 | tf_op jit(solution)/shard_map/ppermute | solution.py:46
  44.0 1.9 collective-permute-start.12
  47.1 8.6 %shard_map.463 = (bf16[2048,768]{1,0:T(8,128)(2,1)}, f32[2048,128]{1,0:T(8,128)}, s32[2,64]{1,0:T(2,128)}, s32[1]{0:T(128)}) custom-call(s32[1]{0:T(128)} %bitcast.3.core_ref.refs_0_, s32[128]{0:T(128)} %order_ref.1, s32[128]{0:T(128)} %len_ref.3, bf16[128,32,768]{2,1,0:T(8,128)(2,1)} %tok_ref.1), custom_call_target="tpu_custom_call" | custom-call | bytes 30000000 | tf_op jit(solution)/shard_map/pallas_call | solution.py:832
  63.6 1.6 collective-permute-start.14
  65.9 9.8 %collective-permute-done.13 = bf16[4,48,1536]{2,1,0:T(8,128)(2,1)S(1)} collective-permute-done((bf16[4,48,1536]{2,1,0:T(8,128)(2,1)S(1)}, bf16[4,48,1536]{2,1,0:T(8,128)(2,1)S(1)}, u32[]{:S(2)}, u32[]{:S(2)}) %collective-permute-start.13) | collective-permute-done | bytes 589856 | tf_op jit(solution)/shard_map/ppermute | solution.py:46
  75.9 1.6 collective-permute-start.16
  82.5 19.3 %shard_map.464 = (bf16[2048,2304]{1,0:T(8,128)(2,1)}, bf16[2048,768]{1,0:T(8,128)(2,1)}, f32[2048,768]{1,0:T(8,128)}, f32[2048,128]{1,0:T(8,128)}) custom-call(s32[1]{0:T(128)} %get-tuple-element.233.tiles_ref, s32[1]{0:T(128)} %bitcast.3.core_ref.refs_0_, bf16[2048,768]{1,0:T(8,128)(2,1)} %get-tuple-element.202.refs_1_.refs_2_, ...), custom_call_target="tpu_custom_call" | custom-call | flops 11596411904 | bytes 30000000 | tf_op jit(solution)/shard_map/pallas_call | solution.py:517
  103.4 2.2 collective-permute-done.17
  105.6 2.0 maximum_select_fusion
  107.9 3.5 %maximum_select_fusion.1 = bf16[4,2,2,48,1536]{4,3,0,2,1:T(8,128)(2,1)S(1)} fusion(bf16[4,1,2,48,1536]{4,3,0,2,1:T(8,128)(2,1)} %bitcast.40, bf16[4,1,2,48,1536]{4,3,0,2,1:T(8,128)(2,1)} %bitcast.39, pred[]{:T(512)S(6)} %eq.30), kind=kLoop, calls=%fused_computation.3 | loop fusion | flops 3538944 | bytes 4718593 | tf_op jit(solution)/shard_map/jit(_where)/select_n | solution.py:62
  113.0 3.2 collective-permute-done.19.refs_11_
  117.7 62.8 %shard_map.465 = (f32[2048,768]{1,0:T(8,128)}, f32[64,768]{1,0:T(8,128)}, f32[8,9216]{1,0:T(8,128)}, bf16[768,1408]{1,0:T(8,128)(2,1)}, bf16[768,1408]{1,0:T(8,1...) custom-call(s32[1]{0:T(128)} %get-tuple-element.233.tiles_ref, ...), custom_call_target="tpu_custom_call" | custom-call | flops 34789236736 | bytes 30000000 | tf_op jit(solution)/shard_map/pallas_call | solution.py:517
  181.2 1.7 reshape.168
  182.9 5.5 %all-to-all-start.1 = ((f32[16,4,768]{2,1,0:T(4,128)}), f32[16,4,768]{2,1,0:T(4,128)}, u32[]{:S(2)}, u32[]{:S(2)}) async-start(f32[16,4,768]{2,1,0:T(4,128)} %reshape.168), calls=%async_computation.1 | async-start | bytes 393216 | tf_op jit(solution)/shard_map/all_to_all | solution.py:953
  191.8 5.8 %shard_map.466 = (bf16[4,2,48,1408]{3,2,1,0:T(8,128)(2,1)}, bf16[4,2,48,1280]{3,2,1,0:T(8,128)(2,1)}, bf16[1,2,2,48,768]{4,3,2,1,0:T(8,128)(2,1)}, bf16[1,2,2,48...) custom-call(s32[3]{0:T(128)} %pad_add_fusion.places_ref, bf16[4,2,2,48,1408]{4,3,2,1,0:T(8,128)(2,1)} %bitcast.143, ...), custom_call_target="tpu_custom_call" | custom-call | bytes 8000000 | tf_op jit(solution)/shard_map/pallas_call | solution.py:641
  197.7 1.6 collective-permute-start.23
  200.5 1.5 collective-permute-start.25
  202.0 2.3 collective-permute-start.26
  204.3 1.5 collective-permute-start.27
  205.9 27.9 %shard_map.467 = (f32[2048,384]{1,0:T(8,128)}, bf16[2048,384]{1,0:T(8,128)(2,1)}, f32[72,128]{1,0:T(8,128)}, bf16[768,1152]{1,0:T(8,128)(2,1)}, bf16[768,1152]{1,0:T(8,128)(2,1)}) custom-call(s32[1]{0:T(128)} %get-tuple-element.233.tiles_ref, s32[1]{0:T(128)} %bitcast.3.core_ref.refs_0_, f32[2048,768]{1,0:T(8,128)} %get-tuple-element.234.refs_1_, ...), custom_call_target="tpu_custom_call" | custom-call | flops 26091925504 | bytes 30000000 | tf_op jit(solution)/shard_map/pallas_call | solution.py:517
  235.2 5.2 %shard_map.468 = (bf16[4,48,1408]{2,1,0:T(8,128)(2,1)}, bf16[4,48,1280]{2,1,0:T(8,128)(2,1)}, bf16[1,2,48,768]{3,2,1,0:T(8,128)(2,1)}) custom-call(s32[3]{0:T(128)} %pad_add_fusion.places_ref, bf16[4,2,2,48,1408]{4,3,2,1,0:T(8,128)(2,1)} %bitcast.144, bf16[4,2,2,48,1408]{4,3,2,1,0:T(8,128)(2,1)} %bitcast.43.refs_1_.refs_5_.refs_9_.refs_13_, ...), custom_call_target="tpu_custom_call" | custom-call | bytes 8000000 | tf_op jit(solution)/shard_map/pallas_call | solution.py:641
  240.5 1.5 collective-permute-start.30
  242.6 3.1 shard_map.470
  247.3 6.7 %shard_map.469 = f32[128,32,384]{2,1,0:T(8,128)} custom-call(s32[1]{0:T(128)} %bitcast.3.core_ref.refs_0_, s32[128]{0:T(128)} %order_ref.1, s32[128]{0:T(128)} %len_ref.3, s32[2,64]{1,0:T(2,128)} %get-tuple-element.258.off_ref, f32[2048,384]{1,0:T(8,128)} %get-tuple-element.259.mine_ref, bf16[2048,384]{1,0:T(8,128)(2,1)} %collective-permute-done.32.recv_ref), custom_call_target="tpu_custom_call" | custom-call | bytes 20000000 | tf_op jit(solution)/shard_map/pallas_call | solution.py:1004
  254.0 3.4 %collective-permute-done.31.refs_37_.refs_43_ = bf16[2,48,768]{2,1,0:T(8,128)(2,1)S(1)} collective-permute-done((bf16[2,48,768]{2,1,0:T(8,128)(2,1)}, bf16[2,48,768]{2,1,0:T(8,128)(2,1)S(1)}, u32[]{:S(2)}, u32[]{:S(2)}) %collective-permute-start.31) | collective-permute-done | bytes 147488 | tf_op jit(solution)/shard_map/ppermute | solution.py:46
  258.1 4.8 %shard_map.471 = (f32[1,48,768]{2,1,0:T(8,128)}, bf16[1,48,768]{2,1,0:T(8,128)(2,1)}, f32[48,2688]{1,0:T(8,128)}, bf16[48,2688]{1,0:T(8,128)(2,1)}, bf16[48,2688]{1,0:T(8,128)(2,1)}, /*index=5*/bf16[48,2688]{1,0:T(8,128)(2,1)}) custom-call(s32[3]{0:T(128)} %pad_add_fusion.places_ref, bf16[4,2,2,48,1408]{4,3,2,1,0:T(8,128)(2,1)} %bitcast.145, ...), custom_call_target="tpu_custom_call" | custom-call | bytes 8000000 | tf_op jit(solution)/shard_map/pallas_call | solution.py:641
  262.9 1.7 collective-permute-start.34
  266.3 2.9 collective-permute-start.39
  269.2 5.6 %collective-permute-done.33.refs_2_.refs_6_.refs_10_.refs_14_ = bf16[4,2,48,512]{3,2,1,0:T(8,128)(2,1)S(1)} collective-permute-done((bf16[4,2,48,512]{3,2,1,0:T(8,128)(2,1)}, bf16[4,2,48,512]{3,2,1,0:T(8,128)(2,1)S(1)}, u32[]{:S(2)}, u32[]{:S(2)}) %collective-permute-start.33) | collective-permute-done | bytes 393248 | tf_op jit(solution)/shard_map/ppermute | solution.py:46
  275.8 2.7 shard_map.472
  280.8 4.7 %collective-permute-done.38.refs_10_ = bf16[48,2688]{1,0:T(8,128)(2,1)S(1)} collective-permute-done((bf16[48,2688]{1,0:T(8,128)(2,1)}, bf16[48,2688]{1,0:T(8,128)(2,1)S(1)}, u32[]{:S(2)}, u32[]{:S(2)}) %collective-permute-start.38) | collective-permute-done | bytes 258080 | tf_op jit(solution)/shard_map/ppermute | solution.py:46
  287.8 2.9 shard_map.473
  291.4 4.3 %collective-permute-start.40 = (bf16[48,1152]{1,0:T(8,128)(2,1)}, bf16[48,1152]{1,0:T(8,128)(2,1)S(1)}, u32[]{:S(2)}, u32[]{:S(2)}) collective-permute-start(bf16[48,1152]{1,0:T(8,128)(2,1)} %get-tuple-element.282), channel_id=1, source_target_pairs={{0,8},{2,10},{4,12},{6,14},{8,16},{10,18},{12,20},{14,22},{16,24},... | collective-permute-start | bytes 331784 | tf_op jit(solution)/shard_map/ppermute | solution.py:46
  298.2 2.9 shard_map.474
  306.9 2.8 collective-permute-start.46
  309.7 2.0 collective-permute-done.46
  311.7 2.0 collective-permute-start.47
  313.7 2.9 collective-permute-done.47
  317.9 2.7 collective-permute-done.48
  322.1 2.6 collective-permute-done.49
  (234 shorter events, 58.5 us)
Async XLA Ops:
  2.6 12.2 %collective-permute-start = (bf16[48,1536]{1,0:T(8,128)(2,1)S(1)}, bf16[48,1536]{1,0:T(8,128)(2,1)S(1)}, u32[]{:S(2)}, u32[]{:S(2)}) collective-permute-start(bf16[48,1536]{1,0:T(8,128)(2,1)S(1)} %pad_maximum_fusion.5), channel_id=1, source_target_pairs={{0,8},{2,10},{4,12},{6,14},{8,16},{10,18},{12,20},{14,22},{16,24},... | collective-permute-start | bytes 442376 | tf_op jit(solution)/shard_map/ppermute | solution.py:46
  5.7 12.3 %collective-permute-start.1 = (bf16[48,1536]{1,0:T(8,128)(2,1)S(1)}, bf16[48,1536]{1,0:T(8,128)(2,1)S(1)}, u32[]{:S(2)}, u32[]{:S(2)}) collective-permute-start(bf16[48,1536]{1,0:T(8,128)(2,1)S(1)} %pad_maximum_fusion.5), channel_id=1, source_target_pairs={{0,16},{2,18},{4,20},{6,22},{8,24},{10,26},{12,28},{14,30},{16,0},... | collective-permute-start | bytes 442376 | tf_op jit(solution)/shard_map/ppermute | solution.py:46
  8.3 9.7 %collective-permute-start.2 = (bf16[48,1536]{1,0:T(8,128)(2,1)S(1)}, bf16[48,1536]{1,0:T(8,128)(2,1)S(1)}, u32[]{:S(2)}, u32[]{:S(2)}) collective-permute-start(bf16[48,1536]{1,0:T(8,128)(2,1)S(1)} %pad_maximum_fusion.5), channel_id=1, source_target_pairs={{0,24},{2,26},{4,28},{6,30},{8,0},{10,2},{12,4},{14,6},{16,8},{18,... | collective-permute-start | bytes 442376 | tf_op jit(solution)/shard_map/ppermute | solution.py:46
  10.8 19.3 %all-to-all-start = ((f32[16,4,768]{2,1,0:T(4,128)}), f32[16,4,768]{2,1,0:T(4,128)S(1)}, u32[]{:S(2)}, u32[]{:S(2)}) async-start(f32[16,4,768]{2,1,0:T(4,128)} %bitcast.113), calls=%async_computation | async-start | bytes 393216 | tf_op jit(solution)/shard_map/all_to_all | solution.py:812
  18.4 23.0 %collective-permute-start.3 = (bf16[4,48,768]{2,1,0:T(8,128)(2,1)S(1)}, bf16[4,48,768]{2,1,0:T(8,128)(2,1)S(1)}, u32[]{:S(2)}, u32[]{:S(2)}) collective-permute-start(bf16[4,48,768]{2,1,0:T(8,128)(2,1)S(1)} %get-tuple-element.181), channel_id=1, source_target_pairs={{0,4},{2,6},{4,0},{6,2},{8,12},{10,14},{12,8},{14,10},{16,20},{18,... | collective-permute-start | bytes 884744 | tf_op jit(solution)/shard_map/ppermute | solution.py:46
  20.0 21.4 %collective-permute-start.4 = (bf16[4,48,768]{2,1,0:T(8,128)(2,1)S(1)}, bf16[4,48,768]{2,1,0:T(8,128)(2,1)S(1)}, u32[]{:S(2)}, u32[]{:S(2)}) collective-permute-start(bf16[4,48,768]{2,1,0:T(8,128)(2,1)S(1)} %get-tuple-element.183), channel_id=1, source_target_pairs={{0,2},{2,0},{4,6},{6,4},{8,10},{10,8},{12,14},{14,12},{16,18},{18,... | collective-permute-start | bytes 884744 | tf_op jit(solution)/shard_map/ppermute | solution.py:46
  21.5 11.7 %collective-permute-start.5 = (bf16[48,1536]{1,0:T(8,128)(2,1)S(1)}, bf16[48,1536]{1,0:T(8,128)(2,1)S(1)}, u32[]{:S(2)}, u32[]{:S(2)}) collective-permute-start(bf16[48,1536]{1,0:T(8,128)(2,1)S(1)} %convert_element_type.25), channel_id=1, source_target_pairs={{0,24},{2,26},{4,28},{6,30},{8,0},{10,2},{12,4},{14,6},{16,8},{18,... | collective-permute-start | bytes 442376 | tf_op jit(solution)/shard_map/ppermute | solution.py:46
  29.4 12.0 %collective-permute-start.6 = (bf16[48,1536]{1,0:T(8,128)(2,1)S(1)}, bf16[48,1536]{1,0:T(8,128)(2,1)S(1)}, u32[]{:S(2)}, u32[]{:S(2)}) collective-permute-start(bf16[48,1536]{1,0:T(8,128)(2,1)S(1)} %convert_element_type.25), channel_id=1, source_target_pairs={{0,16},{2,18},{4,20},{6,22},{8,24},{10,26},{12,28},{14,30},{16,0},... | collective-permute-start | bytes 442376 | tf_op jit(solution)/shard_map/ppermute | solution.py:46
  29.4 12.0 %collective-permute-start.7 = (bf16[48,1536]{1,0:T(8,128)(2,1)S(1)}, bf16[48,1536]{1,0:T(8,128)(2,1)S(1)}, u32[]{:S(2)}, u32[]{:S(2)}) collective-permute-start(bf16[48,1536]{1,0:T(8,128)(2,1)S(1)} %convert_element_type.25), channel_id=1, source_target_pairs={{0,8},{2,10},{4,12},{6,14},{8,16},{10,18},{12,20},{14,22},{16,24},... | collective-permute-start | bytes 442376 | tf_op jit(solution)/shard_map/ppermute | solution.py:46
  41.6 14.8 %collective-permute-start.8 = (bf16[4,2,48,768]{3,2,0,1:T(8,128)(2,1)S(1)}, bf16[4,2,48,768]{3,2,0,1:T(8,128)(2,1)}, u32[]{:S(2)}, u32[]{:S(2)}) collective-permute-start(bf16[4,2,48,768]{3,2,0,1:T(8,128)(2,1)S(1)} %maximum_select_fusion.6), channel_id=1, source_target_pairs={{0,2},{2,0},{4,6},{6,4},{8,10},{10,8},{12,14},{14,12},{16,18},{18,... | collective-permute-start | bytes 1769480 | tf_op jit(solution)/shard_map/ppermute | solution.py:46
  42.3 14.1 %collective-permute-start.9 = (bf16[4,2,48,768]{3,2,0,1:T(8,128)(2,1)S(1)}, bf16[4,2,48,768]{3,2,0,1:T(8,128)(2,1)}, u32[]{:S(2)}, u32[]{:S(2)}) collective-permute-start(bf16[4,2,48,768]{3,2,0,1:T(8,128)(2,1)S(1)} %maximum_select_fusion.7), channel_id=1, source_target_pairs={{0,4},{2,6},{4,0},{6,2},{8,12},{10,14},{12,8},{14,10},{16,20},{18,... | collective-permute-start | bytes 1769480 | tf_op jit(solution)/shard_map/ppermute | solution.py:46
  43.1 12.6 %collective-permute-start.10 = (bf16[48,1536]{1,0:T(8,128)(2,1)S(1)}, bf16[48,1536]{1,0:T(8,128)(2,1)}, u32[]{:S(2)}, u32[]{:S(2)}) collective-permute-start(bf16[48,1536]{1,0:T(8,128)(2,1)S(1)} %bitcast_convert_fusion), channel_id=1, source_target_pairs={{0,24},{2,26},{4,28},{6,30},{8,0},{10,2},{12,4},{14,6},{16,8},{18,... | collective-permute-start | bytes 442376 | tf_op jit(solution)/shard_map/ppermute | solution.py:46
  43.2 13.2 %collective-permute-start.11 = (bf16[48,1536]{1,0:T(8,128)(2,1)S(1)}, bf16[48,1536]{1,0:T(8,128)(2,1)}, u32[]{:S(2)}, u32[]{:S(2)}) collective-permute-start(bf16[48,1536]{1,0:T(8,128)(2,1)S(1)} %bitcast_convert_fusion), channel_id=1, source_target_pairs={{0,16},{2,18},{4,20},{6,22},{8,24},{10,26},{12,28},{14,30},{16,0},... | collective-permute-start | bytes 442376 | tf_op jit(solution)/shard_map/ppermute | solution.py:46
  44.0 12.3 %collective-permute-start.12 = (bf16[48,1536]{1,0:T(8,128)(2,1)S(1)}, bf16[48,1536]{1,0:T(8,128)(2,1)}, u32[]{:S(2)}, u32[]{:S(2)}) collective-permute-start(bf16[48,1536]{1,0:T(8,128)(2,1)S(1)} %bitcast_convert_fusion), channel_id=1, source_target_pairs={{0,8},{2,10},{4,12},{6,14},{8,16},{10,18},{12,20},{14,22},{16,24},... | collective-permute-start | bytes 442376 | tf_op jit(solution)/shard_map/ppermute | solution.py:46
  59.7 21.5 %collective-permute-start.15 = (bf16[768,1536]{1,0:T(8,128)(2,1)S(1)}, bf16[768,1536]{1,0:T(8,128)(2,1)S(1)}, u32[]{:S(2)}, u32[]{:S(2)}) collective-permute-start(bf16[768,1536]{1,0:T(8,128)(2,1)S(1)} %pad_maximum_fusion.refs_4_.refs_5_.refs_6_.refs_7_), channel_id=1, source_target_pairs={{0,1},{1,0},{2,3},{3,2},{4,5},{5,4},{6,7},{7,6},{8,9},{9,8},{10,11... | collective-permute-start | bytes 7077896 | tf_op jit(solution)/shard_map/ppermute | solution.py:55
  61.1 14.6 %collective-permute-start.13 = (bf16[4,48,1536]{2,1,0:T(8,128)(2,1)S(1)}, bf16[4,48,1536]{2,1,0:T(8,128)(2,1)S(1)}, u32[]{:S(2)}, u32[]{:S(2)}) collective-permute-start(bf16[4,48,1536]{2,1,0:T(8,128)(2,1)S(1)} %get-tuple-element.337), channel_id=1, source_target_pairs={{0,4},{2,6},{4,0},{6,2},{8,12},{10,14},{12,8},{14,10},{16,20},{18,... | collective-permute-start | bytes 1769480 | tf_op jit(solution)/shard_map/ppermute | solution.py:46
  63.6 15.3 %collective-permute-start.14 = (bf16[4,48,1536]{2,1,0:T(8,128)(2,1)S(1)}, bf16[4,48,1536]{2,1,0:T(8,128)(2,1)S(1)}, u32[]{:S(2)}, u32[]{:S(2)}) collective-permute-start(bf16[4,48,1536]{2,1,0:T(8,128)(2,1)S(1)} %get-tuple-element.331), channel_id=1, source_target_pairs={{0,2},{2,0},{4,6},{6,4},{8,10},{10,8},{12,14},{14,12},{16,18},{18,... | collective-permute-start | bytes 1769480 | tf_op jit(solution)/shard_map/ppermute | solution.py:46
  75.9 27.4 %collective-permute-start.16 = (bf16[4,2,48,1536]{3,2,0,1:T(8,128)(2,1)S(1)}, bf16[4,2,48,1536]{3,2,0,1:T(8,128)(2,1)}, u32[]{:S(2)}, u32[]{:S(2)}) collective-permute-start(bf16[4,2,48,1536]{3,2,0,1:T(8,128)(2,1)S(1)} %maximum_select_fusion.2), channel_id=1, source_target_pairs={{0,2},{2,0},{4,6},{6,4},{8,10},{10,8},{12,14},{14,12},{16,18},{18,... | collective-permute-start | bytes 3538952 | tf_op jit(solution)/shard_map/ppermute | solution.py:46
  80.1 25.5 %collective-permute-start.17 = (bf16[4,2,48,1536]{3,2,0,1:T(8,128)(2,1)}, bf16[4,2,48,1536]{3,2,0,1:T(8,128)(2,1)}, u32[]{:S(2)}, u32[]{:S(2)}) collective-permute-start(bf16[4,2,48,1536]{3,2,0,1:T(8,128)(2,1)} %maximum_select_fusion.3), channel_id=1, source_target_pairs={{0,4},{2,6},{4,0},{6,2},{8,12},{10,14},{12,8},{14,10},{16,20},{18,... | collective-permute-start | bytes 3538952 | tf_op jit(solution)/shard_map/ppermute | solution.py:46
  107.8 4.6 %collective-permute-start.18 = (bf16[768,1536]{1,0:T(8,128)(2,1)S(1)}, bf16[768,1536]{1,0:T(8,128)(2,1)S(1)}, u32[]{:S(2)}, u32[]{:S(2)}) collective-permute-start(bf16[768,1536]{1,0:T(8,128)(2,1)S(1)} %bitcast.174), channel_id=1, source_target_pairs={{0,1},{1,0},{2,3},{3,2},{4,5},{5,4},{6,7},{7,6},{8,9},{9,8},{10,11... | collective-permute-start | bytes 7077896 | tf_op jit(solution)/shard_map/ppermute | solution.py:55
  180.5 10.1 %collective-permute-start.20 = (bf16[768,1408]{1,0:T(8,128)(2,1)}, bf16[768,1408]{1,0:T(8,128)(2,1)}, u32[]{:S(2)}, u32[]{:S(2)}) collective-permute-start(bf16[768,1408]{1,0:T(8,128)(2,1)} %get-tuple-element.217), channel_id=1, source_target_pairs={{0,1},{1,0},{2,3},{3,2},{4,5},{5,4},{6,7},{7,6},{8,9},{9,8},{10,11... | collective-permute-start | bytes 6488072 | tf_op jit(solution)/shard_map/ppermute | solution.py:55
  180.7 8.8 %collective-permute-start.21 = (bf16[768,1280]{1,0:T(8,128)(2,1)}, bf16[768,1280]{1,0:T(8,128)(2,1)S(1)}, u32[]{:S(2)}, u32[]{:S(2)}) collective-permute-start(bf16[768,1280]{1,0:T(8,128)(2,1)} %get-tuple-element.219), channel_id=1, source_target_pairs={{0,1},{1,0},{2,3},{3,2},{4,5},{5,4},{6,7},{7,6},{8,9},{9,8},{10,11... | collective-permute-start | bytes 5898248 | tf_op jit(solution)/shard_map/ppermute | solution.py:55
  181.0 8.5 %collective-permute-start.22 = (bf16[768,768]{1,0:T(8,128)(2,1)}, bf16[768,768]{1,0:T(8,128)(2,1)S(1)}, u32[]{:S(2)}, u32[]{:S(2)}) collective-permute-start(bf16[768,768]{1,0:T(8,128)(2,1)} %get-tuple-element.221), channel_id=1, source_target_pairs={{0,1},{1,0},{2,3},{3,2},{4,5},{5,4},{6,7},{7,6},{8,9},{9,8},{10,11... | collective-permute-start | bytes 3538952 | tf_op jit(solution)/shard_map/ppermute | solution.py:55
  182.9 14.8 %all-to-all-start.1 = ((f32[16,4,768]{2,1,0:T(4,128)}), f32[16,4,768]{2,1,0:T(4,128)}, u32[]{:S(2)}, u32[]{:S(2)}) async-start(f32[16,4,768]{2,1,0:T(4,128)} %reshape.168), calls=%async_computation.1 | async-start | bytes 393216 | tf_op jit(solution)/shard_map/all_to_all | solution.py:953
  197.7 36.2 %collective-permute-start.23 = (bf16[4,2,48,1408]{3,2,1,0:T(8,128)(2,1)}, bf16[4,2,48,1408]{3,2,1,0:T(8,128)(2,1)S(1)}, u32[]{:S(2)}, u32[]{:S(2)}) collective-permute-start(bf16[4,2,48,1408]{3,2,1,0:T(8,128)(2,1)} %get-tuple-element.228), channel_id=1, source_target_pairs={{0,2},{2,0},{4,6},{6,4},{8,10},{10,8},{12,14},{14,12},{16,18},{18,... | collective-permute-start | bytes 3244040 | tf_op jit(solution)/shard_map/ppermute | solution.py:46
  199.2 34.6 %collective-permute-start.24 = (bf16[4,2,48,1280]{3,2,1,0:T(8,128)(2,1)}, bf16[4,2,48,1280]{3,2,1,0:T(8,128)(2,1)}, u32[]{:S(2)}, u32[]{:S(2)}) collective-permute-start(bf16[4,2,48,1280]{3,2,1,0:T(8,128)(2,1)} %get-tuple-element.229), channel_id=1, source_target_pairs={{0,4},{2,6},{4,0},{6,2},{8,12},{10,14},{12,8},{14,10},{16,20},{18,... | collective-permute-start | bytes 2949128 | tf_op jit(solution)/shard_map/ppermute | solution.py:46
  200.5 33.3 %collective-permute-start.25 = (bf16[2,2,48,768]{3,2,1,0:T(8,128)(2,1)}, bf16[2,2,48,768]{3,2,1,0:T(8,128)(2,1)S(1)}, u32[]{:S(2)}, u32[]{:S(2)}) collective-permute-start(bf16[2,2,48,768]{3,2,1,0:T(8,128)(2,1)} %bitcast.191), channel_id=1, source_target_pairs={{0,8},{2,10},{4,12},{6,14},{8,16},{10,18},{12,20},{14,22},{16,24},... | collective-permute-start | bytes 884744 | tf_op jit(solution)/shard_map/ppermute | solution.py:46
  202.0 31.8 %collective-permute-start.26 = (bf16[2,2,48,768]{3,2,1,0:T(8,128)(2,1)}, bf16[2,2,48,768]{3,2,1,0:T(8,128)(2,1)S(1)}, u32[]{:S(2)}, u32[]{:S(2)}) collective-permute-start(bf16[2,2,48,768]{3,2,1,0:T(8,128)(2,1)} %bitcast.190), channel_id=1, source_target_pairs={{0,16},{2,18},{4,20},{6,22},{8,24},{10,26},{12,28},{14,30},{16,0},... | collective-permute-start | bytes 884744 | tf_op jit(solution)/shard_map/ppermute | solution.py:46
  204.3 29.5 %collective-permute-start.27 = (bf16[2,2,48,768]{3,2,1,0:T(8,128)(2,1)}, bf16[2,2,48,768]{3,2,1,0:T(8,128)(2,1)S(1)}, u32[]{:S(2)}, u32[]{:S(2)}) collective-permute-start(bf16[2,2,48,768]{3,2,1,0:T(8,128)(2,1)} %bitcast.189), channel_id=1, source_target_pairs={{0,24},{2,26},{4,28},{6,30},{8,0},{10,2},{12,4},{14,6},{16,8},{18,... | collective-permute-start | bytes 884744 | tf_op jit(solution)/shard_map/ppermute | solution.py:46
  234.6 5.8 %collective-permute-start.28 = (bf16[768,1152]{1,0:T(8,128)(2,1)}, bf16[768,1152]{1,0:T(8,128)(2,1)}, u32[]{:S(2)}, u32[]{:S(2)}) collective-permute-start(bf16[768,1152]{1,0:T(8,128)(2,1)} %get-tuple-element.241), channel_id=1, source_target_pairs={{0,1},{1,0},{2,3},{3,2},{4,5},{5,4},{6,7},{7,6},{8,9},{9,8},{10,11... | collective-permute-start | bytes 5308424 | tf_op jit(solution)/shard_map/ppermute | solution.py:55
  235.0 12.3 %collective-permute-start.32 = (bf16[2048,384]{1,0:T(8,128)(2,1)}, bf16[2048,384]{1,0:T(8,128)(2,1)}, u32[]{:S(2)}, u32[]{:S(2)}) collective-permute-start(bf16[2048,384]{1,0:T(8,128)(2,1)} %get-tuple-element.260), channel_id=1, source_target_pairs={{0,1},{1,0},{2,3},{3,2},{4,5},{5,4},{6,7},{7,6},{8,9},{9,8},{10,11... | collective-permute-start | bytes 4718600 | tf_op jit(solution)/shard_map/ppermute | solution.py:55
  240.4 17.0 %collective-permute-start.29 = (bf16[4,48,1408]{2,1,0:T(8,128)(2,1)}, bf16[4,48,1408]{2,1,0:T(8,128)(2,1)}, u32[]{:S(2)}, u32[]{:S(2)}) collective-permute-start(bf16[4,48,1408]{2,1,0:T(8,128)(2,1)} %get-tuple-element.254), channel_id=1, source_target_pairs={{0,4},{2,6},{4,0},{6,2},{8,12},{10,14},{12,8},{14,10},{16,20},{18,... | collective-permute-start | bytes 1622024 | tf_op jit(solution)/shard_map/ppermute | solution.py:46
  240.5 16.9 %collective-permute-start.30 = (bf16[4,48,1280]{2,1,0:T(8,128)(2,1)}, bf16[4,48,1280]{2,1,0:T(8,128)(2,1)}, u32[]{:S(2)}, u32[]{:S(2)}) collective-permute-start(bf16[4,48,1280]{2,1,0:T(8,128)(2,1)} %get-tuple-element.255), channel_id=1, source_target_pairs={{0,2},{2,0},{4,6},{6,4},{8,10},{10,8},{12,14},{14,12},{16,18},{18,... | collective-permute-start | bytes 1474568 | tf_op jit(solution)/shard_map/ppermute | solution.py:46
  242.1 15.4 %collective-permute-start.31 = (bf16[2,48,768]{2,1,0:T(8,128)(2,1)}, bf16[2,48,768]{2,1,0:T(8,128)(2,1)S(1)}, u32[]{:S(2)}, u32[]{:S(2)}) collective-permute-start(bf16[2,48,768]{2,1,0:T(8,128)(2,1)} %bitcast.192), channel_id=1, source_target_pairs={{0,2},{2,0},{4,6},{6,4},{8,10},{10,8},{12,14},{14,12},{16,18},{18,... | collective-permute-start | bytes 442376 | tf_op jit(solution)/shard_map/ppermute | solution.py:46
  262.9 13.0 %collective-permute-start.34 = (bf16[4,2,48,640]{3,2,1,0:T(8,128)(2,1)}, bf16[4,2,48,640]{3,2,1,0:T(8,128)(2,1)S(1)}, u32[]{:S(2)}, u32[]{:S(2)}) collective-permute-start(bf16[4,2,48,640]{3,2,1,0:T(8,128)(2,1)} %copy-done.36), channel_id=1, source_target_pairs={{0,4},{2,6},{4,0},{6,2},{8,12},{10,14},{12,8},{14,10},{16,20},{18,... | collective-permute-start | bytes 1474568 | tf_op jit(solution)/shard_map/ppermute | solution.py:46
  264.6 10.2 %collective-permute-start.33 = (bf16[4,2,48,512]{3,2,1,0:T(8,128)(2,1)}, bf16[4,2,48,512]{3,2,1,0:T(8,128)(2,1)S(1)}, u32[]{:S(2)}, u32[]{:S(2)}) collective-permute-start(bf16[4,2,48,512]{3,2,1,0:T(8,128)(2,1)} %copy-done.37), channel_id=1, source_target_pairs={{0,2},{2,0},{4,6},{6,4},{8,10},{10,8},{12,14},{14,12},{16,18},{18,... | collective-permute-start | bytes 1179656 | tf_op jit(solution)/shard_map/ppermute | solution.py:46
  265.4 15.4 %collective-permute-start.37 = (bf16[48,2688]{1,0:T(8,128)(2,1)}, bf16[48,2688]{1,0:T(8,128)(2,1)S(1)}, u32[]{:S(2)}, u32[]{:S(2)}) collective-permute-start(bf16[48,2688]{1,0:T(8,128)(2,1)} %get-tuple-element.275), channel_id=1, source_target_pairs={{0,8},{2,10},{4,12},{6,14},{8,16},{10,18},{12,20},{14,22},{16,24},... | collective-permute-start | bytes 774152 | tf_op jit(solution)/shard_map/ppermute | solution.py:46
  265.7 19.8 %collective-permute-start.38 = (bf16[48,2688]{1,0:T(8,128)(2,1)}, bf16[48,2688]{1,0:T(8,128)(2,1)S(1)}, u32[]{:S(2)}, u32[]{:S(2)}) collective-permute-start(bf16[48,2688]{1,0:T(8,128)(2,1)} %get-tuple-element.276), channel_id=1, source_target_pairs={{0,16},{2,18},{4,20},{6,22},{8,24},{10,26},{12,28},{14,30},{16,0},... | collective-permute-start | bytes 774152 | tf_op jit(solution)/shard_map/ppermute | solution.py:46
  266.3 19.9 %collective-permute-start.39 = (bf16[48,2688]{1,0:T(8,128)(2,1)}, bf16[48,2688]{1,0:T(8,128)(2,1)S(1)}, u32[]{:S(2)}, u32[]{:S(2)}) collective-permute-start(bf16[48,2688]{1,0:T(8,128)(2,1)} %get-tuple-element.277), channel_id=1, source_target_pairs={{0,24},{2,26},{4,28},{6,30},{8,0},{10,2},{12,4},{14,6},{16,8},{18,... | collective-permute-start | bytes 774152 | tf_op jit(solution)/shard_map/ppermute | solution.py:46
  278.6 8.3 %collective-permute-start.36 = (bf16[4,48,640]{2,1,0:T(8,128)(2,1)S(1)}, bf16[4,48,640]{2,1,0:T(8,128)(2,1)S(1)}, u32[]{:S(2)}, u32[]{:S(2)}) collective-permute-start(bf16[4,48,640]{2,1,0:T(8,128)(2,1)S(1)} %get-tuple-element.274), channel_id=1, source_target_pairs={{0,2},{2,0},{4,6},{6,4},{8,10},{10,8},{12,14},{14,12},{16,18},{18,... | collective-permute-start | bytes 737288 | tf_op jit(solution)/shard_map/ppermute | solution.py:46
  279.5 7.3 %collective-permute-start.35 = (bf16[4,48,512]{2,1,0:T(8,128)(2,1)S(1)}, bf16[4,48,512]{2,1,0:T(8,128)(2,1)S(1)}, u32[]{:S(2)}, u32[]{:S(2)}) collective-permute-start(bf16[4,48,512]{2,1,0:T(8,128)(2,1)S(1)} %get-tuple-element.273), channel_id=1, source_target_pairs={{0,4},{2,6},{4,0},{6,2},{8,12},{10,14},{12,8},{14,10},{16,20},{18,... | collective-permute-start | bytes 589832 | tf_op jit(solution)/shard_map/ppermute | solution.py:46
  286.9 14.3 %collective-permute-start.43 = (f32[16,4,768]{2,1,0:T(4,128)}, f32[16,4,768]{2,1,0:T(4,128)}, u32[]{:S(2)}, u32[]{:S(2)}) collective-permute-start(f32[16,4,768]{2,1,0:T(4,128)} %all-to-all-done.1), channel_id=1, source_target_pairs={{0,1},{1,0},{2,3},{3,2},{4,5},{5,4},{6,7},{7,6},{8,9},{9,8},{10,11... | collective-permute-start | bytes 589832 | tf_op jit(solution)/shard_map/ppermute | solution.py:55
  286.9 11.2 %collective-permute-start.44 = (bf16[48,768]{1,0:T(8,128)(2,1)}, bf16[48,768]{1,0:T(8,128)(2,1)}, u32[]{:S(2)}, u32[]{:S(2)}) collective-permute-start(bf16[48,768]{1,0:T(8,128)(2,1)} %bitcast.54), channel_id=1, source_target_pairs={{0,4},{2,6},{4,0},{6,2},{8,12},{10,14},{12,8},{14,10},{16,20},{18,... | collective-permute-start | bytes 221192 | tf_op jit(solution)/shard_map/ppermute | solution.py:46
  291.4 12.4 %collective-permute-start.40 = (bf16[48,1152]{1,0:T(8,128)(2,1)}, bf16[48,1152]{1,0:T(8,128)(2,1)S(1)}, u32[]{:S(2)}, u32[]{:S(2)}) collective-permute-start(bf16[48,1152]{1,0:T(8,128)(2,1)} %get-tuple-element.282), channel_id=1, source_target_pairs={{0,8},{2,10},{4,12},{6,14},{8,16},{10,18},{12,20},{14,22},{16,24},... | collective-permute-start | bytes 331784 | tf_op jit(solution)/shard_map/ppermute | solution.py:46
  295.7 8.8 %collective-permute-start.41 = (bf16[48,1152]{1,0:T(8,128)(2,1)}, bf16[48,1152]{1,0:T(8,128)(2,1)S(1)}, u32[]{:S(2)}, u32[]{:S(2)}) collective-permute-start(bf16[48,1152]{1,0:T(8,128)(2,1)} %get-tuple-element.283), channel_id=1, source_target_pairs={{0,16},{2,18},{4,20},{6,22},{8,24},{10,26},{12,28},{14,30},{16,0},... | collective-permute-start | bytes 331784 | tf_op jit(solution)/shard_map/ppermute | solution.py:46
  296.7 7.9 %collective-permute-start.42 = (bf16[48,1152]{1,0:T(8,128)(2,1)}, bf16[48,1152]{1,0:T(8,128)(2,1)S(1)}, u32[]{:S(2)}, u32[]{:S(2)}) collective-permute-start(bf16[48,1152]{1,0:T(8,128)(2,1)} %get-tuple-element.284), channel_id=1, source_target_pairs={{0,24},{2,26},{4,28},{6,30},{8,0},{10,2},{12,4},{14,6},{16,8},{18,... | collective-permute-start | bytes 331784 | tf_op jit(solution)/shard_map/ppermute | solution.py:46
  306.9 4.8 %collective-permute-start.46 = (f32[80,128]{1,0:T(8,128)S(1)}, f32[80,128]{1,0:T(8,128)S(1)}, u32[]{:S(2)}, u32[]{:S(2)}) collective-permute-start(f32[80,128]{1,0:T(8,128)S(1)} %add.61), channel_id=1, source_target_pairs={{0,8},{2,10},{4,12},{6,14},{8,0},{10,2},{12,4},{14,6},{16,24},{18,... | collective-permute-start | bytes 122888 | tf_op jit(solution)/shard_map/ppermute | solution.py:91
  311.7 4.9 %collective-permute-start.47 = (f32[80,128]{1,0:T(8,128)S(1)}, f32[80,128]{1,0:T(8,128)S(1)}, u32[]{:S(2)}, u32[]{:S(2)}) collective-permute-start(f32[80,128]{1,0:T(8,128)S(1)} %add.62), channel_id=1, source_target_pairs={{0,16},{2,18},{4,20},{6,22},{8,24},{10,26},{12,28},{14,30},{16,0},... | collective-permute-start | bytes 122888 | tf_op jit(solution)/shard_map/ppermute | solution.py:91
  (60 other events, 476.4 us)

commit v3 on v2

--- a/solution.py
+++ b/solution.py
@@ -776,7 +776,6 @@
         return jnp.where(core == 0, value, value[::-1])
 
     chunk = jnp.concatenate([qkv_weight[0], qkv_weight[1], qkv_weight[2], out_weight.T], axis=1)
-    down_t = down_weight.T.astype(BF)
     first, others = dims[0], dims[1:]
     orders = (others, others[::-1])
     sides = (0, 1)
@@ -819,14 +818,14 @@
     pieces0 = gather_send(chunk.astype(BF), first)
     qkvo = gather_start(pieces0)
     pieces0 = gather_out(qkvo)
-    own, held = lax.optimization_barrier((in_weight.astype(BF), [pieces[0] for pieces in pieces0]))
-    pieces1 = gather_send(own, first)
+    own, held = lax.optimization_barrier((in_weight, [pieces[0] for pieces in pieces0]))
+    pieces1 = gather_send(own.astype(BF), first)
     pieces0, pieces1, pair_grad = lax.optimization_barrier((pieces0, pieces1, pair_grad))
     qkvo = gather_in(qkvo, pieces0)
     pieces0 = gather_out(qkvo)
     held = [pieces[0] for pieces in pieces0]
-    own, held = lax.optimization_barrier((down_t, held))
-    pieces2 = gather_send(own, first)
+    own, held = lax.optimization_barrier((down_weight, held))
+    pieces2 = gather_send(own.T.astype(BF), first)
 
     order_word, _ = lax.optimization_barrier((send_order, [pieces[0] for pieces in pieces0]))
     packed = pl.pallas_call(
@@ -1030,14 +1029,8 @@
     (qkv_grad, *slabs), _ = slab_sums(qkv_send, dims, joined=True)
     go = scatter_send(slabs, first)
 
-    both = flip(jnp.stack([pooled, swap_core(pooled)]))
-    if share % 2 == 0:
-        pooled = jnp.moveaxis(both, 0, 2).reshape(sents, width)
-    else:
-        both = jnp.moveaxis(both, 0, 1).reshape(sents, width)
-        pooled = go_pooled(both)
-
-    go, pooled = lax.optimization_barrier((go, pooled))
+    both = [pooled, swap_core(pooled)]
+    go, both = lax.optimization_barrier((go, both))
     ffn_states = [
         (out_weight.T, out_moment.T, out_square.T),
         (in_weight, in_moment, in_square),
@@ -1063,6 +1056,14 @@
         compiler_params=params(SMALL_LIMIT),
         cost_estimate=cost(0, 4e6),
     )(qkv_grad, qkv_weight, qkv_moment, qkv_square, vec_local, norms, *go)
+    totals, both = lax.optimization_barrier((totals, both))
+    both = flip(jnp.stack(both))
+    if share % 2 == 0:
+        pooled = jnp.moveaxis(both, 0, 2).reshape(sents, width)
+    else:
+        both = jnp.moveaxis(both, 0, 1).reshape(sents, width)
+        pooled = go_pooled(both)
+
     totals = sum_all(totals, dims)
     states = [
         (qkv_u, qkv_weight, qkv_average),

time: 328 us -> 325 us (level)
    unnamed x113 -> x99, local copies, waits for them, and re-layouts: 13.3 us -> 11.2 us
  transfers between devices with their start and end apart: 52 -> 52, of which waited for: 21 -> 22; matrix products, arithmetic and copies ran while one was open for 5% -> 5% of each run, Pallas kernels for 26% -> 26%
where the time goes in v3:
time: 325 us; the launch traced here: 324 us
  Pallas kernels  154 us (47%)
  starting transfers between devices  72.9 us (22%)
  waiting for transfers between devices  61.3 us (19%)
  local copies, waits for them, and re-layouts  18 us (6%)
  other arithmetic  16.6 us (5%)
    pallas_call x3, Pallas kernels, call(): pl.pallas_call(body, grid_spec=pltpu.PrefetchScalarGridSpec(num_scalar_pr...  110 us
    ppermute x36, starting transfers between devices, dp_shift(): return lax.ppermute(value, 'dp', pairs)  54.6 us
    ppermute x36, waiting for transfers between devices, dp_shift(): return lax.ppermute(value, 'dp', pairs)  48.6 us
    pallas_call x6, Pallas kernels, slab_sums(): pl.pallas_call(kernel, grid_spec=pltpu.PrefetchScalarGridSpec(num_scalar_...  23.8 us
    unnamed x99, local copies, waits for them, and re-layouts  11.2 us
    select_n x8, other arithmetic, arrange(): jnp.where(place == 0, jnp.stack(pieces, axis), jnp.stack(pieces[::-1], ax...  10.1 us
    pallas_call x1, Pallas kernels, shards(): pl.pallas_call(pack_kernel, out_shape=(shape_of((most, width), BF), shape...  8.62 us
    ppermute x4, starting transfers between devices, sum_all(): value = value + lax.ppermute(value, 'dp', pairs)  7.51 us
  transfers between devices with their start and end apart: 52, of which 22 were waited for; matrix products, arithmetic and copies ran while one was open for 5% of the time, Pallas kernels for 26%

profile of v3, /device:TPU:0, one launch (start us, length us, event | category | flops | bytes accessed | tf_op | source)
XLA Modules:
  0.0 324.1 jit_solution(5017649496510317545)
XLA Ops:
  2.6 3.1 collective-permute-start
  5.7 2.6 collective-permute-start.1
  10.8 3.9 %all-to-all-start = ((f32[16,4,768]{2,1,0:T(4,128)}), f32[16,4,768]{2,1,0:T(4,128)S(1)}, u32[]{:S(2)}, u32[]{:S(2)}) async-start(f32[16,4,768]{2,1,0:T(4,128)} %bitcast.114), calls=%async_computation | async-start | bytes 393216 | tf_op jit(solution)/shard_map/all_to_all | solution.py:811
  14.8 3.2 collective-permute-done.1
  18.4 1.6 collective-permute-start.3
  21.5 7.9 %collective-permute-start.5 = (bf16[48,1536]{1,0:T(8,128)(2,1)S(1)}, bf16[48,1536]{1,0:T(8,128)(2,1)S(1)}, u32[]{:S(2)}, u32[]{:S(2)}) collective-permute-start(bf16[48,1536]{1,0:T(8,128)(2,1)S(1)} %convert_element_type.28), channel_id=1, source_target_pairs={{0,24},{2,26},{4,28},{6,30},{8,0},{10,2},{12,4},{14,6},{16,8},{18,... | collective-permute-start | bytes 442376 | tf_op jit(solution)/shard_map/ppermute | solution.py:46
  30.1 3.1 collective-permute-done.5
  33.2 8.2 %collective-permute-done.6 = bf16[48,1536]{1,0:T(8,128)(2,1)S(1)} collective-permute-done((bf16[48,1536]{1,0:T(8,128)(2,1)S(1)}, bf16[48,1536]{1,0:T(8,128)(2,1)S(1)}, u32[]{:S(2)}, u32[]{:S(2)}) %collective-permute-start.6) | collective-permute-done | bytes 147488 | tf_op jit(solution)/shard_map/ppermute | solution.py:46
  44.0 1.9 collective-permute-start.12
  47.1 8.6 %shard_map.463 = (bf16[2048,768]{1,0:T(8,128)(2,1)}, f32[2048,128]{1,0:T(8,128)}, s32[2,64]{1,0:T(2,128)}, s32[1]{0:T(128)}) custom-call(s32[1]{0:T(128)} %bitcast.3.core_ref.refs_0_, s32[128]{0:T(128)} %order_ref.1, s32[128]{0:T(128)} %len_ref.3, bf16[128,32,768]{2,1,0:T(8,128)(2,1)} %tok_ref.1), custom_call_target="tpu_custom_call" | custom-call | bytes 30000000 | tf_op jit(solution)/shard_map/pallas_call | solution.py:831
  63.6 1.6 collective-permute-start.14
  66.0 9.8 %collective-permute-done.13 = bf16[4,48,1536]{2,1,0:T(8,128)(2,1)S(1)} collective-permute-done((bf16[4,48,1536]{2,1,0:T(8,128)(2,1)S(1)}, bf16[4,48,1536]{2,1,0:T(8,128)(2,1)S(1)}, u32[]{:S(2)}, u32[]{:S(2)}) %collective-permute-start.13) | collective-permute-done | bytes 589856 | tf_op jit(solution)/shard_map/ppermute | solution.py:46
  75.9 1.6 collective-permute-start.16
  82.5 19.4 %shard_map.464 = (bf16[2048,2304]{1,0:T(8,128)(2,1)}, bf16[2048,768]{1,0:T(8,128)(2,1)}, f32[2048,768]{1,0:T(8,128)}, f32[2048,128]{1,0:T(8,128)}) custom-call(s32[1]{0:T(128)} %get-tuple-element.237.tiles_ref, s32[1]{0:T(128)} %bitcast.3.core_ref.refs_0_, bf16[2048,768]{1,0:T(8,128)(2,1)} %get-tuple-element.206.refs_1_.refs_2_, ...), custom_call_target="tpu_custom_call" | custom-call | flops 11596411904 | bytes 30000000 | tf_op jit(solution)/shard_map/pallas_call | solution.py:517
  103.4 2.2 collective-permute-done.17
  105.5 2.1 maximum_select_fusion
  107.9 3.5 %maximum_select_fusion.1 = bf16[4,2,2,48,1536]{4,3,0,2,1:T(8,128)(2,1)S(1)} fusion(bf16[4,1,2,48,1536]{4,3,0,2,1:T(8,128)(2,1)} %bitcast.40, bf16[4,1,2,48,1536]{4,3,0,2,1:T(8,128)(2,1)} %bitcast.39, pred[]{:T(512)S(6)} %eq.31), kind=kLoop, calls=%fused_computation.3 | loop fusion | flops 3538944 | bytes 4718593 | tf_op jit(solution)/shard_map/jit(_where)/select_n | solution.py:62
  113.0 3.2 collective-permute-done.19.refs_11_
  117.7 62.8 %shard_map.465 = (f32[2048,768]{1,0:T(8,128)}, f32[64,768]{1,0:T(8,128)}, f32[8,9216]{1,0:T(8,128)}, bf16[768,1408]{1,0:T(8,128)(2,1)}, bf16[768,1408]{1,0:T(8,1...) custom-call(s32[1]{0:T(128)} %get-tuple-element.237.tiles_ref, ...), custom_call_target="tpu_custom_call" | custom-call | flops 34789236736 | bytes 30000000 | tf_op jit(solution)/shard_map/pallas_call | solution.py:517
  181.3 1.7 reshape.168
  182.9 5.5 %all-to-all-start.1 = ((f32[16,4,768]{2,1,0:T(4,128)}), f32[16,4,768]{2,1,0:T(4,128)}, u32[]{:S(2)}, u32[]{:S(2)}) async-start(f32[16,4,768]{2,1,0:T(4,128)} %reshape.168), calls=%async_computation.1 | async-start | bytes 393216 | tf_op jit(solution)/shard_map/all_to_all | solution.py:952
  191.8 5.8 %shard_map.466 = (bf16[4,2,48,1408]{3,2,1,0:T(8,128)(2,1)}, bf16[4,2,48,1280]{3,2,1,0:T(8,128)(2,1)}, bf16[1,2,2,48,768]{4,3,2,1,0:T(8,128)(2,1)}, bf16[1,2,2,48...) custom-call(s32[3]{0:T(128)} %pad_add_fusion.places_ref, bf16[4,2,2,48,1408]{4,3,2,1,0:T(8,128)(2,1)} %bitcast.144, ...), custom_call_target="tpu_custom_call" | custom-call | bytes 8000000 | tf_op jit(solution)/shard_map/pallas_call | solution.py:641
  197.7 1.5 collective-permute-start.23
  202.1 2.3 collective-permute-start.26
  204.4 1.5 collective-permute-start.27
  205.9 27.9 %shard_map.467 = (f32[2048,384]{1,0:T(8,128)}, bf16[2048,384]{1,0:T(8,128)(2,1)}, f32[72,128]{1,0:T(8,128)}, bf16[768,1152]{1,0:T(8,128)(2,1)}, bf16[768,1152]{1,0:T(8,128)(2,1)}) custom-call(s32[1]{0:T(128)} %get-tuple-element.237.tiles_ref, s32[1]{0:T(128)} %bitcast.3.core_ref.refs_0_, f32[2048,768]{1,0:T(8,128)} %get-tuple-element.238.refs_1_, ...), custom_call_target="tpu_custom_call" | custom-call | flops 26091925504 | bytes 30000000 | tf_op jit(solution)/shard_map/pallas_call | solution.py:517
  235.3 5.2 %shard_map.468 = (bf16[4,48,1408]{2,1,0:T(8,128)(2,1)}, bf16[4,48,1280]{2,1,0:T(8,128)(2,1)}, bf16[1,2,48,768]{3,2,1,0:T(8,128)(2,1)}) custom-call(s32[3]{0:T(128)} %pad_add_fusion.places_ref, bf16[4,2,2,48,1408]{4,3,2,1,0:T(8,128)(2,1)} %bitcast.145, bf16[4,2,2,48,1408]{4,3,2,1,0:T(8,128)(2,1)} %bitcast.43.refs_1_.refs_5_.refs_9_.refs_13_, ...), custom_call_target="tpu_custom_call" | custom-call | bytes 8000000 | tf_op jit(solution)/shard_map/pallas_call | solution.py:641
  240.5 1.5 collective-permute-start.29
  242.1 2.0 collective-permute-start.31
  244.1 3.1 shard_map.470
  248.8 6.7 %shard_map.469 = f32[128,32,384]{2,1,0:T(8,128)} custom-call(s32[1]{0:T(128)} %bitcast.3.core_ref.refs_0_, s32[128]{0:T(128)} %order_ref.1, s32[128]{0:T(128)} %len_ref.3, s32[2,64]{1,0:T(2,128)} %get-tuple-element.262.off_ref, f32[2048,384]{1,0:T(8,128)} %get-tuple-element.263.mine_ref, bf16[2048,384]{1,0:T(8,128)(2,1)} %collective-permute-done.32.recv_ref), custom_call_target="tpu_custom_call" | custom-call | bytes 20000000 | tf_op jit(solution)/shard_map/pallas_call | solution.py:1003
  255.5 3.2 collective-permute-done.31.refs_37_.refs_43_
  259.3 4.8 %shard_map.471 = (f32[1,48,768]{2,1,0:T(8,128)}, bf16[1,48,768]{2,1,0:T(8,128)(2,1)}, f32[48,2688]{1,0:T(8,128)}, bf16[48,2688]{1,0:T(8,128)(2,1)}, bf16[48,2688]{1,0:T(8,128)(2,1)}, /*index=5*/bf16[48,2688]{1,0:T(8,128)(2,1)}) custom-call(s32[3]{0:T(128)} %pad_add_fusion.places_ref, bf16[4,2,2,48,1408]{4,3,2,1,0:T(8,128)(2,1)} %bitcast.146, ...), custom_call_target="tpu_custom_call" | custom-call | bytes 8000000 | tf_op jit(solution)/shard_map/pallas_call | solution.py:641
  266.4 2.9 collective-permute-start.39
  269.3 5.6 %collective-permute-done.33.refs_2_.refs_6_.refs_10_.refs_14_ = bf16[4,2,48,512]{3,2,1,0:T(8,128)(2,1)S(1)} collective-permute-done((bf16[4,2,48,512]{3,2,1,0:T(8,128)(2,1)}, bf16[4,2,48,512]{3,2,1,0:T(8,128)(2,1)S(1)}, u32[]{:S(2)}, u32[]{:S(2)}) %collective-permute-start.33) | collective-permute-done | bytes 393248 | tf_op jit(solution)/shard_map/ppermute | solution.py:46
  274.9 1.8 collective-permute-done.34.refs_5_.refs_18_.refs_22_.refs_26_.refs_30_
  276.7 2.7 shard_map.472
  280.8 4.7 %collective-permute-done.38.refs_10_ = bf16[48,2688]{1,0:T(8,128)(2,1)S(1)} collective-permute-done((bf16[48,2688]{1,0:T(8,128)(2,1)}, bf16[48,2688]{1,0:T(8,128)(2,1)S(1)}, u32[]{:S(2)}, u32[]{:S(2)}) %collective-permute-start.38) | collective-permute-done | bytes 258080 | tf_op jit(solution)/shard_map/ppermute | solution.py:46
  286.0 2.1 shard_map.473
  288.1 4.9 %collective-permute-start.41 = (bf16[48,1152]{1,0:T(8,128)(2,1)S(1)}, bf16[48,1152]{1,0:T(8,128)(2,1)S(1)}, u32[]{:S(2)}, u32[]{:S(2)}) collective-permute-start(bf16[48,1152]{1,0:T(8,128)(2,1)S(1)} %get-tuple-element.295), channel_id=1, source_target_pairs={{0,8},{2,10},{4,12},{6,14},{8,16},{10,18},{12,20},{14,22},{16,24},... | collective-permute-start | bytes 331784 | tf_op jit(solution)/shard_map/ppermute | solution.py:46
  293.2 2.2 collective-permute-start.43
  296.7 3.1 collective-permute-done.40.refs_12_
  299.9 2.0 shard_map.474
  304.3 2.1 collective-permute-start.46
  306.4 2.0 collective-permute-done.46
  308.4 2.6 collective-permute-start.47
  311.0 2.3 collective-permute-done.47
  315.6 1.7 collective-permute-done.48
  (220 shorter events, 56.8 us)
Async XLA Ops:
  2.6 12.2 %collective-permute-start = (bf16[48,1536]{1,0:T(8,128)(2,1)S(1)}, bf16[48,1536]{1,0:T(8,128)(2,1)S(1)}, u32[]{:S(2)}, u32[]{:S(2)}) collective-permute-start(bf16[48,1536]{1,0:T(8,128)(2,1)S(1)} %pad_maximum_fusion.5), channel_id=1, source_target_pairs={{0,8},{2,10},{4,12},{6,14},{8,16},{10,18},{12,20},{14,22},{16,24},... | collective-permute-start | bytes 442376 | tf_op jit(solution)/shard_map/ppermute | solution.py:46
  5.7 12.3 %collective-permute-start.1 = (bf16[48,1536]{1,0:T(8,128)(2,1)S(1)}, bf16[48,1536]{1,0:T(8,128)(2,1)S(1)}, u32[]{:S(2)}, u32[]{:S(2)}) collective-permute-start(bf16[48,1536]{1,0:T(8,128)(2,1)S(1)} %pad_maximum_fusion.5), channel_id=1, source_target_pairs={{0,16},{2,18},{4,20},{6,22},{8,24},{10,26},{12,28},{14,30},{16,0},... | collective-permute-start | bytes 442376 | tf_op jit(solution)/shard_map/ppermute | solution.py:46
  8.3 9.7 %collective-permute-start.2 = (bf16[48,1536]{1,0:T(8,128)(2,1)S(1)}, bf16[48,1536]{1,0:T(8,128)(2,1)S(1)}, u32[]{:S(2)}, u32[]{:S(2)}) collective-permute-start(bf16[48,1536]{1,0:T(8,128)(2,1)S(1)} %pad_maximum_fusion.5), channel_id=1, source_target_pairs={{0,24},{2,26},{4,28},{6,30},{8,0},{10,2},{12,4},{14,6},{16,8},{18,... | collective-permute-start | bytes 442376 | tf_op jit(solution)/shard_map/ppermute | solution.py:46
  10.8 19.3 %all-to-all-start = ((f32[16,4,768]{2,1,0:T(4,128)}), f32[16,4,768]{2,1,0:T(4,128)S(1)}, u32[]{:S(2)}, u32[]{:S(2)}) async-start(f32[16,4,768]{2,1,0:T(4,128)} %bitcast.114), calls=%async_computation | async-start | bytes 393216 | tf_op jit(solution)/shard_map/all_to_all | solution.py:811
  18.4 23.0 %collective-permute-start.3 = (bf16[4,48,768]{2,1,0:T(8,128)(2,1)S(1)}, bf16[4,48,768]{2,1,0:T(8,128)(2,1)S(1)}, u32[]{:S(2)}, u32[]{:S(2)}) collective-permute-start(bf16[4,48,768]{2,1,0:T(8,128)(2,1)S(1)} %get-tuple-element.185), channel_id=1, source_target_pairs={{0,4},{2,6},{4,0},{6,2},{8,12},{10,14},{12,8},{14,10},{16,20},{18,... | collective-permute-start | bytes 884744 | tf_op jit(solution)/shard_map/ppermute | solution.py:46
  20.0 21.4 %collective-permute-start.4 = (bf16[4,48,768]{2,1,0:T(8,128)(2,1)S(1)}, bf16[4,48,768]{2,1,0:T(8,128)(2,1)S(1)}, u32[]{:S(2)}, u32[]{:S(2)}) collective-permute-start(bf16[4,48,768]{2,1,0:T(8,128)(2,1)S(1)} %get-tuple-element.187), channel_id=1, source_target_pairs={{0,2},{2,0},{4,6},{6,4},{8,10},{10,8},{12,14},{14,12},{16,18},{18,... | collective-permute-start | bytes 884744 | tf_op jit(solution)/shard_map/ppermute | solution.py:46
  21.5 11.7 %collective-permute-start.5 = (bf16[48,1536]{1,0:T(8,128)(2,1)S(1)}, bf16[48,1536]{1,0:T(8,128)(2,1)S(1)}, u32[]{:S(2)}, u32[]{:S(2)}) collective-permute-start(bf16[48,1536]{1,0:T(8,128)(2,1)S(1)} %convert_element_type.28), channel_id=1, source_target_pairs={{0,24},{2,26},{4,28},{6,30},{8,0},{10,2},{12,4},{14,6},{16,8},{18,... | collective-permute-start | bytes 442376 | tf_op jit(solution)/shard_map/ppermute | solution.py:46
  29.4 12.0 %collective-permute-start.6 = (bf16[48,1536]{1,0:T(8,128)(2,1)S(1)}, bf16[48,1536]{1,0:T(8,128)(2,1)S(1)}, u32[]{:S(2)}, u32[]{:S(2)}) collective-permute-start(bf16[48,1536]{1,0:T(8,128)(2,1)S(1)} %convert_element_type.28), channel_id=1, source_target_pairs={{0,16},{2,18},{4,20},{6,22},{8,24},{10,26},{12,28},{14,30},{16,0},... | collective-permute-start | bytes 442376 | tf_op jit(solution)/shard_map/ppermute | solution.py:46
  29.4 12.0 %collective-permute-start.7 = (bf16[48,1536]{1,0:T(8,128)(2,1)S(1)}, bf16[48,1536]{1,0:T(8,128)(2,1)S(1)}, u32[]{:S(2)}, u32[]{:S(2)}) collective-permute-start(bf16[48,1536]{1,0:T(8,128)(2,1)S(1)} %convert_element_type.28), channel_id=1, source_target_pairs={{0,8},{2,10},{4,12},{6,14},{8,16},{10,18},{12,20},{14,22},{16,24},... | collective-permute-start | bytes 442376 | tf_op jit(solution)/shard_map/ppermute | solution.py:46
  41.6 14.8 %collective-permute-start.8 = (bf16[4,2,48,768]{3,2,0,1:T(8,128)(2,1)S(1)}, bf16[4,2,48,768]{3,2,0,1:T(8,128)(2,1)}, u32[]{:S(2)}, u32[]{:S(2)}) collective-permute-start(bf16[4,2,48,768]{3,2,0,1:T(8,128)(2,1)S(1)} %maximum_select_fusion.6), channel_id=1, source_target_pairs={{0,2},{2,0},{4,6},{6,4},{8,10},{10,8},{12,14},{14,12},{16,18},{18,... | collective-permute-start | bytes 1769480 | tf_op jit(solution)/shard_map/ppermute | solution.py:46
  42.3 14.1 %collective-permute-start.9 = (bf16[4,2,48,768]{3,2,0,1:T(8,128)(2,1)S(1)}, bf16[4,2,48,768]{3,2,0,1:T(8,128)(2,1)}, u32[]{:S(2)}, u32[]{:S(2)}) collective-permute-start(bf16[4,2,48,768]{3,2,0,1:T(8,128)(2,1)S(1)} %maximum_select_fusion.7), channel_id=1, source_target_pairs={{0,4},{2,6},{4,0},{6,2},{8,12},{10,14},{12,8},{14,10},{16,20},{18,... | collective-permute-start | bytes 1769480 | tf_op jit(solution)/shard_map/ppermute | solution.py:46
  43.1 12.6 %collective-permute-start.10 = (bf16[48,1536]{1,0:T(8,128)(2,1)S(1)}, bf16[48,1536]{1,0:T(8,128)(2,1)}, u32[]{:S(2)}, u32[]{:S(2)}) collective-permute-start(bf16[48,1536]{1,0:T(8,128)(2,1)S(1)} %convert_bitcast_fusion), channel_id=1, source_target_pairs={{0,24},{2,26},{4,28},{6,30},{8,0},{10,2},{12,4},{14,6},{16,8},{18,... | collective-permute-start | bytes 442376 | tf_op jit(solution)/shard_map/ppermute | solution.py:46
  43.2 13.2 %collective-permute-start.11 = (bf16[48,1536]{1,0:T(8,128)(2,1)S(1)}, bf16[48,1536]{1,0:T(8,128)(2,1)}, u32[]{:S(2)}, u32[]{:S(2)}) collective-permute-start(bf16[48,1536]{1,0:T(8,128)(2,1)S(1)} %convert_bitcast_fusion), channel_id=1, source_target_pairs={{0,16},{2,18},{4,20},{6,22},{8,24},{10,26},{12,28},{14,30},{16,0},... | collective-permute-start | bytes 442376 | tf_op jit(solution)/shard_map/ppermute | solution.py:46
  44.0 12.3 %collective-permute-start.12 = (bf16[48,1536]{1,0:T(8,128)(2,1)S(1)}, bf16[48,1536]{1,0:T(8,128)(2,1)}, u32[]{:S(2)}, u32[]{:S(2)}) collective-permute-start(bf16[48,1536]{1,0:T(8,128)(2,1)S(1)} %convert_bitcast_fusion), channel_id=1, source_target_pairs={{0,8},{2,10},{4,12},{6,14},{8,16},{10,18},{12,20},{14,22},{16,24},... | collective-permute-start | bytes 442376 | tf_op jit(solution)/shard_map/ppermute | solution.py:46
  59.7 21.5 %collective-permute-start.15 = (bf16[768,1536]{1,0:T(8,128)(2,1)S(1)}, bf16[768,1536]{1,0:T(8,128)(2,1)S(1)}, u32[]{:S(2)}, u32[]{:S(2)}) collective-permute-start(bf16[768,1536]{1,0:T(8,128)(2,1)S(1)} %pad_maximum_fusion.refs_4_.refs_5_.refs_6_.refs_7_), channel_id=1, source_target_pairs={{0,1},{1,0},{2,3},{3,2},{4,5},{5,4},{6,7},{7,6},{8,9},{9,8},{10,11... | collective-permute-start | bytes 7077896 | tf_op jit(solution)/shard_map/ppermute | solution.py:55
  61.2 14.6 %collective-permute-start.13 = (bf16[4,48,1536]{2,1,0:T(8,128)(2,1)S(1)}, bf16[4,48,1536]{2,1,0:T(8,128)(2,1)S(1)}, u32[]{:S(2)}, u32[]{:S(2)}) collective-permute-start(bf16[4,48,1536]{2,1,0:T(8,128)(2,1)S(1)} %get-tuple-element.345), channel_id=1, source_target_pairs={{0,4},{2,6},{4,0},{6,2},{8,12},{10,14},{12,8},{14,10},{16,20},{18,... | collective-permute-start | bytes 1769480 | tf_op jit(solution)/shard_map/ppermute | solution.py:46
  63.6 15.3 %collective-permute-start.14 = (bf16[4,48,1536]{2,1,0:T(8,128)(2,1)S(1)}, bf16[4,48,1536]{2,1,0:T(8,128)(2,1)S(1)}, u32[]{:S(2)}, u32[]{:S(2)}) collective-permute-start(bf16[4,48,1536]{2,1,0:T(8,128)(2,1)S(1)} %get-tuple-element.339), channel_id=1, source_target_pairs={{0,2},{2,0},{4,6},{6,4},{8,10},{10,8},{12,14},{14,12},{16,18},{18,... | collective-permute-start | bytes 1769480 | tf_op jit(solution)/shard_map/ppermute | solution.py:46
  75.9 27.4 %collective-permute-start.16 = (bf16[4,2,48,1536]{3,2,0,1:T(8,128)(2,1)S(1)}, bf16[4,2,48,1536]{3,2,0,1:T(8,128)(2,1)}, u32[]{:S(2)}, u32[]{:S(2)}) collective-permute-start(bf16[4,2,48,1536]{3,2,0,1:T(8,128)(2,1)S(1)} %maximum_select_fusion.2), channel_id=1, source_target_pairs={{0,2},{2,0},{4,6},{6,4},{8,10},{10,8},{12,14},{14,12},{16,18},{18,... | collective-permute-start | bytes 3538952 | tf_op jit(solution)/shard_map/ppermute | solution.py:46
  80.1 25.5 %collective-permute-start.17 = (bf16[4,2,48,1536]{3,2,0,1:T(8,128)(2,1)}, bf16[4,2,48,1536]{3,2,0,1:T(8,128)(2,1)}, u32[]{:S(2)}, u32[]{:S(2)}) collective-permute-start(bf16[4,2,48,1536]{3,2,0,1:T(8,128)(2,1)} %maximum_select_fusion.3), channel_id=1, source_target_pairs={{0,4},{2,6},{4,0},{6,2},{8,12},{10,14},{12,8},{14,10},{16,20},{18,... | collective-permute-start | bytes 3538952 | tf_op jit(solution)/shard_map/ppermute | solution.py:46
  107.8 4.6 %collective-permute-start.18 = (bf16[768,1536]{1,0:T(8,128)(2,1)S(1)}, bf16[768,1536]{1,0:T(8,128)(2,1)S(1)}, u32[]{:S(2)}, u32[]{:S(2)}) collective-permute-start(bf16[768,1536]{1,0:T(8,128)(2,1)S(1)} %bitcast.175), channel_id=1, source_target_pairs={{0,1},{1,0},{2,3},{3,2},{4,5},{5,4},{6,7},{7,6},{8,9},{9,8},{10,11... | collective-permute-start | bytes 7077896 | tf_op jit(solution)/shard_map/ppermute | solution.py:55
  111.6 4.6 %collective-permute-start.19 = (bf16[768,1536]{1,0:T(8,128)(2,1)S(1)}, bf16[768,1536]{1,0:T(8,128)(2,1)S(1)}, u32[]{:S(2)}, u32[]{:S(2)}) collective-permute-start(bf16[768,1536]{1,0:T(8,128)(2,1)S(1)} %bitcast.177), channel_id=1, source_target_pairs={{0,1},{1,0},{2,3},{3,2},{4,5},{5,4},{6,7},{7,6},{8,9},{9,8},{10,11... | collective-permute-start | bytes 7077896 | tf_op jit(solution)/shard_map/ppermute | solution.py:55
  180.5 10.1 %collective-permute-start.20 = (bf16[768,1408]{1,0:T(8,128)(2,1)}, bf16[768,1408]{1,0:T(8,128)(2,1)}, u32[]{:S(2)}, u32[]{:S(2)}) collective-permute-start(bf16[768,1408]{1,0:T(8,128)(2,1)} %get-tuple-element.221), channel_id=1, source_target_pairs={{0,1},{1,0},{2,3},{3,2},{4,5},{5,4},{6,7},{7,6},{8,9},{9,8},{10,11... | collective-permute-start | bytes 6488072 | tf_op jit(solution)/shard_map/ppermute | solution.py:55
  180.8 8.8 %collective-permute-start.21 = (bf16[768,1280]{1,0:T(8,128)(2,1)}, bf16[768,1280]{1,0:T(8,128)(2,1)S(1)}, u32[]{:S(2)}, u32[]{:S(2)}) collective-permute-start(bf16[768,1280]{1,0:T(8,128)(2,1)} %get-tuple-element.223), channel_id=1, source_target_pairs={{0,1},{1,0},{2,3},{3,2},{4,5},{5,4},{6,7},{7,6},{8,9},{9,8},{10,11... | collective-permute-start | bytes 5898248 | tf_op jit(solution)/shard_map/ppermute | solution.py:55
  181.1 8.5 %collective-permute-start.22 = (bf16[768,768]{1,0:T(8,128)(2,1)}, bf16[768,768]{1,0:T(8,128)(2,1)S(1)}, u32[]{:S(2)}, u32[]{:S(2)}) collective-permute-start(bf16[768,768]{1,0:T(8,128)(2,1)} %get-tuple-element.225), channel_id=1, source_target_pairs={{0,1},{1,0},{2,3},{3,2},{4,5},{5,4},{6,7},{7,6},{8,9},{9,8},{10,11... | collective-permute-start | bytes 3538952 | tf_op jit(solution)/shard_map/ppermute | solution.py:55
  182.9 14.7 %all-to-all-start.1 = ((f32[16,4,768]{2,1,0:T(4,128)}), f32[16,4,768]{2,1,0:T(4,128)}, u32[]{:S(2)}, u32[]{:S(2)}) async-start(f32[16,4,768]{2,1,0:T(4,128)} %reshape.168), calls=%async_computation.1 | async-start | bytes 393216 | tf_op jit(solution)/shard_map/all_to_all | solution.py:952
  197.7 36.3 %collective-permute-start.23 = (bf16[4,2,48,1408]{3,2,1,0:T(8,128)(2,1)}, bf16[4,2,48,1408]{3,2,1,0:T(8,128)(2,1)S(1)}, u32[]{:S(2)}, u32[]{:S(2)}) collective-permute-start(bf16[4,2,48,1408]{3,2,1,0:T(8,128)(2,1)} %get-tuple-element.232), channel_id=1, source_target_pairs={{0,2},{2,0},{4,6},{6,4},{8,10},{10,8},{12,14},{14,12},{16,18},{18,... | collective-permute-start | bytes 3244040 | tf_op jit(solution)/shard_map/ppermute | solution.py:46
  199.2 34.7 %collective-permute-start.24 = (bf16[4,2,48,1280]{3,2,1,0:T(8,128)(2,1)}, bf16[4,2,48,1280]{3,2,1,0:T(8,128)(2,1)}, u32[]{:S(2)}, u32[]{:S(2)}) collective-permute-start(bf16[4,2,48,1280]{3,2,1,0:T(8,128)(2,1)} %get-tuple-element.233), channel_id=1, source_target_pairs={{0,4},{2,6},{4,0},{6,2},{8,12},{10,14},{12,8},{14,10},{16,20},{18,... | collective-permute-start | bytes 2949128 | tf_op jit(solution)/shard_map/ppermute | solution.py:46
  200.6 33.3 %collective-permute-start.25 = (bf16[2,2,48,768]{3,2,1,0:T(8,128)(2,1)}, bf16[2,2,48,768]{3,2,1,0:T(8,128)(2,1)S(1)}, u32[]{:S(2)}, u32[]{:S(2)}) collective-permute-start(bf16[2,2,48,768]{3,2,1,0:T(8,128)(2,1)} %bitcast.193), channel_id=1, source_target_pairs={{0,8},{2,10},{4,12},{6,14},{8,16},{10,18},{12,20},{14,22},{16,24},... | collective-permute-start | bytes 884744 | tf_op jit(solution)/shard_map/ppermute | solution.py:46
  202.1 31.8 %collective-permute-start.26 = (bf16[2,2,48,768]{3,2,1,0:T(8,128)(2,1)}, bf16[2,2,48,768]{3,2,1,0:T(8,128)(2,1)S(1)}, u32[]{:S(2)}, u32[]{:S(2)}) collective-permute-start(bf16[2,2,48,768]{3,2,1,0:T(8,128)(2,1)} %bitcast.192), channel_id=1, source_target_pairs={{0,16},{2,18},{4,20},{6,22},{8,24},{10,26},{12,28},{14,30},{16,0},... | collective-permute-start | bytes 884744 | tf_op jit(solution)/shard_map/ppermute | solution.py:46
  204.4 29.5 %collective-permute-start.27 = (bf16[2,2,48,768]{3,2,1,0:T(8,128)(2,1)}, bf16[2,2,48,768]{3,2,1,0:T(8,128)(2,1)S(1)}, u32[]{:S(2)}, u32[]{:S(2)}) collective-permute-start(bf16[2,2,48,768]{3,2,1,0:T(8,128)(2,1)} %bitcast.191), channel_id=1, source_target_pairs={{0,24},{2,26},{4,28},{6,30},{8,0},{10,2},{12,4},{14,6},{16,8},{18,... | collective-permute-start | bytes 884744 | tf_op jit(solution)/shard_map/ppermute | solution.py:46
  234.7 5.8 %collective-permute-start.28 = (bf16[768,1152]{1,0:T(8,128)(2,1)}, bf16[768,1152]{1,0:T(8,128)(2,1)}, u32[]{:S(2)}, u32[]{:S(2)}) collective-permute-start(bf16[768,1152]{1,0:T(8,128)(2,1)} %get-tuple-element.245), channel_id=1, source_target_pairs={{0,1},{1,0},{2,3},{3,2},{4,5},{5,4},{6,7},{7,6},{8,9},{9,8},{10,11... | collective-permute-start | bytes 5308424 | tf_op jit(solution)/shard_map/ppermute | solution.py:55
  235.1 13.7 %collective-permute-start.32 = (bf16[2048,384]{1,0:T(8,128)(2,1)}, bf16[2048,384]{1,0:T(8,128)(2,1)}, u32[]{:S(2)}, u32[]{:S(2)}) collective-permute-start(bf16[2048,384]{1,0:T(8,128)(2,1)} %get-tuple-element.264), channel_id=1, source_target_pairs={{0,1},{1,0},{2,3},{3,2},{4,5},{5,4},{6,7},{7,6},{8,9},{9,8},{10,11... | collective-permute-start | bytes 4718600 | tf_op jit(solution)/shard_map/ppermute | solution.py:55
  240.5 18.1 %collective-permute-start.29 = (bf16[4,48,1408]{2,1,0:T(8,128)(2,1)}, bf16[4,48,1408]{2,1,0:T(8,128)(2,1)}, u32[]{:S(2)}, u32[]{:S(2)}) collective-permute-start(bf16[4,48,1408]{2,1,0:T(8,128)(2,1)} %get-tuple-element.258), channel_id=1, source_target_pairs={{0,4},{2,6},{4,0},{6,2},{8,12},{10,14},{12,8},{14,10},{16,20},{18,... | collective-permute-start | bytes 1622024 | tf_op jit(solution)/shard_map/ppermute | solution.py:46
  242.1 16.6 %collective-permute-start.30 = (bf16[4,48,1280]{2,1,0:T(8,128)(2,1)}, bf16[4,48,1280]{2,1,0:T(8,128)(2,1)}, u32[]{:S(2)}, u32[]{:S(2)}) collective-permute-start(bf16[4,48,1280]{2,1,0:T(8,128)(2,1)} %get-tuple-element.259), channel_id=1, source_target_pairs={{0,2},{2,0},{4,6},{6,4},{8,10},{10,8},{12,14},{14,12},{16,18},{18,... | collective-permute-start | bytes 1474568 | tf_op jit(solution)/shard_map/ppermute | solution.py:46
  242.1 16.6 %collective-permute-start.31 = (bf16[2,48,768]{2,1,0:T(8,128)(2,1)}, bf16[2,48,768]{2,1,0:T(8,128)(2,1)S(1)}, u32[]{:S(2)}, u32[]{:S(2)}) collective-permute-start(bf16[2,48,768]{2,1,0:T(8,128)(2,1)} %bitcast.194), channel_id=1, source_target_pairs={{0,2},{2,0},{4,6},{6,4},{8,10},{10,8},{12,14},{14,12},{16,18},{18,... | collective-permute-start | bytes 442376 | tf_op jit(solution)/shard_map/ppermute | solution.py:46
  264.1 12.6 %collective-permute-start.34 = (bf16[4,2,48,640]{3,2,1,0:T(8,128)(2,1)}, bf16[4,2,48,640]{3,2,1,0:T(8,128)(2,1)S(1)}, u32[]{:S(2)}, u32[]{:S(2)}) collective-permute-start(bf16[4,2,48,640]{3,2,1,0:T(8,128)(2,1)} %copy-done.28), channel_id=1, source_target_pairs={{0,4},{2,6},{4,0},{6,2},{8,12},{10,14},{12,8},{14,10},{16,20},{18,... | collective-permute-start | bytes 1474568 | tf_op jit(solution)/shard_map/ppermute | solution.py:46
  264.7 10.2 %collective-permute-start.33 = (bf16[4,2,48,512]{3,2,1,0:T(8,128)(2,1)}, bf16[4,2,48,512]{3,2,1,0:T(8,128)(2,1)S(1)}, u32[]{:S(2)}, u32[]{:S(2)}) collective-permute-start(bf16[4,2,48,512]{3,2,1,0:T(8,128)(2,1)} %copy-done.29), channel_id=1, source_target_pairs={{0,2},{2,0},{4,6},{6,4},{8,10},{10,8},{12,14},{14,12},{16,18},{18,... | collective-permute-start | bytes 1179656 | tf_op jit(solution)/shard_map/ppermute | solution.py:46
  265.5 15.4 %collective-permute-start.37 = (bf16[48,2688]{1,0:T(8,128)(2,1)}, bf16[48,2688]{1,0:T(8,128)(2,1)S(1)}, u32[]{:S(2)}, u32[]{:S(2)}) collective-permute-start(bf16[48,2688]{1,0:T(8,128)(2,1)} %get-tuple-element.279), channel_id=1, source_target_pairs={{0,8},{2,10},{4,12},{6,14},{8,16},{10,18},{12,20},{14,22},{16,24},... | collective-permute-start | bytes 774152 | tf_op jit(solution)/shard_map/ppermute | solution.py:46
  265.8 19.8 %collective-permute-start.38 = (bf16[48,2688]{1,0:T(8,128)(2,1)}, bf16[48,2688]{1,0:T(8,128)(2,1)S(1)}, u32[]{:S(2)}, u32[]{:S(2)}) collective-permute-start(bf16[48,2688]{1,0:T(8,128)(2,1)} %get-tuple-element.280), channel_id=1, source_target_pairs={{0,16},{2,18},{4,20},{6,22},{8,24},{10,26},{12,28},{14,30},{16,0},... | collective-permute-start | bytes 774152 | tf_op jit(solution)/shard_map/ppermute | solution.py:46
  266.4 19.2 %collective-permute-start.39 = (bf16[48,2688]{1,0:T(8,128)(2,1)}, bf16[48,2688]{1,0:T(8,128)(2,1)S(1)}, u32[]{:S(2)}, u32[]{:S(2)}) collective-permute-start(bf16[48,2688]{1,0:T(8,128)(2,1)} %get-tuple-element.281), channel_id=1, source_target_pairs={{0,24},{2,26},{4,28},{6,30},{8,0},{10,2},{12,4},{14,6},{16,8},{18,... | collective-permute-start | bytes 774152 | tf_op jit(solution)/shard_map/ppermute | solution.py:46
  279.4 6.3 %collective-permute-start.36 = (bf16[4,48,640]{2,1,0:T(8,128)(2,1)S(1)}, bf16[4,48,640]{2,1,0:T(8,128)(2,1)S(1)}, u32[]{:S(2)}, u32[]{:S(2)}) collective-permute-start(bf16[4,48,640]{2,1,0:T(8,128)(2,1)S(1)} %get-tuple-element.278), channel_id=1, source_target_pairs={{0,2},{2,0},{4,6},{6,4},{8,10},{10,8},{12,14},{14,12},{16,18},{18,... | collective-permute-start | bytes 737288 | tf_op jit(solution)/shard_map/ppermute | solution.py:46
  280.1 5.7 %collective-permute-start.35 = (bf16[4,48,512]{2,1,0:T(8,128)(2,1)S(1)}, bf16[4,48,512]{2,1,0:T(8,128)(2,1)S(1)}, u32[]{:S(2)}, u32[]{:S(2)}) collective-permute-start(bf16[4,48,512]{2,1,0:T(8,128)(2,1)S(1)} %get-tuple-element.277), channel_id=1, source_target_pairs={{0,4},{2,6},{4,0},{6,2},{8,12},{10,14},{12,8},{14,10},{16,20},{18,... | collective-permute-start | bytes 589832 | tf_op jit(solution)/shard_map/ppermute | solution.py:46
  285.9 16.0 %collective-permute-start.44 = (f32[16,4,768]{2,1,0:T(4,128)}, f32[16,4,768]{2,1,0:T(4,128)S(1)}, u32[]{:S(2)}, u32[]{:S(2)}) collective-permute-start(f32[16,4,768]{2,1,0:T(4,128)} %all-to-all-done.1), channel_id=1, source_target_pairs={{0,1},{1,0},{2,3},{3,2},{4,5},{5,4},{6,7},{7,6},{8,9},{9,8},{10,11... | collective-permute-start | bytes 589832 | tf_op jit(solution)/shard_map/ppermute | solution.py:55
  288.1 13.8 %collective-permute-start.41 = (bf16[48,1152]{1,0:T(8,128)(2,1)S(1)}, bf16[48,1152]{1,0:T(8,128)(2,1)S(1)}, u32[]{:S(2)}, u32[]{:S(2)}) collective-permute-start(bf16[48,1152]{1,0:T(8,128)(2,1)S(1)} %get-tuple-element.295), channel_id=1, source_target_pairs={{0,8},{2,10},{4,12},{6,14},{8,16},{10,18},{12,20},{14,22},{16,24},... | collective-permute-start | bytes 331784 | tf_op jit(solution)/shard_map/ppermute | solution.py:46
  292.9 8.9 %collective-permute-start.42 = (bf16[48,1152]{1,0:T(8,128)(2,1)S(1)}, bf16[48,1152]{1,0:T(8,128)(2,1)S(1)}, u32[]{:S(2)}, u32[]{:S(2)}) collective-permute-start(bf16[48,1152]{1,0:T(8,128)(2,1)S(1)} %get-tuple-element.296), channel_id=1, source_target_pairs={{0,16},{2,18},{4,20},{6,22},{8,24},{10,26},{12,28},{14,30},{16,0},... | collective-permute-start | bytes 331784 | tf_op jit(solution)/shard_map/ppermute | solution.py:46
  293.2 8.7 %collective-permute-start.43 = (bf16[48,1152]{1,0:T(8,128)(2,1)S(1)}, bf16[48,1152]{1,0:T(8,128)(2,1)S(1)}, u32[]{:S(2)}, u32[]{:S(2)}) collective-permute-start(bf16[48,1152]{1,0:T(8,128)(2,1)S(1)} %get-tuple-element.297), channel_id=1, source_target_pairs={{0,24},{2,26},{4,28},{6,30},{8,0},{10,2},{12,4},{14,6},{16,8},{18,... | collective-permute-start | bytes 331784 | tf_op jit(solution)/shard_map/ppermute | solution.py:46
  295.4 4.4 %collective-permute-start.40 = (bf16[48,768]{1,0:T(8,128)(2,1)S(1)}, bf16[48,768]{1,0:T(8,128)(2,1)S(1)}, u32[]{:S(2)}, u32[]{:S(2)}) collective-permute-start(bf16[48,768]{1,0:T(8,128)(2,1)S(1)} %bitcast.198), channel_id=1, source_target_pairs={{0,4},{2,6},{4,0},{6,2},{8,12},{10,14},{12,8},{14,10},{16,20},{18,... | collective-permute-start | bytes 221192 | tf_op jit(solution)/shard_map/ppermute | solution.py:46
  308.4 4.9 %collective-permute-start.47 = (f32[80,128]{1,0:T(8,128)S(1)}, f32[80,128]{1,0:T(8,128)S(1)}, u32[]{:S(2)}, u32[]{:S(2)}) collective-permute-start(f32[80,128]{1,0:T(8,128)S(1)} %add.62), channel_id=1, source_target_pairs={{0,16},{2,18},{4,20},{6,22},{8,24},{10,26},{12,28},{14,30},{16,0},... | collective-permute-start | bytes 122888 | tf_op jit(solution)/shard_map/ppermute | solution.py:91
  (53 other events, 324.2 us)

commit v4 on v3

--- a/solution.py
+++ b/solution.py
@@ -775,7 +775,7 @@
     def flip(value):
         return jnp.where(core == 0, value, value[::-1])
 
-    chunk = jnp.concatenate([qkv_weight[0], qkv_weight[1], qkv_weight[2], out_weight.T], axis=1)
+    chunk = jnp.concatenate([part.astype(BF) for part in (*qkv_weight, out_weight.T)], axis=1)
     first, others = dims[0], dims[1:]
     orders = (others, others[::-1])
     sides = (0, 1)
@@ -815,7 +815,7 @@
             own.reshape(mine, 2, width), core, 1, keepdims=False
         )
 
-    pieces0 = gather_send(chunk.astype(BF), first)
+    pieces0 = gather_send(chunk, first)
     qkvo = gather_start(pieces0)
     pieces0 = gather_out(qkvo)
     own, held = lax.optimization_barrier((in_weight, [pieces[0] for pieces in pieces0]))

time: 325 us -> 325 us (level)
  no operation moved by 1% of the time
where the time goes in v4:
time: 325 us; the launch traced here: 324 us
  Pallas kernels  154 us (47%)
  starting transfers between devices  73 us (22%)
  waiting for transfers between devices  61.3 us (19%)
  local copies, waits for them, and re-layouts  18 us (6%)
  other arithmetic  16.6 us (5%)
    pallas_call x3, Pallas kernels, call(): pl.pallas_call(body, grid_spec=pltpu.PrefetchScalarGridSpec(num_scalar_pr...  110 us
    ppermute x36, starting transfers between devices, dp_shift(): return lax.ppermute(value, 'dp', pairs)  54.8 us
    ppermute x36, waiting for transfers between devices, dp_shift(): return lax.ppermute(value, 'dp', pairs)  48.5 us
    pallas_call x6, Pallas kernels, slab_sums(): pl.pallas_call(kernel, grid_spec=pltpu.PrefetchScalarGridSpec(num_scalar_...  23.8 us
    unnamed x99, local copies, waits for them, and re-layouts  11.2 us
    select_n x8, other arithmetic, arrange(): jnp.where(place == 0, jnp.stack(pieces, axis), jnp.stack(pieces[::-1], ax...  10.1 us
    pallas_call x1, Pallas kernels, shards(): pl.pallas_call(pack_kernel, out_shape=(shape_of((most, width), BF), shape...  8.62 us
    ppermute x4, starting transfers between devices, sum_all(): value = value + lax.ppermute(value, 'dp', pairs)  7.36 us
  transfers between devices with their start and end apart: 52, of which 22 were waited for; matrix products, arithmetic and copies ran while one was open for 5% of the time, Pallas kernels for 26%

profile of v4, /device:TPU:0, one launch (start us, length us, event | category | flops | bytes accessed | tf_op | source)
XLA Modules:
  0.0 324.2 jit_solution(5017649496510317545)
XLA Ops:
  2.6 3.1 collective-permute-start
  5.7 2.6 collective-permute-start.1
  10.8 3.9 %all-to-all-start = ((f32[16,4,768]{2,1,0:T(4,128)}), f32[16,4,768]{2,1,0:T(4,128)S(1)}, u32[]{:S(2)}, u32[]{:S(2)}) async-start(f32[16,4,768]{2,1,0:T(4,128)} %bitcast.114), calls=%async_computation | async-start | bytes 393216 | tf_op jit(solution)/shard_map/all_to_all | solution.py:811
  14.8 3.2 collective-permute-done.1
  18.4 1.6 collective-permute-start.3
  21.5 7.9 %collective-permute-start.5 = (bf16[48,1536]{1,0:T(8,128)(2,1)S(1)}, bf16[48,1536]{1,0:T(8,128)(2,1)S(1)}, u32[]{:S(2)}, u32[]{:S(2)}) collective-permute-start(bf16[48,1536]{1,0:T(8,128)(2,1)S(1)} %convert_element_type.46), channel_id=1, source_target_pairs={{0,24},{2,26},{4,28},{6,30},{8,0},{10,2},{12,4},{14,6},{16,8},{18,... | collective-permute-start | bytes 442376 | tf_op jit(solution)/shard_map/ppermute | solution.py:46
  30.1 3.1 collective-permute-done.5
  33.2 8.2 %collective-permute-done.6 = bf16[48,1536]{1,0:T(8,128)(2,1)S(1)} collective-permute-done((bf16[48,1536]{1,0:T(8,128)(2,1)S(1)}, bf16[48,1536]{1,0:T(8,128)(2,1)S(1)}, u32[]{:S(2)}, u32[]{:S(2)}) %collective-permute-start.6) | collective-permute-done | bytes 147488 | tf_op jit(solution)/shard_map/ppermute | solution.py:46
  44.0 1.9 collective-permute-start.12
  47.1 8.6 %shard_map.463 = (bf16[2048,768]{1,0:T(8,128)(2,1)}, f32[2048,128]{1,0:T(8,128)}, s32[2,64]{1,0:T(2,128)}, s32[1]{0:T(128)}) custom-call(s32[1]{0:T(128)} %bitcast.3.core_ref.refs_0_, s32[128]{0:T(128)} %order_ref.1, s32[128]{0:T(128)} %len_ref.3, bf16[128,32,768]{2,1,0:T(8,128)(2,1)} %tok_ref.1), custom_call_target="tpu_custom_call" | custom-call | bytes 30000000 | tf_op jit(solution)/shard_map/pallas_call | solution.py:831
  63.6 1.6 collective-permute-start.14
  66.0 9.8 %collective-permute-done.13 = bf16[4,48,1536]{2,1,0:T(8,128)(2,1)S(1)} collective-permute-done((bf16[4,48,1536]{2,1,0:T(8,128)(2,1)S(1)}, bf16[4,48,1536]{2,1,0:T(8,128)(2,1)S(1)}, u32[]{:S(2)}, u32[]{:S(2)}) %collective-permute-start.13) | collective-permute-done | bytes 589856 | tf_op jit(solution)/shard_map/ppermute | solution.py:46
  75.9 1.6 collective-permute-start.16
  82.5 19.4 %shard_map.464 = (bf16[2048,2304]{1,0:T(8,128)(2,1)}, bf16[2048,768]{1,0:T(8,128)(2,1)}, f32[2048,768]{1,0:T(8,128)}, f32[2048,128]{1,0:T(8,128)}) custom-call(s32[1]{0:T(128)} %get-tuple-element.237.tiles_ref, s32[1]{0:T(128)} %bitcast.3.core_ref.refs_0_, bf16[2048,768]{1,0:T(8,128)(2,1)} %get-tuple-element.206.refs_1_.refs_2_, ...), custom_call_target="tpu_custom_call" | custom-call | flops 11596411904 | bytes 30000000 | tf_op jit(solution)/shard_map/pallas_call | solution.py:517
  101.9 1.5 collective-permute-done.16
  103.4 2.2 collective-permute-done.17
  105.5 2.1 maximum_select_fusion
  107.9 3.5 %maximum_select_fusion.1 = bf16[4,2,2,48,1536]{4,3,0,2,1:T(8,128)(2,1)S(1)} fusion(bf16[4,1,2,48,1536]{4,3,0,2,1:T(8,128)(2,1)} %bitcast.40, bf16[4,1,2,48,1536]{4,3,0,2,1:T(8,128)(2,1)} %bitcast.39, pred[]{:T(512)S(6)} %eq.31), kind=kLoop, calls=%fused_computation.3 | loop fusion | flops 3538944 | bytes 4718593 | tf_op jit(solution)/shard_map/jit(_where)/select_n | solution.py:62
  113.0 3.2 collective-permute-done.19.refs_11_
  117.7 62.8 %shard_map.465 = (f32[2048,768]{1,0:T(8,128)}, f32[64,768]{1,0:T(8,128)}, f32[8,9216]{1,0:T(8,128)}, bf16[768,1408]{1,0:T(8,128)(2,1)}, bf16[768,1408]{1,0:T(8,1...) custom-call(s32[1]{0:T(128)} %get-tuple-element.237.tiles_ref, ...), custom_call_target="tpu_custom_call" | custom-call | flops 34789236736 | bytes 30000000 | tf_op jit(solution)/shard_map/pallas_call | solution.py:517
  181.3 1.7 reshape.171
  182.9 5.5 %all-to-all-start.1 = ((f32[16,4,768]{2,1,0:T(4,128)}), f32[16,4,768]{2,1,0:T(4,128)}, u32[]{:S(2)}, u32[]{:S(2)}) async-start(f32[16,4,768]{2,1,0:T(4,128)} %reshape.171), calls=%async_computation.1 | async-start | bytes 393216 | tf_op jit(solution)/shard_map/all_to_all | solution.py:952
  191.8 5.8 %shard_map.466 = (bf16[4,2,48,1408]{3,2,1,0:T(8,128)(2,1)}, bf16[4,2,48,1280]{3,2,1,0:T(8,128)(2,1)}, bf16[1,2,2,48,768]{4,3,2,1,0:T(8,128)(2,1)}, bf16[1,2,2,48...) custom-call(s32[3]{0:T(128)} %pad_add_fusion.places_ref, bf16[4,2,2,48,1408]{4,3,2,1,0:T(8,128)(2,1)} %bitcast.144, ...), custom_call_target="tpu_custom_call" | custom-call | bytes 8000000 | tf_op jit(solution)/shard_map/pallas_call | solution.py:641
  197.7 1.5 collective-permute-start.23
  200.6 1.5 collective-permute-start.25
  202.1 2.3 collective-permute-start.26
  204.4 1.5 collective-permute-start.27
  205.9 27.9 %shard_map.467 = (f32[2048,384]{1,0:T(8,128)}, bf16[2048,384]{1,0:T(8,128)(2,1)}, f32[72,128]{1,0:T(8,128)}, bf16[768,1152]{1,0:T(8,128)(2,1)}, bf16[768,1152]{1,0:T(8,128)(2,1)}) custom-call(s32[1]{0:T(128)} %get-tuple-element.237.tiles_ref, s32[1]{0:T(128)} %bitcast.3.core_ref.refs_0_, f32[2048,768]{1,0:T(8,128)} %get-tuple-element.238.refs_1_, ...), custom_call_target="tpu_custom_call" | custom-call | flops 26091925504 | bytes 30000000 | tf_op jit(solution)/shard_map/pallas_call | solution.py:517
  235.3 5.2 %shard_map.468 = (bf16[4,48,1408]{2,1,0:T(8,128)(2,1)}, bf16[4,48,1280]{2,1,0:T(8,128)(2,1)}, bf16[1,2,48,768]{3,2,1,0:T(8,128)(2,1)}) custom-call(s32[3]{0:T(128)} %pad_add_fusion.places_ref, bf16[4,2,2,48,1408]{4,3,2,1,0:T(8,128)(2,1)} %bitcast.145, bf16[4,2,2,48,1408]{4,3,2,1,0:T(8,128)(2,1)} %bitcast.43.refs_1_.refs_5_.refs_9_.refs_13_, ...), custom_call_target="tpu_custom_call" | custom-call | bytes 8000000 | tf_op jit(solution)/shard_map/pallas_call | solution.py:641
  243.9 3.1 shard_map.470
  248.6 6.7 %shard_map.469 = f32[128,32,384]{2,1,0:T(8,128)} custom-call(s32[1]{0:T(128)} %bitcast.3.core_ref.refs_0_, s32[128]{0:T(128)} %order_ref.1, s32[128]{0:T(128)} %len_ref.3, s32[2,64]{1,0:T(2,128)} %get-tuple-element.262.off_ref, f32[2048,384]{1,0:T(8,128)} %get-tuple-element.263.mine_ref, bf16[2048,384]{1,0:T(8,128)(2,1)} %collective-permute-done.32.recv_ref), custom_call_target="tpu_custom_call" | custom-call | bytes 20000000 | tf_op jit(solution)/shard_map/pallas_call | solution.py:1003
  255.3 3.2 collective-permute-done.31.refs_37_.refs_43_
  259.1 4.8 %shard_map.471 = (f32[1,48,768]{2,1,0:T(8,128)}, bf16[1,48,768]{2,1,0:T(8,128)(2,1)}, f32[48,2688]{1,0:T(8,128)}, bf16[48,2688]{1,0:T(8,128)(2,1)}, bf16[48,2688]{1,0:T(8,128)(2,1)}, /*index=5*/bf16[48,2688]{1,0:T(8,128)(2,1)}) custom-call(s32[3]{0:T(128)} %pad_add_fusion.places_ref, bf16[4,2,2,48,1408]{4,3,2,1,0:T(8,128)(2,1)} %bitcast.146, ...), custom_call_target="tpu_custom_call" | custom-call | bytes 8000000 | tf_op jit(solution)/shard_map/pallas_call | solution.py:641
  266.4 2.9 collective-permute-start.39
  269.3 5.6 %collective-permute-done.33.refs_2_.refs_6_.refs_10_.refs_14_ = bf16[4,2,48,512]{3,2,1,0:T(8,128)(2,1)S(1)} collective-permute-done((bf16[4,2,48,512]{3,2,1,0:T(8,128)(2,1)}, bf16[4,2,48,512]{3,2,1,0:T(8,128)(2,1)S(1)}, u32[]{:S(2)}, u32[]{:S(2)}) %collective-permute-start.33) | collective-permute-done | bytes 393248 | tf_op jit(solution)/shard_map/ppermute | solution.py:46
  274.9 1.6 collective-permute-done.34.refs_5_.refs_18_.refs_22_.refs_26_.refs_30_
  276.5 2.7 shard_map.472
  280.8 4.7 %collective-permute-done.38.refs_10_ = bf16[48,2688]{1,0:T(8,128)(2,1)S(1)} collective-permute-done((bf16[48,2688]{1,0:T(8,128)(2,1)}, bf16[48,2688]{1,0:T(8,128)(2,1)S(1)}, u32[]{:S(2)}, u32[]{:S(2)}) %collective-permute-start.38) | collective-permute-done | bytes 258080 | tf_op jit(solution)/shard_map/ppermute | solution.py:46
  285.9 2.1 shard_map.473
  288.0 5.0 %collective-permute-start.41 = (bf16[48,1152]{1,0:T(8,128)(2,1)S(1)}, bf16[48,1152]{1,0:T(8,128)(2,1)S(1)}, u32[]{:S(2)}, u32[]{:S(2)}) collective-permute-start(bf16[48,1152]{1,0:T(8,128)(2,1)S(1)} %get-tuple-element.295), channel_id=1, source_target_pairs={{0,8},{2,10},{4,12},{6,14},{8,16},{10,18},{12,20},{14,22},{16,24},... | collective-permute-start | bytes 331784 | tf_op jit(solution)/shard_map/ppermute | solution.py:46
  293.2 2.2 collective-permute-start.43
  296.6 3.2 collective-permute-done.40.refs_12_
  299.9 2.0 shard_map.474
  304.3 2.1 collective-permute-start.46
  306.5 2.0 collective-permute-done.46
  308.5 2.6 collective-permute-start.47
  311.0 2.3 collective-permute-done.47
  315.5 1.8 collective-permute-done.48
  (220 shorter events, 57.2 us)
Async XLA Ops:
  2.6 12.2 %collective-permute-start = (bf16[48,1536]{1,0:T(8,128)(2,1)S(1)}, bf16[48,1536]{1,0:T(8,128)(2,1)S(1)}, u32[]{:S(2)}, u32[]{:S(2)}) collective-permute-start(bf16[48,1536]{1,0:T(8,128)(2,1)S(1)} %pad_maximum_fusion.5), channel_id=1, source_target_pairs={{0,8},{2,10},{4,12},{6,14},{8,16},{10,18},{12,20},{14,22},{16,24},... | collective-permute-start | bytes 442376 | tf_op jit(solution)/shard_map/ppermute | solution.py:46
  5.7 12.3 %collective-permute-start.1 = (bf16[48,1536]{1,0:T(8,128)(2,1)S(1)}, bf16[48,1536]{1,0:T(8,128)(2,1)S(1)}, u32[]{:S(2)}, u32[]{:S(2)}) collective-permute-start(bf16[48,1536]{1,0:T(8,128)(2,1)S(1)} %pad_maximum_fusion.5), channel_id=1, source_target_pairs={{0,16},{2,18},{4,20},{6,22},{8,24},{10,26},{12,28},{14,30},{16,0},... | collective-permute-start | bytes 442376 | tf_op jit(solution)/shard_map/ppermute | solution.py:46
  8.3 9.7 %collective-permute-start.2 = (bf16[48,1536]{1,0:T(8,128)(2,1)S(1)}, bf16[48,1536]{1,0:T(8,128)(2,1)S(1)}, u32[]{:S(2)}, u32[]{:S(2)}) collective-permute-start(bf16[48,1536]{1,0:T(8,128)(2,1)S(1)} %pad_maximum_fusion.5), channel_id=1, source_target_pairs={{0,24},{2,26},{4,28},{6,30},{8,0},{10,2},{12,4},{14,6},{16,8},{18,... | collective-permute-start | bytes 442376 | tf_op jit(solution)/shard_map/ppermute | solution.py:46
  10.8 19.3 %all-to-all-start = ((f32[16,4,768]{2,1,0:T(4,128)}), f32[16,4,768]{2,1,0:T(4,128)S(1)}, u32[]{:S(2)}, u32[]{:S(2)}) async-start(f32[16,4,768]{2,1,0:T(4,128)} %bitcast.114), calls=%async_computation | async-start | bytes 393216 | tf_op jit(solution)/shard_map/all_to_all | solution.py:811
  18.4 23.0 %collective-permute-start.3 = (bf16[4,48,768]{2,1,0:T(8,128)(2,1)S(1)}, bf16[4,48,768]{2,1,0:T(8,128)(2,1)S(1)}, u32[]{:S(2)}, u32[]{:S(2)}) collective-permute-start(bf16[4,48,768]{2,1,0:T(8,128)(2,1)S(1)} %get-tuple-element.185), channel_id=1, source_target_pairs={{0,4},{2,6},{4,0},{6,2},{8,12},{10,14},{12,8},{14,10},{16,20},{18,... | collective-permute-start | bytes 884744 | tf_op jit(solution)/shard_map/ppermute | solution.py:46
  20.0 21.4 %collective-permute-start.4 = (bf16[4,48,768]{2,1,0:T(8,128)(2,1)S(1)}, bf16[4,48,768]{2,1,0:T(8,128)(2,1)S(1)}, u32[]{:S(2)}, u32[]{:S(2)}) collective-permute-start(bf16[4,48,768]{2,1,0:T(8,128)(2,1)S(1)} %get-tuple-element.187), channel_id=1, source_target_pairs={{0,2},{2,0},{4,6},{6,4},{8,10},{10,8},{12,14},{14,12},{16,18},{18,... | collective-permute-start | bytes 884744 | tf_op jit(solution)/shard_map/ppermute | solution.py:46
  21.5 11.7 %collective-permute-start.5 = (bf16[48,1536]{1,0:T(8,128)(2,1)S(1)}, bf16[48,1536]{1,0:T(8,128)(2,1)S(1)}, u32[]{:S(2)}, u32[]{:S(2)}) collective-permute-start(bf16[48,1536]{1,0:T(8,128)(2,1)S(1)} %convert_element_type.46), channel_id=1, source_target_pairs={{0,24},{2,26},{4,28},{6,30},{8,0},{10,2},{12,4},{14,6},{16,8},{18,... | collective-permute-start | bytes 442376 | tf_op jit(solution)/shard_map/ppermute | solution.py:46
  29.4 12.0 %collective-permute-start.6 = (bf16[48,1536]{1,0:T(8,128)(2,1)S(1)}, bf16[48,1536]{1,0:T(8,128)(2,1)S(1)}, u32[]{:S(2)}, u32[]{:S(2)}) collective-permute-start(bf16[48,1536]{1,0:T(8,128)(2,1)S(1)} %convert_element_type.46), channel_id=1, source_target_pairs={{0,16},{2,18},{4,20},{6,22},{8,24},{10,26},{12,28},{14,30},{16,0},... | collective-permute-start | bytes 442376 | tf_op jit(solution)/shard_map/ppermute | solution.py:46
  29.4 12.0 %collective-permute-start.7 = (bf16[48,1536]{1,0:T(8,128)(2,1)S(1)}, bf16[48,1536]{1,0:T(8,128)(2,1)S(1)}, u32[]{:S(2)}, u32[]{:S(2)}) collective-permute-start(bf16[48,1536]{1,0:T(8,128)(2,1)S(1)} %convert_element_type.46), channel_id=1, source_target_pairs={{0,8},{2,10},{4,12},{6,14},{8,16},{10,18},{12,20},{14,22},{16,24},... | collective-permute-start | bytes 442376 | tf_op jit(solution)/shard_map/ppermute | solution.py:46
  41.6 14.8 %collective-permute-start.8 = (bf16[4,2,48,768]{3,2,0,1:T(8,128)(2,1)S(1)}, bf16[4,2,48,768]{3,2,0,1:T(8,128)(2,1)}, u32[]{:S(2)}, u32[]{:S(2)}) collective-permute-start(bf16[4,2,48,768]{3,2,0,1:T(8,128)(2,1)S(1)} %maximum_select_fusion.6), channel_id=1, source_target_pairs={{0,2},{2,0},{4,6},{6,4},{8,10},{10,8},{12,14},{14,12},{16,18},{18,... | collective-permute-start | bytes 1769480 | tf_op jit(solution)/shard_map/ppermute | solution.py:46
  42.3 14.1 %collective-permute-start.9 = (bf16[4,2,48,768]{3,2,0,1:T(8,128)(2,1)S(1)}, bf16[4,2,48,768]{3,2,0,1:T(8,128)(2,1)}, u32[]{:S(2)}, u32[]{:S(2)}) collective-permute-start(bf16[4,2,48,768]{3,2,0,1:T(8,128)(2,1)S(1)} %maximum_select_fusion.7), channel_id=1, source_target_pairs={{0,4},{2,6},{4,0},{6,2},{8,12},{10,14},{12,8},{14,10},{16,20},{18,... | collective-permute-start | bytes 1769480 | tf_op jit(solution)/shard_map/ppermute | solution.py:46
  43.1 12.6 %collective-permute-start.10 = (bf16[48,1536]{1,0:T(8,128)(2,1)S(1)}, bf16[48,1536]{1,0:T(8,128)(2,1)}, u32[]{:S(2)}, u32[]{:S(2)}) collective-permute-start(bf16[48,1536]{1,0:T(8,128)(2,1)S(1)} %convert_bitcast_fusion), channel_id=1, source_target_pairs={{0,24},{2,26},{4,28},{6,30},{8,0},{10,2},{12,4},{14,6},{16,8},{18,... | collective-permute-start | bytes 442376 | tf_op jit(solution)/shard_map/ppermute | solution.py:46
  43.2 13.2 %collective-permute-start.11 = (bf16[48,1536]{1,0:T(8,128)(2,1)S(1)}, bf16[48,1536]{1,0:T(8,128)(2,1)}, u32[]{:S(2)}, u32[]{:S(2)}) collective-permute-start(bf16[48,1536]{1,0:T(8,128)(2,1)S(1)} %convert_bitcast_fusion), channel_id=1, source_target_pairs={{0,16},{2,18},{4,20},{6,22},{8,24},{10,26},{12,28},{14,30},{16,0},... | collective-permute-start | bytes 442376 | tf_op jit(solution)/shard_map/ppermute | solution.py:46
  44.0 12.3 %collective-permute-start.12 = (bf16[48,1536]{1,0:T(8,128)(2,1)S(1)}, bf16[48,1536]{1,0:T(8,128)(2,1)}, u32[]{:S(2)}, u32[]{:S(2)}) collective-permute-start(bf16[48,1536]{1,0:T(8,128)(2,1)S(1)} %convert_bitcast_fusion), channel_id=1, source_target_pairs={{0,8},{2,10},{4,12},{6,14},{8,16},{10,18},{12,20},{14,22},{16,24},... | collective-permute-start | bytes 442376 | tf_op jit(solution)/shard_map/ppermute | solution.py:46
  59.7 21.5 %collective-permute-start.15 = (bf16[768,1536]{1,0:T(8,128)(2,1)S(1)}, bf16[768,1536]{1,0:T(8,128)(2,1)S(1)}, u32[]{:S(2)}, u32[]{:S(2)}) collective-permute-start(bf16[768,1536]{1,0:T(8,128)(2,1)S(1)} %pad_maximum_fusion.refs_4_.refs_5_.refs_6_.refs_7_), channel_id=1, source_target_pairs={{0,1},{1,0},{2,3},{3,2},{4,5},{5,4},{6,7},{7,6},{8,9},{9,8},{10,11... | collective-permute-start | bytes 7077896 | tf_op jit(solution)/shard_map/ppermute | solution.py:55
  61.2 14.6 %collective-permute-start.13 = (bf16[4,48,1536]{2,1,0:T(8,128)(2,1)S(1)}, bf16[4,48,1536]{2,1,0:T(8,128)(2,1)S(1)}, u32[]{:S(2)}, u32[]{:S(2)}) collective-permute-start(bf16[4,48,1536]{2,1,0:T(8,128)(2,1)S(1)} %get-tuple-element.345), channel_id=1, source_target_pairs={{0,4},{2,6},{4,0},{6,2},{8,12},{10,14},{12,8},{14,10},{16,20},{18,... | collective-permute-start | bytes 1769480 | tf_op jit(solution)/shard_map/ppermute | solution.py:46
  63.6 15.3 %collective-permute-start.14 = (bf16[4,48,1536]{2,1,0:T(8,128)(2,1)S(1)}, bf16[4,48,1536]{2,1,0:T(8,128)(2,1)S(1)}, u32[]{:S(2)}, u32[]{:S(2)}) collective-permute-start(bf16[4,48,1536]{2,1,0:T(8,128)(2,1)S(1)} %get-tuple-element.339), channel_id=1, source_target_pairs={{0,2},{2,0},{4,6},{6,4},{8,10},{10,8},{12,14},{14,12},{16,18},{18,... | collective-permute-start | bytes 1769480 | tf_op jit(solution)/shard_map/ppermute | solution.py:46
  75.9 27.4 %collective-permute-start.16 = (bf16[4,2,48,1536]{3,2,0,1:T(8,128)(2,1)S(1)}, bf16[4,2,48,1536]{3,2,0,1:T(8,128)(2,1)}, u32[]{:S(2)}, u32[]{:S(2)}) collective-permute-start(bf16[4,2,48,1536]{3,2,0,1:T(8,128)(2,1)S(1)} %maximum_select_fusion.2), channel_id=1, source_target_pairs={{0,2},{2,0},{4,6},{6,4},{8,10},{10,8},{12,14},{14,12},{16,18},{18,... | collective-permute-start | bytes 3538952 | tf_op jit(solution)/shard_map/ppermute | solution.py:46
  80.1 25.5 %collective-permute-start.17 = (bf16[4,2,48,1536]{3,2,0,1:T(8,128)(2,1)}, bf16[4,2,48,1536]{3,2,0,1:T(8,128)(2,1)}, u32[]{:S(2)}, u32[]{:S(2)}) collective-permute-start(bf16[4,2,48,1536]{3,2,0,1:T(8,128)(2,1)} %maximum_select_fusion.3), channel_id=1, source_target_pairs={{0,4},{2,6},{4,0},{6,2},{8,12},{10,14},{12,8},{14,10},{16,20},{18,... | collective-permute-start | bytes 3538952 | tf_op jit(solution)/shard_map/ppermute | solution.py:46
  107.8 4.6 %collective-permute-start.18 = (bf16[768,1536]{1,0:T(8,128)(2,1)S(1)}, bf16[768,1536]{1,0:T(8,128)(2,1)S(1)}, u32[]{:S(2)}, u32[]{:S(2)}) collective-permute-start(bf16[768,1536]{1,0:T(8,128)(2,1)S(1)} %bitcast.175), channel_id=1, source_target_pairs={{0,1},{1,0},{2,3},{3,2},{4,5},{5,4},{6,7},{7,6},{8,9},{9,8},{10,11... | collective-permute-start | bytes 7077896 | tf_op jit(solution)/shard_map/ppermute | solution.py:55
  111.6 4.6 %collective-permute-start.19 = (bf16[768,1536]{1,0:T(8,128)(2,1)S(1)}, bf16[768,1536]{1,0:T(8,128)(2,1)S(1)}, u32[]{:S(2)}, u32[]{:S(2)}) collective-permute-start(bf16[768,1536]{1,0:T(8,128)(2,1)S(1)} %bitcast.177), channel_id=1, source_target_pairs={{0,1},{1,0},{2,3},{3,2},{4,5},{5,4},{6,7},{7,6},{8,9},{9,8},{10,11... | collective-permute-start | bytes 7077896 | tf_op jit(solution)/shard_map/ppermute | solution.py:55
  180.5 10.1 %collective-permute-start.20 = (bf16[768,1408]{1,0:T(8,128)(2,1)}, bf16[768,1408]{1,0:T(8,128)(2,1)}, u32[]{:S(2)}, u32[]{:S(2)}) collective-permute-start(bf16[768,1408]{1,0:T(8,128)(2,1)} %get-tuple-element.221), channel_id=1, source_target_pairs={{0,1},{1,0},{2,3},{3,2},{4,5},{5,4},{6,7},{7,6},{8,9},{9,8},{10,11... | collective-permute-start | bytes 6488072 | tf_op jit(solution)/shard_map/ppermute | solution.py:55
  180.8 8.8 %collective-permute-start.21 = (bf16[768,1280]{1,0:T(8,128)(2,1)}, bf16[768,1280]{1,0:T(8,128)(2,1)S(1)}, u32[]{:S(2)}, u32[]{:S(2)}) collective-permute-start(bf16[768,1280]{1,0:T(8,128)(2,1)} %get-tuple-element.223), channel_id=1, source_target_pairs={{0,1},{1,0},{2,3},{3,2},{4,5},{5,4},{6,7},{7,6},{8,9},{9,8},{10,11... | collective-permute-start | bytes 5898248 | tf_op jit(solution)/shard_map/ppermute | solution.py:55
  181.1 8.5 %collective-permute-start.22 = (bf16[768,768]{1,0:T(8,128)(2,1)}, bf16[768,768]{1,0:T(8,128)(2,1)S(1)}, u32[]{:S(2)}, u32[]{:S(2)}) collective-permute-start(bf16[768,768]{1,0:T(8,128)(2,1)} %get-tuple-element.225), channel_id=1, source_target_pairs={{0,1},{1,0},{2,3},{3,2},{4,5},{5,4},{6,7},{7,6},{8,9},{9,8},{10,11... | collective-permute-start | bytes 3538952 | tf_op jit(solution)/shard_map/ppermute | solution.py:55
  182.9 14.7 %all-to-all-start.1 = ((f32[16,4,768]{2,1,0:T(4,128)}), f32[16,4,768]{2,1,0:T(4,128)}, u32[]{:S(2)}, u32[]{:S(2)}) async-start(f32[16,4,768]{2,1,0:T(4,128)} %reshape.171), calls=%async_computation.1 | async-start | bytes 393216 | tf_op jit(solution)/shard_map/all_to_all | solution.py:952
  197.7 36.3 %collective-permute-start.23 = (bf16[4,2,48,1408]{3,2,1,0:T(8,128)(2,1)}, bf16[4,2,48,1408]{3,2,1,0:T(8,128)(2,1)S(1)}, u32[]{:S(2)}, u32[]{:S(2)}) collective-permute-start(bf16[4,2,48,1408]{3,2,1,0:T(8,128)(2,1)} %get-tuple-element.232), channel_id=1, source_target_pairs={{0,2},{2,0},{4,6},{6,4},{8,10},{10,8},{12,14},{14,12},{16,18},{18,... | collective-permute-start | bytes 3244040 | tf_op jit(solution)/shard_map/ppermute | solution.py:46
  199.2 34.7 %collective-permute-start.24 = (bf16[4,2,48,1280]{3,2,1,0:T(8,128)(2,1)}, bf16[4,2,48,1280]{3,2,1,0:T(8,128)(2,1)}, u32[]{:S(2)}, u32[]{:S(2)}) collective-permute-start(bf16[4,2,48,1280]{3,2,1,0:T(8,128)(2,1)} %get-tuple-element.233), channel_id=1, source_target_pairs={{0,4},{2,6},{4,0},{6,2},{8,12},{10,14},{12,8},{14,10},{16,20},{18,... | collective-permute-start | bytes 2949128 | tf_op jit(solution)/shard_map/ppermute | solution.py:46
  200.6 33.3 %collective-permute-start.25 = (bf16[2,2,48,768]{3,2,1,0:T(8,128)(2,1)}, bf16[2,2,48,768]{3,2,1,0:T(8,128)(2,1)S(1)}, u32[]{:S(2)}, u32[]{:S(2)}) collective-permute-start(bf16[2,2,48,768]{3,2,1,0:T(8,128)(2,1)} %bitcast.193), channel_id=1, source_target_pairs={{0,8},{2,10},{4,12},{6,14},{8,16},{10,18},{12,20},{14,22},{16,24},... | collective-permute-start | bytes 884744 | tf_op jit(solution)/shard_map/ppermute | solution.py:46
  202.1 31.8 %collective-permute-start.26 = (bf16[2,2,48,768]{3,2,1,0:T(8,128)(2,1)}, bf16[2,2,48,768]{3,2,1,0:T(8,128)(2,1)S(1)}, u32[]{:S(2)}, u32[]{:S(2)}) collective-permute-start(bf16[2,2,48,768]{3,2,1,0:T(8,128)(2,1)} %bitcast.192), channel_id=1, source_target_pairs={{0,16},{2,18},{4,20},{6,22},{8,24},{10,26},{12,28},{14,30},{16,0},... | collective-permute-start | bytes 884744 | tf_op jit(solution)/shard_map/ppermute | solution.py:46
  204.4 29.5 %collective-permute-start.27 = (bf16[2,2,48,768]{3,2,1,0:T(8,128)(2,1)}, bf16[2,2,48,768]{3,2,1,0:T(8,128)(2,1)S(1)}, u32[]{:S(2)}, u32[]{:S(2)}) collective-permute-start(bf16[2,2,48,768]{3,2,1,0:T(8,128)(2,1)} %bitcast.191), channel_id=1, source_target_pairs={{0,24},{2,26},{4,28},{6,30},{8,0},{10,2},{12,4},{14,6},{16,8},{18,... | collective-permute-start | bytes 884744 | tf_op jit(solution)/shard_map/ppermute | solution.py:46
  234.7 5.8 %collective-permute-start.28 = (bf16[768,1152]{1,0:T(8,128)(2,1)}, bf16[768,1152]{1,0:T(8,128)(2,1)}, u32[]{:S(2)}, u32[]{:S(2)}) collective-permute-start(bf16[768,1152]{1,0:T(8,128)(2,1)} %get-tuple-element.245), channel_id=1, source_target_pairs={{0,1},{1,0},{2,3},{3,2},{4,5},{5,4},{6,7},{7,6},{8,9},{9,8},{10,11... | collective-permute-start | bytes 5308424 | tf_op jit(solution)/shard_map/ppermute | solution.py:55
  235.1 13.5 %collective-permute-start.32 = (bf16[2048,384]{1,0:T(8,128)(2,1)}, bf16[2048,384]{1,0:T(8,128)(2,1)}, u32[]{:S(2)}, u32[]{:S(2)}) collective-permute-start(bf16[2048,384]{1,0:T(8,128)(2,1)} %get-tuple-element.264), channel_id=1, source_target_pairs={{0,1},{1,0},{2,3},{3,2},{4,5},{5,4},{6,7},{7,6},{8,9},{9,8},{10,11... | collective-permute-start | bytes 4718600 | tf_op jit(solution)/shard_map/ppermute | solution.py:55
  240.5 17.9 %collective-permute-start.29 = (bf16[4,48,1408]{2,1,0:T(8,128)(2,1)}, bf16[4,48,1408]{2,1,0:T(8,128)(2,1)}, u32[]{:S(2)}, u32[]{:S(2)}) collective-permute-start(bf16[4,48,1408]{2,1,0:T(8,128)(2,1)} %get-tuple-element.258), channel_id=1, source_target_pairs={{0,4},{2,6},{4,0},{6,2},{8,12},{10,14},{12,8},{14,10},{16,20},{18,... | collective-permute-start | bytes 1622024 | tf_op jit(solution)/shard_map/ppermute | solution.py:46
  241.9 16.6 %collective-permute-start.30 = (bf16[4,48,1280]{2,1,0:T(8,128)(2,1)}, bf16[4,48,1280]{2,1,0:T(8,128)(2,1)}, u32[]{:S(2)}, u32[]{:S(2)}) collective-permute-start(bf16[4,48,1280]{2,1,0:T(8,128)(2,1)} %get-tuple-element.259), channel_id=1, source_target_pairs={{0,2},{2,0},{4,6},{6,4},{8,10},{10,8},{12,14},{14,12},{16,18},{18,... | collective-permute-start | bytes 1474568 | tf_op jit(solution)/shard_map/ppermute | solution.py:46
  242.6 15.9 %collective-permute-start.31 = (bf16[2,48,768]{2,1,0:T(8,128)(2,1)}, bf16[2,48,768]{2,1,0:T(8,128)(2,1)S(1)}, u32[]{:S(2)}, u32[]{:S(2)}) collective-permute-start(bf16[2,48,768]{2,1,0:T(8,128)(2,1)} %bitcast.194), channel_id=1, source_target_pairs={{0,2},{2,0},{4,6},{6,4},{8,10},{10,8},{12,14},{14,12},{16,18},{18,... | collective-permute-start | bytes 442376 | tf_op jit(solution)/shard_map/ppermute | solution.py:46
  263.9 12.6 %collective-permute-start.34 = (bf16[4,2,48,640]{3,2,1,0:T(8,128)(2,1)}, bf16[4,2,48,640]{3,2,1,0:T(8,128)(2,1)S(1)}, u32[]{:S(2)}, u32[]{:S(2)}) collective-permute-start(bf16[4,2,48,640]{3,2,1,0:T(8,128)(2,1)} %copy-done.28), channel_id=1, source_target_pairs={{0,4},{2,6},{4,0},{6,2},{8,12},{10,14},{12,8},{14,10},{16,20},{18,... | collective-permute-start | bytes 1474568 | tf_op jit(solution)/shard_map/ppermute | solution.py:46
  264.7 10.2 %collective-permute-start.33 = (bf16[4,2,48,512]{3,2,1,0:T(8,128)(2,1)}, bf16[4,2,48,512]{3,2,1,0:T(8,128)(2,1)S(1)}, u32[]{:S(2)}, u32[]{:S(2)}) collective-permute-start(bf16[4,2,48,512]{3,2,1,0:T(8,128)(2,1)} %copy-done.29), channel_id=1, source_target_pairs={{0,2},{2,0},{4,6},{6,4},{8,10},{10,8},{12,14},{14,12},{16,18},{18,... | collective-permute-start | bytes 1179656 | tf_op jit(solution)/shard_map/ppermute | solution.py:46
  265.5 15.4 %collective-permute-start.37 = (bf16[48,2688]{1,0:T(8,128)(2,1)}, bf16[48,2688]{1,0:T(8,128)(2,1)S(1)}, u32[]{:S(2)}, u32[]{:S(2)}) collective-permute-start(bf16[48,2688]{1,0:T(8,128)(2,1)} %get-tuple-element.279), channel_id=1, source_target_pairs={{0,8},{2,10},{4,12},{6,14},{8,16},{10,18},{12,20},{14,22},{16,24},... | collective-permute-start | bytes 774152 | tf_op jit(solution)/shard_map/ppermute | solution.py:46
  265.5 20.1 %collective-permute-start.38 = (bf16[48,2688]{1,0:T(8,128)(2,1)}, bf16[48,2688]{1,0:T(8,128)(2,1)S(1)}, u32[]{:S(2)}, u32[]{:S(2)}) collective-permute-start(bf16[48,2688]{1,0:T(8,128)(2,1)} %get-tuple-element.280), channel_id=1, source_target_pairs={{0,16},{2,18},{4,20},{6,22},{8,24},{10,26},{12,28},{14,30},{16,0},... | collective-permute-start | bytes 774152 | tf_op jit(solution)/shard_map/ppermute | solution.py:46
  266.4 19.2 %collective-permute-start.39 = (bf16[48,2688]{1,0:T(8,128)(2,1)}, bf16[48,2688]{1,0:T(8,128)(2,1)S(1)}, u32[]{:S(2)}, u32[]{:S(2)}) collective-permute-start(bf16[48,2688]{1,0:T(8,128)(2,1)} %get-tuple-element.281), channel_id=1, source_target_pairs={{0,24},{2,26},{4,28},{6,30},{8,0},{10,2},{12,4},{14,6},{16,8},{18,... | collective-permute-start | bytes 774152 | tf_op jit(solution)/shard_map/ppermute | solution.py:46
  279.3 6.4 %collective-permute-start.36 = (bf16[4,48,640]{2,1,0:T(8,128)(2,1)S(1)}, bf16[4,48,640]{2,1,0:T(8,128)(2,1)S(1)}, u32[]{:S(2)}, u32[]{:S(2)}) collective-permute-start(bf16[4,48,640]{2,1,0:T(8,128)(2,1)S(1)} %get-tuple-element.278), channel_id=1, source_target_pairs={{0,2},{2,0},{4,6},{6,4},{8,10},{10,8},{12,14},{14,12},{16,18},{18,... | collective-permute-start | bytes 737288 | tf_op jit(solution)/shard_map/ppermute | solution.py:46
  280.0 5.7 %collective-permute-start.35 = (bf16[4,48,512]{2,1,0:T(8,128)(2,1)S(1)}, bf16[4,48,512]{2,1,0:T(8,128)(2,1)S(1)}, u32[]{:S(2)}, u32[]{:S(2)}) collective-permute-start(bf16[4,48,512]{2,1,0:T(8,128)(2,1)S(1)} %get-tuple-element.277), channel_id=1, source_target_pairs={{0,4},{2,6},{4,0},{6,2},{8,12},{10,14},{12,8},{14,10},{16,20},{18,... | collective-permute-start | bytes 589832 | tf_op jit(solution)/shard_map/ppermute | solution.py:46
  285.8 16.1 %collective-permute-start.44 = (f32[16,4,768]{2,1,0:T(4,128)}, f32[16,4,768]{2,1,0:T(4,128)S(1)}, u32[]{:S(2)}, u32[]{:S(2)}) collective-permute-start(f32[16,4,768]{2,1,0:T(4,128)} %all-to-all-done.1), channel_id=1, source_target_pairs={{0,1},{1,0},{2,3},{3,2},{4,5},{5,4},{6,7},{7,6},{8,9},{9,8},{10,11... | collective-permute-start | bytes 589832 | tf_op jit(solution)/shard_map/ppermute | solution.py:55
  288.0 13.9 %collective-permute-start.41 = (bf16[48,1152]{1,0:T(8,128)(2,1)S(1)}, bf16[48,1152]{1,0:T(8,128)(2,1)S(1)}, u32[]{:S(2)}, u32[]{:S(2)}) collective-permute-start(bf16[48,1152]{1,0:T(8,128)(2,1)S(1)} %get-tuple-element.295), channel_id=1, source_target_pairs={{0,8},{2,10},{4,12},{6,14},{8,16},{10,18},{12,20},{14,22},{16,24},... | collective-permute-start | bytes 331784 | tf_op jit(solution)/shard_map/ppermute | solution.py:46
  293.0 8.9 %collective-permute-start.42 = (bf16[48,1152]{1,0:T(8,128)(2,1)S(1)}, bf16[48,1152]{1,0:T(8,128)(2,1)S(1)}, u32[]{:S(2)}, u32[]{:S(2)}) collective-permute-start(bf16[48,1152]{1,0:T(8,128)(2,1)S(1)} %get-tuple-element.296), channel_id=1, source_target_pairs={{0,16},{2,18},{4,20},{6,22},{8,24},{10,26},{12,28},{14,30},{16,0},... | collective-permute-start | bytes 331784 | tf_op jit(solution)/shard_map/ppermute | solution.py:46
  293.2 8.7 %collective-permute-start.43 = (bf16[48,1152]{1,0:T(8,128)(2,1)S(1)}, bf16[48,1152]{1,0:T(8,128)(2,1)S(1)}, u32[]{:S(2)}, u32[]{:S(2)}) collective-permute-start(bf16[48,1152]{1,0:T(8,128)(2,1)S(1)} %get-tuple-element.297), channel_id=1, source_target_pairs={{0,24},{2,26},{4,28},{6,30},{8,0},{10,2},{12,4},{14,6},{16,8},{18,... | collective-permute-start | bytes 331784 | tf_op jit(solution)/shard_map/ppermute | solution.py:46
  295.4 4.4 %collective-permute-start.40 = (bf16[48,768]{1,0:T(8,128)(2,1)S(1)}, bf16[48,768]{1,0:T(8,128)(2,1)S(1)}, u32[]{:S(2)}, u32[]{:S(2)}) collective-permute-start(bf16[48,768]{1,0:T(8,128)(2,1)S(1)} %bitcast.198), channel_id=1, source_target_pairs={{0,4},{2,6},{4,0},{6,2},{8,12},{10,14},{12,8},{14,10},{16,20},{18,... | collective-permute-start | bytes 221192 | tf_op jit(solution)/shard_map/ppermute | solution.py:46
  308.5 4.9 %collective-permute-start.47 = (f32[80,128]{1,0:T(8,128)S(1)}, f32[80,128]{1,0:T(8,128)S(1)}, u32[]{:S(2)}, u32[]{:S(2)}) collective-permute-start(f32[80,128]{1,0:T(8,128)S(1)} %add.62), channel_id=1, source_target_pairs={{0,16},{2,18},{4,20},{6,22},{8,24},{10,26},{12,28},{14,30},{16,0},... | collective-permute-start | bytes 122888 | tf_op jit(solution)/shard_map/ppermute | solution.py:91
  (53 other events, 325.3 us)
